TPU v7x, 32 devices: a whole 2x2x4 slice. The times are simulated.
32 devices in a mesh: rep: 4 (over y, core), shard: 8 (over z, x).
Axes of the slice: x: 2, y: 2, z: 4, core: 2. Of those that a mesh axis runs over, the one named last changes fastest.
Arguments:
- tokens: bfloat16 [8192, 768], P(('rep', 'shard')), may hold values from -6 to 6
- cotangent: bfloat16 [8192, 768], P(('rep', 'shard')), may hold values from -6 to 6
- segments: int32 [8192], P(('rep', 'shard')), may hold values from 1 to 24, as said below
- qkv_weight: float32 [768, 2304], P('shard'), may hold values from -0.21875 to 0.21875
- out_weight: float32 [768, 768], P('shard'), may hold values from -0.875 to 0.875
- up_weight: float32 [768, 3072], P('shard'), may hold values from -0.21875 to 0.21875
- down_weight: float32 [3072, 768], P('shard'), may hold values from -0.109375 to 0.109375
- small_weights: float32 [12, 768], P(None, 'shard'), may hold values from -1.2 to 1.6
- qkv_first: float32 [768, 2304], P('shard'), may hold values from -64 to 64
- out_first: float32 [768, 768], P('shard'), may hold values from -16 to 16
- up_first: float32 [768, 3072], P('shard'), may hold values from -16 to 16
- down_first: float32 [3072, 768], P('shard'), may hold values from -40 to 40
- small_first: float32 [12, 768], P(None, 'shard'), may hold values from -40 to 40
- qkv_second: float32 [768, 2304], P('shard'), may hold values from 245.76 to 3276.8
- out_second: float32 [768, 768], P('shard'), may hold values from 16.384 to 204.8
- up_second: float32 [768, 3072], P('shard'), may hold values from 24.576 to 294.912
- down_second: float32 [3072, 768], P('shard'), may hold values from 106.496 to 1392.64
- small_second: float32 [12, 768], P(None, 'shard'), may hold values from 122.88 to 1638.4
Outputs:
- mixed: bfloat16 [8192, 768], P(('rep', 'shard'))
- input_grad: float32 [8192, 768], P(('rep', 'shard'))
- qkv_next: float32 [768, 2304], P('shard')
- out_next: float32 [768, 768], P('shard')
- up_next: float32 [768, 3072], P('shard')
- down_next: float32 [3072, 768], P('shard')
- small_next: float32 [12, 768], P(None, 'shard')
- qkv_first_next: float32 [768, 2304], P('shard')
- out_first_next: float32 [768, 768], P('shard')
- up_first_next: float32 [768, 3072], P('shard')
- down_first_next: float32 [3072, 768], P('shard')
- small_first_next: float32 [12, 768], P(None, 'shard')
- qkv_second_next: float32 [768, 2304], P('shard')
- out_second_next: float32 [768, 768], P('shard')
- up_second_next: float32 [768, 3072], P('shard')
- down_second_next: float32 [3072, 768], P('shard')
- small_second_next: float32 [12, 768], P(None, 'shard')
Inputs may be any that keep to these rules, and one draw needn't show every extreme that they name: `segments`: rows are laid out as in the attention step: piece r of sequence s starts at row r * 2048 + s * 256. Along each sequence's positions the numbers never fall, and no two sequences share one; a document is a run of one number and holds at least 128 tokens; in every draw some sequence is a single document.
All inputs are finite; a program needn't handle non-finite values.
Results may differ from a plain program's by a relative error of at most 0.022.
Values may be sent and summed in bfloat16 or wider, within the bound.
No kernel may reach another device: no remote copies, remote signals or barrier semaphores. Data moves between devices by JAX's collectives and lax.ppermute only.
A program may use at most 192 MiB of HBM per device.

v0:
```python
import jax
import jax.numpy as jnp
from jax import lax
from jax.experimental import pallas as pl
from jax.experimental.pallas import tpu as pltpu
from jax.sharding import PartitionSpec as P

HEAD_DIM = 64
SPAN = 4
STEP_NUM = 10


NORM_EPS = 1e-05
BETA_ONE = 0.9
BETA_TWO = 0.95
ADAM_EPS = 1e-08
DECAY = 0.1
RATE_MATRIX = 0.05
RATE_SMALL = 0.3
MASKED = -1e30
BLOCK = 256
FEW = 8
F32 = jnp.float32
BF16 = jnp.bfloat16


def swapped(block, bit):
    return lax.ppermute(block, "rep", [(i, i ^ bit) for i in range(SPAN)])


def rep_blocks(block):
    far = swapped(block, 2)
    near = swapped(block, 1)
    return (block, near, far, swapped(far, 1))


def swap_shard(block, bits):
    return lax.ppermute(block, "shard", [(i, i ^ bits) for i in range(lax.axis_size("shard"))])


def after(block, other):
    return lax.optimization_barrier((block, other))[0]


class Pieces:
    def __init__(self, arrays, codes, rows):
        self.arrays, self.codes, self.rows = arrays, codes, rows

    def place(self, shard, refs, store):
        if self.codes is None:
            store(0, refs[0], 0, refs[0].shape[0])
            return
        for ref, codes in zip(refs, self.codes):
            for index, code in enumerate(codes):
                start = pl.multiple_of((shard ^ code) * self.rows, self.rows)
                store(start, ref, index * self.rows, self.rows)


def shard_gather(block, gate=None):
    shards = lax.axis_size("shard")
    if shards != FEW:
        full = lax.all_gather(block, "shard", axis=0, tiled=True)
        return Pieces([full], None, block.shape[0])
    cross = swap_shard(block, 1)
    sent = block if gate is None else after(block, gate)
    one = swap_shard(sent, 2)
    two = swap_shard(sent, 4)
    three = swap_shard(sent, 6)
    other = swap_shard(jnp.concatenate([one, two, three], axis=0), 1)
    codes = [[0], [1], [2], [4], [6], [3, 5, 7]]
    return Pieces([block, cross, one, two, three, other], codes, block.shape[0])


def scatter(blocks):
    return [blocks[0]] + [swap_shard(block, code + 1) for code, block in enumerate(blocks[1:])]


def scatter_end(blocks):
    total = blocks[0].astype(F32)
    for block in blocks[1:]:
        total = total + block.astype(F32)
    return total.astype(BF16)


def emit(place_ref, full_ref, refs):
    if len(refs) == 1:
        refs[0][...] = full_ref[...]
        return
    rows = full_ref.shape[0] // len(refs)
    for code, ref in enumerate(refs):
        start = pl.multiple_of((place_ref[1] ^ code) * rows, rows)
        ref[...] = full_ref[pl.ds(start, rows), :]


def norm_parts(values):
    center = jnp.mean(values, axis=-1, keepdims=True)
    centered = values - center
    variance = jnp.mean(centered * centered, axis=-1, keepdims=True)
    inverse = lax.rsqrt(variance + NORM_EPS)
    return centered * inverse, inverse


def norm_back(normalized, inverse, gain, grad):
    scaled = grad * gain
    mean_one = jnp.mean(scaled, axis=-1, keepdims=True)
    mean_two = jnp.mean(scaled * normalized, axis=-1, keepdims=True)
    return inverse * (scaled - mean_one - normalized * mean_two)


def contract_rows(left_side, right_side):
    return lax.dot_general(
        left_side, right_side, (((0,), (0,)), ((), ())), preferred_element_type=F32
    )


def contract_cols(left_side, right_side):
    return lax.dot_general(
        left_side, right_side, (((1,), (1,)), ((), ())), preferred_element_type=F32
    )


def adam_update(master, gradient, moment_one, moment_two, step_rate):
    first_new = BETA_ONE * moment_one + (1.0 - BETA_ONE) * gradient
    second_new = BETA_TWO * moment_two + (1.0 - BETA_TWO) * gradient * gradient
    fix_one = 1.0 - BETA_ONE**STEP_NUM
    fix_two = 1.0 - BETA_TWO**STEP_NUM
    step_dir = first_new / fix_one / (jnp.sqrt(second_new / fix_two) + ADAM_EPS)
    return (master - step_rate * (step_dir + DECAY * master), first_new, second_new)


def dot(left_side, right_side):
    return jnp.dot(left_side, right_side, preferred_element_type=F32)


def chosen(values, index):
    result = values[0]
    for at in range(1, len(values)):
        result = jnp.where(index == at, values[at], result)
    return result


def mask_bias(seg_col_ref, seg_row_ref, start, keys):
    same = seg_col_ref[:keys, 0:1] == seg_row_ref[0:1, start : start + BLOCK]
    key_at = lax.broadcasted_iota(jnp.int32, (keys, BLOCK), 0)
    query_at = lax.broadcasted_iota(jnp.int32, (keys, BLOCK), 1) + start
    return jnp.where(same & (key_at <= query_at), 0.0, MASKED)


def head_lanes(shape, head):
    lane = lax.broadcasted_iota(jnp.int32, shape, 1)
    return (lane >= head * HEAD_DIM) & (lane < (head + 1) * HEAD_DIM)


def attend(q_ref, k_ref, v_ref, seg_col_ref, seg_row_ref, out_ref, lse_ref):
    total, width = q_ref.shape
    heads = width // HEAD_DIM
    value_t = v_ref[...].T
    lse_ref[...] = jnp.zeros_like(lse_ref)
    for start in range(0, total, BLOCK):
        keys = start + BLOCK
        bias = mask_bias(seg_col_ref, seg_row_ref, start, keys)
        query = q_ref[start : start + BLOCK, :]
        pieces = []
        for head in range(heads):
            masked = jnp.where(head_lanes(query.shape, head), query, 0)
            scores = contract_cols(k_ref[:keys, :], masked) + bias
            peak = jnp.max(scores, axis=0, keepdims=True)
            exponent = jnp.exp(scores - peak)
            row_total = jnp.sum(exponent, axis=0, keepdims=True)
            mixed = dot(
                value_t[head * HEAD_DIM : (head + 1) * HEAD_DIM, :keys], exponent.astype(BF16)
            )
            pieces.append(mixed / row_total)
            lse_ref[head : head + 1, start : start + BLOCK] = peak + jnp.log(row_total)
        out_ref[start : start + BLOCK, :] = jnp.concatenate(pieces, axis=0).T.astype(BF16)


def attend_back(
    q_ref, k_ref, v_ref, do_ref, lse_ref, seg_col_ref, seg_row_ref, grad_ref, dk_ref, dv_ref
):
    total, width = q_ref.shape
    heads = width // HEAD_DIM
    key_t = k_ref[...].T
    dk_ref[...] = jnp.zeros_like(dk_ref)
    dv_ref[...] = jnp.zeros_like(dv_ref)
    for start in range(0, total, BLOCK):
        keys = start + BLOCK
        bias = mask_bias(seg_col_ref, seg_row_ref, start, keys)
        query = q_ref[start : start + BLOCK, :]
        grad = do_ref[start : start + BLOCK, :]
        pieces = []
        dk = dk_ref[:keys, :]
        dv = dv_ref[:keys, :]
        for head in range(heads):
            lanes = head_lanes(query.shape, head)
            query_h = jnp.where(lanes, query, 0)
            grad_h = jnp.where(lanes, grad, 0)
            scores = contract_cols(k_ref[:keys, :], query_h) + bias
            probs = jnp.exp(scores - lse_ref[head : head + 1, start : start + BLOCK])
            prob_grad = contract_cols(v_ref[:keys, :], grad_h)
            inner = jnp.sum(prob_grad * probs, axis=0, keepdims=True)
            score_grad = (probs * (prob_grad - inner)).astype(BF16)
            dv = dv + dot(probs.astype(BF16), grad_h)
            dk = dk + dot(score_grad, query_h)
            pieces.append(
                dot(key_t[head * HEAD_DIM : (head + 1) * HEAD_DIM, :keys], score_grad)
            )
        dk_ref[:keys, :] = dk
        dv_ref[:keys, :] = dv
        dq = jnp.concatenate(pieces, axis=0).T * HEAD_DIM ** (-0.5)
        grad_ref[start : start + BLOCK, :width] = dq.astype(BF16)
    grad_ref[:, width : 2 * width] = dk_ref[...].astype(BF16)
    grad_ref[:, 2 * width :] = dv_ref[...].astype(BF16)


def call(kernel, outs, scratch, flops, limit, *operands):
    sizes = [o.size * o.dtype.itemsize for o in operands] + [
        o.size * jnp.dtype(o.dtype).itemsize for o in outs
    ]
    vmem = pl.BlockSpec(memory_space=pltpu.VMEM)
    return pl.pallas_call(
        kernel,
        out_shape=tuple(outs),
        in_specs=[pl.BlockSpec(memory_space=pltpu.SMEM)] + [vmem] * (len(operands) - 1),
        out_specs=tuple([vmem] * len(outs)),
        scratch_shapes=scratch,
        compiler_params=pltpu.CompilerParams(vmem_limit_bytes=limit * 2**20),
        cost_estimate=pl.CostEstimate(
            flops=flops, bytes_accessed=sum(sizes), transcendentals=0
        ),
    )(*operands)


def shape(*dims, dtype=BF16):
    return jax.ShapeDtypeStruct(dims, dtype)


def send_parts(value, at, near_ref, far_ref, own_ref):
    rows = value.shape[0]

    @pl.when(at == 0)
    def _():
        own_ref[...] = value

    @pl.when(at == 1)
    def _():
        near_ref[rows:, :] = value.astype(BF16)

    @pl.when(at == 2)
    def _():
        far_ref[...] = value

    @pl.when(at == 3)
    def _():
        near_ref[:rows, :] = value.astype(BF16)


def rep_sum(near_send, far_part, gate=None):
    rows = far_part.shape[0]
    near = swapped(near_send, 1)
    far_send = (far_part + near[:rows].astype(F32)).astype(BF16)
    if gate is not None:
        far_send = after(far_send, gate)
    return near, swapped(far_send, 2), far_send


def place_store(target, columns, limit=None):
    def store(start, ref, first, rows):
        target[pl.ds(start, rows), :limit] = ref[first : first + rows, columns]

    return store


def prep_kernel(
    place_ref,
    qkv_ref,
    out_ref,
    up_ref,
    down_ref,
    small_ref,
    first_ref,
    second_ref,
    third_ref,
    small_rows,
):
    rep = place_ref[0]
    owned, width = out_ref.shape
    part, half = width // SPAN, width // 2
    units = third_ref.shape[0]
    small_rows[...] = jnp.zeros_like(small_rows)
    small_rows[: small_ref.shape[0], : small_ref.shape[1]] = small_ref[...]
    for which in range(3):
        first = which * width
        options = [qkv_ref[:, first + r * part : first + (r + 1) * part] for r in range(SPAN)]
        first_ref[:, which * part : (which + 1) * part] = chosen(options, rep).astype(BF16)
    first_ref[:, 3 * part :] = small_rows[...].T[:owned, :64].astype(BF16)
    second_ref[:, :half] = out_ref[:, :half].astype(BF16)
    pieces = []
    for first in range(0, up_ref.shape[1], SPAN * units):
        options = [up_ref[:, first + r * units : first + (r + 1) * units] for r in range(SPAN)]
        pieces.append(chosen(options, rep))
    second_ref[:, half:] = jnp.concatenate(pieces, axis=1).astype(BF16)
    third_ref[:, :half] = out_ref[:, half:].astype(BF16)
    start = pl.multiple_of(rep * units, units)
    third_ref[:, half:] = down_ref[pl.ds(start, units), :].astype(BF16)


def first_kernel(pieces, *refs):
    place_ref, refs = refs[0], refs[1:]
    token_refs, refs = refs[:SPAN], refs[SPAN:]
    count = len(pieces.arrays)
    weight_refs, refs = refs[:count], refs[count:]
    (
        all_ref,
        weight_ref,
        small_ref,
        q_ref,
        k_ref,
        v_ref,
        seg_col_ref,
        seg_row_ref,
        out_ref,
        lse_ref,
        small_cols,
    ) = refs
    rep, shard = place_ref[0], place_ref[1]
    total, width = all_ref.shape
    rows = total // SPAN
    part = q_ref.shape[1]
    pieces.place(shard, weight_refs, place_store(weight_ref, slice(0, 3 * part)))
    last = small_cols.shape[1]
    pieces.place(
        shard, weight_refs, place_store(small_cols, slice(3 * part + 64 - last, 3 * part + 64))
    )
    small = small_cols[...].astype(F32).T
    small = small[last - 64 : last - 48, :]
    small_ref[...] = small
    gain, bias = small[0:1, :], small[1:2, :]
    query_bias = chosen([small[2:3, r * part : (r + 1) * part] for r in range(SPAN)], rep)
    value_bias = chosen([small[3:4, r * part : (r + 1) * part] for r in range(SPAN)], rep)
    for at in range(SPAN):
        start = pl.multiple_of((rep ^ at) * rows, rows)
        block = token_refs[at][:rows, :]
        all_ref[pl.ds(start, rows), :] = block
        hidden = (norm_parts(block.astype(F32))[0] * gain + bias).astype(BF16)
        segs = token_refs[at][rows : rows + 16, :rows].astype(F32)
        seg_row_ref[:, pl.ds(start, rows)] = segs[:8, :]
        seg_col_ref[pl.ds(start, rows), 0:16] = segs.T
        projected = dot(hidden, weight_ref[...])
        q_ref[pl.ds(start, rows), :] = (
            (projected[:, :part] + query_bias) * HEAD_DIM ** (-0.5)
        ).astype(BF16)
        k_ref[pl.ds(start, rows), :] = projected[:, part : 2 * part].astype(BF16)
        v_ref[pl.ds(start, rows), :] = (projected[:, 2 * part :] + value_bias).astype(BF16)
    attend(q_ref, k_ref, v_ref, seg_col_ref, seg_row_ref, out_ref, lse_ref)


def second_kernel(pieces, place_ref, *refs):
    attended_refs, refs = refs[:SPAN], refs[SPAN:]
    cot_refs, refs = refs[:SPAN], refs[SPAN:]
    count = len(pieces.arrays)
    piece_refs, refs = refs[:count], refs[count:]
    (
        wide_ref,
        all_ref,
        small_ref,
        up_bias_ref,
        out_weight,
        cot_ref,
        hidden_ref,
        act_ref,
        pre_ref,
        residual_ref,
        near_ref,
        far_ref,
        own_ref,
        up_weight,
    ) = refs
    rep = place_ref[0]
    total, width = all_ref.shape
    rows = total // SPAN
    part = attended_refs[0].shape[1]
    half = width // 2
    pieces.place(place_ref[1], piece_refs, place_store(up_weight, slice(half, None)))
    pieces.place(place_ref[1], piece_refs, place_store(out_weight, slice(0, half), half))
    out_weight[:, half:] = wide_ref[:, :half]
    for at in range(SPAN):
        cot_ref[pl.ds(pl.multiple_of((rep ^ at) * rows, rows), rows), :] = cot_refs[at][...]
    out_bias, gain, bias = small_ref[4:5, :], small_ref[5:6, :], small_ref[6:7, :]

    @pl.loop(0, SPAN)
    def _(index):
        block = pl.ds(pl.multiple_of(index * rows, rows), rows)
        mixed = out_bias
        for at in range(SPAN):
            from_rows = pl.ds(pl.multiple_of((rep ^ at) * part, part), part)
            mixed = mixed + dot(attended_refs[at][block, :], out_weight[from_rows, :])
        residual = all_ref[block, :].astype(F32) + mixed

        @pl.when(index == rep)
        def _():
            residual_ref[...] = residual

        hidden = (norm_parts(residual)[0] * gain + bias).astype(BF16)
        hidden_ref[block, :] = hidden
        pre_act = dot(hidden, up_weight[...]) + up_bias_ref[...]
        cdf = 0.5 * (1.0 + lax.erf(pre_act * (0.5**0.5)))
        act_ref[block, :] = (pre_act * cdf).astype(BF16)
        slope = cdf + pre_act * (jnp.exp(-0.5 * pre_act * pre_act) * 0.3989422804014327)
        pre_low = (contract_cols(cot_ref[block, :], wide_ref[:, half:]) * slope).astype(BF16)
        pre_ref[block, :] = pre_low
        grad = contract_cols(pre_low, up_weight[...])
        send_parts(grad, index ^ rep, near_ref, far_ref, own_ref)


def third_kernel(place_ref, act_ref, hidden_ref, pre_ref, cot_ref, wide_ref, *refs):
    grad_refs, (near_ref, far_ref, own_ref, sum_ref, grad_ref) = refs[:-5], refs[-5:]
    rep = place_ref[0]
    total, width = cot_ref.shape
    rows = total // SPAN
    units = act_ref.shape[1]
    step = units // 3
    for first in range(0, units, step):
        grad_ref[first : first + step, :width] = contract_rows(
            act_ref[:, first : first + step], cot_ref[...]
        ).astype(BF16)
    step = width // 3
    for first in range(0, width, step):
        grad_ref[first : first + step, width:] = contract_rows(
            hidden_ref[:, first : first + step], pre_ref[...]
        ).astype(BF16)
    sum_ref[...] = jnp.broadcast_to(
        jnp.sum(pre_ref[...].astype(F32), axis=0, keepdims=True), sum_ref.shape
    )

    @pl.loop(0, SPAN)
    def _(index):
        block = pl.ds(pl.multiple_of(index * rows, rows), rows)
        send_parts(
            dot(act_ref[block, :], wide_ref[:, -width:]), index ^ rep, near_ref, far_ref, own_ref
        )

    emit(place_ref, grad_ref, grad_refs)

def fourth_kernel(
    place_ref,
    own_ref,
    near_ref,
    far_ref,
    residual_ref,
    cotangent_ref,
    small_ref,
    resid_grad_ref,
    branch_ref,
    sums_ref,
):
    grad = own_ref[...] + near_ref[own_ref.shape[0] :, :].astype(F32) + far_ref[...].astype(F32)
    normalized, inverse = norm_parts(residual_ref[...])
    cotangent = cotangent_ref[...].astype(F32)
    resid_grad = cotangent + norm_back(normalized, inverse, small_ref[5:6, :], grad)
    branch = resid_grad.astype(BF16)
    resid_grad_ref[...] = resid_grad
    branch_ref[...] = branch
    sums_ref[...] = jnp.zeros_like(sums_ref)
    sums_ref[4:5, :] = jnp.sum(branch.astype(F32), axis=0, keepdims=True)
    sums_ref[5:6, :] = jnp.sum(grad * normalized, axis=0, keepdims=True)
    sums_ref[6:7, :] = jnp.sum(grad, axis=0, keepdims=True)
    sums_ref[7:8, :] = jnp.sum(cotangent, axis=0, keepdims=True)


def fifth_kernel(
    place_ref,
    branch_a,
    branch_b,
    branch_c,
    branch_d,
    attended_a,
    attended_b,
    attended_c,
    attended_d,
    out_weight,
    qkv_weight,
    q_ref,
    k_ref,
    v_ref,
    lse_ref,
    seg_col_ref,
    seg_row_ref,
    all_ref,
    small_ref,
    sums_ref,
    unit_sums_ref,
    *refs,
):
    grad_refs, refs = refs[:-11], refs[-11:]
    (
        near_ref,
        far_ref,
        own_ref,
        branch_ref,
        back_ref,
        proj_ref,
        dk_ref,
        dv_ref,
        small_grads,
        grad_ref,
        hidden_ref,
    ) = refs
    rep = place_ref[0]
    total, width = all_ref.shape
    rows = total // SPAN
    part = q_ref.shape[1]
    own_rows = pl.ds(pl.multiple_of(rep * part, part), part)
    for at, ref in enumerate((branch_a, branch_b, branch_c, branch_d)):
        start = pl.multiple_of((rep ^ at) * rows, rows)
        branch_ref[pl.ds(start, rows), :] = ref[...]
    back_ref[...] = contract_cols(branch_ref[...], out_weight[own_rows, :]).astype(BF16)
    attend_back(
        q_ref,
        k_ref,
        v_ref,
        back_ref,
        lse_ref,
        seg_col_ref,
        seg_row_ref,
        proj_ref,
        dk_ref,
        dv_ref,
    )
    gain = small_ref[0:1, :]
    small_grads[...] = jnp.zeros_like(small_grads)
    small_grads[0:8, :] = sums_ref[...]
    small_grads[8:16, :] = unit_sums_ref[...]

    @pl.loop(0, SPAN)
    def _(index):
        block = pl.ds(pl.multiple_of(index * rows, rows), rows)
        grad = contract_cols(proj_ref[block, :], qkv_weight[...])
        normalized = norm_parts(all_ref[block, :].astype(F32))[0]
        hidden_ref[block, :] = (normalized * gain + small_ref[1:2, :]).astype(BF16)
        small_grads[0:1, :] += jnp.sum(grad * normalized, axis=0, keepdims=True)
        small_grads[1:2, :] += jnp.sum(grad, axis=0, keepdims=True)
        send_parts(grad, index ^ rep, near_ref, far_ref, own_ref)

    lane = lax.broadcasted_iota(jnp.int32, (1, width), 1)
    mine = (lane >= rep * part) & (lane < (rep + 1) * part)
    for row, first in ((2, 0), (3, 2 * part)):
        column_sum = jnp.sum(
            proj_ref[:, first : first + part].astype(F32), axis=0, keepdims=True
        )
        small_grads[row : row + 1, :] = jnp.where(
            mine, jnp.concatenate([column_sum] * SPAN, axis=1), 0.0
        )
    step = width // 3
    for first in range(0, width, step):
        grad_ref[first : first + step, : 3 * part] = contract_rows(
            hidden_ref[:, first : first + step], proj_ref[...]
        ).astype(BF16)
    branch_part = chosen(
        [branch_ref[:, r * part : (r + 1) * part] for r in range(SPAN)], rep
    )
    for at, ref in enumerate((attended_a, attended_b, attended_c, attended_d)):
        from_rows = pl.ds(pl.multiple_of((rep ^ at) * part, part), part)
        grad_ref[from_rows, 3 * part : 4 * part] = contract_rows(ref[...], branch_part).astype(
            BF16
        )
    grad_ref[:, 4 * part :] = small_grads[...].T[:, :64].astype(BF16)
    emit(place_ref, grad_ref, grad_refs)

def sixth_kernel(
    place_ref, own_ref, near_ref, far_ref, tokens_ref, resid_grad_ref, small_ref, out_ref
):
    grad = own_ref[...] + near_ref[own_ref.shape[0] :, :].astype(F32) + far_ref[...].astype(F32)
    normalized, inverse = norm_parts(tokens_ref[...].astype(F32))
    out_ref[...] = resid_grad_ref[...] + norm_back(normalized, inverse, small_ref[0:1, :], grad)


def rep_order(refs, rep):
    blocks = [ref[...].astype(F32) for ref in refs]
    odd, high = (rep & 1) == 1, (rep & 2) == 2
    pairs = []
    for first in (0, 2):
        lower, upper = blocks[first], blocks[first + 1]
        pairs.append((jnp.where(odd, upper, lower), jnp.where(odd, lower, upper)))
    low = [jnp.where(high, b, a) for a, b in zip(*pairs)]
    return low + [jnp.where(high, a, b) for a, b in zip(*pairs)]


def adam_kernel(place_ref, *refs):
    blocks = rep_order(refs[:SPAN], place_ref[0])
    ins, outs = refs[SPAN : SPAN + 9], refs[SPAN + 9 :]
    part = ins[3].shape[1] // SPAN
    qkv = [b[:, c * part : (c + 1) * part] for c in range(3) for b in blocks]
    out = [b[:, 3 * part : 4 * part] for b in blocks]
    small = blocks[0][:, 4 * part :]
    for block in blocks[1:]:
        small = small + block[:, 4 * part :]
    small = jnp.concatenate([small, small], axis=1).T[:12, :]
    grads = (jnp.concatenate(qkv, axis=1), jnp.concatenate(out, axis=1), small)
    for at, (gradient, rate) in enumerate(zip(grads, (RATE_MATRIX, RATE_MATRIX, RATE_SMALL))):
        weight, first, second = (ref[...] for ref in ins[3 * at : 3 * at + 3])
        results = adam_update(weight, gradient, first, second, rate)
        for ref, value in zip(outs[3 * at : 3 * at + 3], results):
            ref[...] = value


def up_adam_kernel(place_ref, *refs):
    blocks = rep_order(refs[:SPAN], place_ref[0])
    weight, first, second, *outs = refs[SPAN:]
    width = weight.shape[1] // SPAN
    units = width // FEW
    pieces = [b[:, at * units : (at + 1) * units] for at in range(FEW) for b in blocks]
    results = adam_update(
        weight[...], jnp.concatenate(pieces, axis=1), first[...], second[...], RATE_MATRIX
    )
    for ref, value in zip(outs, results):
        ref[...] = value


def down_adam_kernel(place_ref, *refs):
    at = pl.program_id(0) ^ place_ref[0]
    gradient = chosen([ref[...] for ref in refs[:SPAN]], at).astype(F32)
    weight, first, second, *outs = refs[SPAN:]
    results = adam_update(weight[...], gradient, first[...], second[...], RATE_MATRIX)
    for ref, value in zip(outs, results):
        ref[...] = value


def grid_adam(kernel, steps, place, blocks, block_spec, arrays):
    rows, columns = arrays[0].shape
    spec = pl.BlockSpec((rows // steps, columns), lambda i: (i, 0))
    return pl.pallas_call(
        kernel,
        grid=(steps,),
        out_shape=[shape(rows, columns, dtype=F32)] * 3,
        in_specs=[pl.BlockSpec(memory_space=pltpu.SMEM)]
        + [block_spec] * SPAN
        + [spec] * 3,
        out_specs=[spec] * 3,
        compiler_params=pltpu.CompilerParams(vmem_limit_bytes=16 * 2**20),
        cost_estimate=pl.CostEstimate(
            flops=20 * rows * columns, bytes_accessed=26 * rows * columns, transcendentals=0
        ),
    )(place, *blocks, *arrays)


def in_order(blocks, rep):
    odd = (rep & 1) == 1
    high = (rep & 2) == 2
    low_pair = (jnp.where(odd, blocks[1], blocks[0]), jnp.where(odd, blocks[0], blocks[1]))
    high_pair = (jnp.where(odd, blocks[3], blocks[2]), jnp.where(odd, blocks[2], blocks[3]))
    return (
        jnp.where(high, high_pair[0], low_pair[0]),
        jnp.where(high, high_pair[1], low_pair[1]),
        jnp.where(high, low_pair[0], high_pair[0]),
        jnp.where(high, low_pair[1], high_pair[1]),
    )


def local(
    tokens,
    cotangent,
    segments,
    qkv_weight,
    out_weight,
    up_weight,
    down_weight,
    small_weights,
    qkv_first,
    out_first,
    up_first,
    down_first,
    small_first,
    qkv_second,
    out_second,
    up_second,
    down_second,
    small_second,
):
    rep = lax.axis_index("rep")
    shards = lax.axis_size("shard")
    place = jnp.stack([rep, lax.axis_index("shard")]).astype(jnp.int32)
    rows, width = tokens.shape
    total = SPAN * rows
    part = width // SPAN
    owned = qkv_weight.shape[0]
    ff = up_weight.shape[1]
    ff_part = ff // SPAN
    units = down_weight.shape[0] // SPAN

    def rep_part(block, size, axis):
        return lax.dynamic_slice_in_dim(block, rep * size, size, axis)

    few = shards == FEW
    half = width // 2
    if few:
        first_send, second_send, third_send = call(
            prep_kernel,
            [
                shape(owned, 3 * part + 64),
                shape(owned, half + ff_part),
                shape(units, half + width),
            ],
            [pltpu.VMEM((128, 128), F32)],
            owned * width,
            16,
            place,
            qkv_weight,
            out_weight,
            up_weight,
            down_weight,
            small_weights,
        )
    else:
        low_small = small_weights.astype(BF16).T
        low_qkv = rep_part(qkv_weight.astype(BF16).reshape(owned, 3, SPAN, part), 1, 2)
        low_qkv = low_qkv.reshape(owned, 3 * part)
        pad = 64 - low_small.shape[1]
        first_send = jnp.concatenate([low_qkv, jnp.pad(low_small, ((0, 0), (0, pad)))], axis=1)
        low_up = rep_part(up_weight.astype(BF16).reshape(owned, shards, SPAN, units), 1, 2)
        low_down = rep_part(down_weight, units, 0).astype(BF16)
        low_out = out_weight.astype(BF16)
        second_send = jnp.concatenate([low_out[:, :half], low_up.reshape(owned, -1)], axis=1)
        third_send = jnp.concatenate([low_out[:, half:], low_down], axis=1)
    third_full = lax.all_gather(third_send, "shard", axis=0, tiled=True)
    first_pieces = shard_gather(first_send)
    second_pieces = shard_gather(second_send, first_pieces.arrays[-2 * few])

    seg_block = jnp.pad(segments.astype(BF16)[None, :], ((0, 15), (0, width - rows)))
    token_blocks = rep_blocks(jnp.concatenate([tokens, seg_block], axis=0))
    cot_blocks = rep_blocks(after(cotangent, token_blocks[2]))

    (
        all_tokens,
        qkv_part,
        small,
        queries,
        keys,
        values,
        seg_col,
        seg_row,
        attended,
        log_total,
    ) = call(
        lambda *refs: first_kernel(first_pieces, *refs),
        [
            shape(total, width),
            shape(width, 3 * part),
            shape(16, width, dtype=F32),
            shape(total, part),
            shape(total, part),
            shape(total, part),
            shape(total, 128, dtype=F32),
            shape(8, total, dtype=F32),
            shape(total, part),
            shape(8, total, dtype=F32),
        ],
        [pltpu.VMEM((width, 128), BF16)],
        2 * total * width * 3 * part + 16 * total * total * part,
        20,
        place,
        *token_blocks,
        *first_pieces.arrays,
    )
    up_bias = rep_part(small[8:12].reshape(shards, SPAN, units), 1, 1).reshape(1, -1)
    attended_blocks = rep_blocks(attended)
    (
        out_part,
        all_cot,
        hidden_two,
        act_low,
        pre_low,
        residual,
        near_send,
        far_part,
        own,
    ) = call(
        lambda *refs: second_kernel(second_pieces, *refs),
        [
            shape(width, width),
            shape(total, width),
            shape(total, width),
            shape(total, ff_part),
            shape(total, ff_part),
            shape(rows, width, dtype=F32),
            shape(2 * rows, width),
            shape(rows, width, dtype=F32),
            shape(rows, width, dtype=F32),
        ],
        [pltpu.VMEM((width, ff_part), BF16)],
        10 * total * width * width,
        28,
        place,
        *attended_blocks,
        *cot_blocks,
        *second_pieces.arrays,
        third_full,
        all_tokens,
        small,
        up_bias,
    )
    near, far, far_send = rep_sum(near_send, far_part)
    hidden_two_terms = own, near, far
    *wide_grad, mixed_near, mixed_far, mixed_own, unit_sums = call(
        third_kernel,
        [shape(owned, 2 * width)] * FEW * few
        + [shape(ff_part, 2 * width)] * (not few)
        + [
            shape(2 * rows, width),
            shape(rows, width, dtype=F32),
            shape(rows, width, dtype=F32),
            shape(8, ff_part, dtype=F32),
        ],
        [pltpu.VMEM((ff_part, 2 * width), BF16)],
        6 * total * width * width,
        22,
        place,
        after(act_low, far_send),
        hidden_two,
        pre_low,
        all_cot,
        third_full,
    )
    if few:
        wide_blocks = scatter(lax.optimization_barrier((wide_grad, far))[0])
    resid_grad, branch, sums = call(
        fourth_kernel,
        [
            shape(rows, width, dtype=F32),
            shape(rows, width),
            shape(8, width, dtype=F32),
        ],
        [],
        10 * rows * width,
        16,
        place,
        *hidden_two_terms,
        residual,
        cotangent,
        small,
    )
    branch_blocks = rep_blocks(branch)
    near_mixed, far_mixed, _ = rep_sum(after(mixed_near, branch), mixed_far, branch_blocks[2])
    unit_rows = lax.dynamic_update_slice(
        jnp.zeros((shards, SPAN, units), F32), unit_sums[0].reshape(shards, 1, units), (0, rep, 0)
    ).reshape(ff // width, width)
    unit_rows = jnp.pad(unit_rows, ((0, 8 - ff // width), (0, 0)))
    *last_grad, near_send, far_part, own = call(
        fifth_kernel,
        [shape(owned, 4 * part + 64)] * FEW * few
        + [shape(width, 4 * part + 64)] * (not few)
        + [
            shape(2 * rows, width),
            shape(rows, width, dtype=F32),
            shape(rows, width, dtype=F32),
        ],
        [
            pltpu.VMEM((total, width), BF16),
            pltpu.VMEM((total, part), BF16),
            pltpu.VMEM((total, 3 * part), BF16),
            pltpu.VMEM((total, part), F32),
            pltpu.VMEM((total, part), F32),
            pltpu.VMEM((128, width), F32),
            pltpu.VMEM((width, 4 * part + 64), BF16),
            pltpu.VMEM((total, width), BF16),
        ],
        6 * total * width * width + 40 * total * total * part,
        32,
        place,
        *branch_blocks,
        *attended_blocks,
        out_part,
        qkv_part,
        queries,
        keys,
        values,
        log_total,
        seg_col,
        seg_row,
        all_tokens,
        small,
        sums,
        unit_rows,
    )
    near, far, far_send = rep_sum(near_send, far_part)
    if few:
        last_blocks = scatter(last_grad)
        wide_blocks = rep_blocks(scatter_end(wide_blocks))
    else:
        last_total, wide_total = (
            lax.psum_scatter(grad, "shard", scatter_dimension=0, tiled=True)
            for grad in (last_grad[0], wide_grad[0])
        )
        wide_blocks = rep_blocks(wide_total)
    mixed = residual + (
        mixed_own + near_mixed[rows:].astype(F32) + far_mixed.astype(F32) + small[7]
    )
    mixed = mixed.astype(BF16)
    input_grad = call(
        sixth_kernel,
        [shape(rows, width, dtype=F32)],
        [],
        10 * rows * width,
        16,
        place,
        own,
        near,
        far,
        tokens,
        resid_grad,
        small,
    )[0]
    if few:
        up_res = grid_adam(
            up_adam_kernel,
            3,
            place,
            wide_blocks,
            pl.BlockSpec((owned // 3, width), lambda i: (i, 1)),
            (up_weight, up_first, up_second),
        )
        down_res = grid_adam(
            down_adam_kernel,
            SPAN,
            place,
            wide_blocks,
            pl.BlockSpec((units, width), lambda i: (0, 0)),
            (down_weight, down_first, down_second),
        )
        last_blocks, input_grad, mixed = lax.optimization_barrier(
            (last_blocks, input_grad, mixed)
        )
        last_total = scatter_end(last_blocks)
        results = call(
            adam_kernel,
            [shape(*ref.shape, dtype=F32) for ref in (qkv_weight, out_weight, small_weights)
             for _ in range(3)],
            [],
            20 * qkv_weight.size,
            24,
            place,
            *rep_blocks(last_total),
            qkv_weight,
            qkv_first,
            qkv_second,
            out_weight,
            out_first,
            out_second,
            small_weights,
            small_first,
            small_second,
        )
        qkv_res, out_res, small_res = results[:3], results[3:6], results[6:]
    else:
        wide_own = in_order(wide_blocks, rep)
        down_own = jnp.concatenate([g[:, :width] for g in wide_own], axis=0).astype(F32)
        up_own = [g[:, width:].reshape(owned, shards, units) for g in wide_own]
        up_own = jnp.stack(up_own, axis=2).reshape(owned, ff).astype(F32)
        up_res = adam_update(up_weight, up_own, up_first, up_second, RATE_MATRIX)
        down_res = adam_update(down_weight, down_own, down_first, down_second, RATE_MATRIX)
        last_own = in_order(rep_blocks(last_total), rep)
        out_own = jnp.concatenate([g[:, 3 * part : 4 * part] for g in last_own], axis=1)
        qkv_own = [g[:, : 3 * part].reshape(owned, 3, part) for g in last_own]
        qkv_own = jnp.stack(qkv_own, axis=2).reshape(owned, 3 * width).astype(F32)
        small_own = sum(g[:, 4 * part : 4 * part + 12].astype(F32) for g in last_own).T
        qkv_res = adam_update(qkv_weight, qkv_own, qkv_first, qkv_second, RATE_MATRIX)
        out_res = adam_update(
            out_weight, out_own.astype(F32), out_first, out_second, RATE_MATRIX
        )
        small_res = adam_update(
            small_weights, small_own, small_first, small_second, RATE_SMALL
        )
    return (
        mixed,
        input_grad,
        qkv_res[0],
        out_res[0],
        up_res[0],
        down_res[0],
        small_res[0],
        qkv_res[1],
        out_res[1],
        up_res[1],
        down_res[1],
        small_res[1],
        qkv_res[2],
        out_res[2],
        up_res[2],
        down_res[2],
        small_res[2],
    )


def solution(mesh):
    tokens_spec = P(("rep", "shard"), None)
    rows = P("shard", None)
    columns = P(None, "shard")
    weights = (rows, rows, rows, rows, columns)
    return jax.shard_map(
        local,
        mesh=mesh,
        in_specs=(tokens_spec, tokens_spec, P(("rep", "shard"))) + weights * 3,
        out_specs=(tokens_spec, tokens_spec) + weights * 3,
        check_vma=False,
    )
```

profile of v0, /device:TPU:11, one launch (start us, length us, event | category | flops | bytes accessed | tf_op | source)
XLA Modules:
  0.0 310.6 jit_solution(4943095537770841982)
XLA Ops:
  12.7 2.9 shard_map.305
  18.3 2.2 collective-permute-start.4
  20.5 1.5 collective-permute-start
  22.0 4.3 %collective-permute-done.1.refs_3_ = bf16[272,768]{1,0:T(8,128)(2,1)S(1)} collective-permute-done((bf16[272,768]{1,0:T(8,128)(2,1)S(1)}, bf16[272,768]{1,0:T(8,128)(2,1)S(1)}, u32[]{:S(2)}, u32[]{:S(2)}) %collective-permute-start.1) | collective-permute-done | bytes 417824 | tf_op jit(solution)/shard_map/ppermute | solution.py:28
  26.2 1.5 collective-permute-start.2
  29.4 4.3 %collective-permute-start.15 = (bf16[96,1152]{1,0:T(8,128)(2,1)S(1)}, bf16[96,1152]{1,0:T(8,128)(2,1)S(1)}, u32[]{:S(2)}, u32[]{:S(2)}) collective-permute-start(bf16[96,1152]{1,0:T(8,128)(2,1)S(1)} %get-tuple-element.107.refs_9_), channel_id=1, source_target_pairs={{0,2},{1,3},{2,0},{3,1},{4,6},{5,7},{6,4},{7,5},{8,10},{9,11},{10,... | collective-permute-start | bytes 663560 | tf_op jit(solution)/shard_map/ppermute | solution.py:38
  33.7 2.3 collective-permute-done.3.refs_6_
  36.0 4.2 %collective-permute-start.16 = (bf16[96,1152]{1,0:T(8,128)(2,1)S(1)}, bf16[96,1152]{1,0:T(8,128)(2,1)S(1)}, u32[]{:S(2)}, u32[]{:S(2)}) collective-permute-start(bf16[96,1152]{1,0:T(8,128)(2,1)S(1)} %get-tuple-element.107.refs_9_), channel_id=1, source_target_pairs={{0,4},{1,5},{2,6},{3,7},{4,0},{5,1},{6,2},{7,3},{8,12},{9,13},{10,... | collective-permute-start | bytes 663560 | tf_op jit(solution)/shard_map/ppermute | solution.py:38
  40.2 1.8 collective-permute-start.17
  42.0 8.5 %shard_map.306 = (bf16[1024,768]{1,0:T(8,128)(2,1)S(1)}, bf16[768,576]{1,0:T(8,128)(2,1)S(1)}, f32[16,768]{1,0:T(8,128)S(1)}, bf16[1024,192]{1,0:T(8,128)(2,1)S(...) custom-call(s32[2]{0:T(128)S(1)} %pad_add_fusion.place_ref.refs_0_, ...), custom_call_target="tpu_custom_call" | custom-call | flops 4127195136 | bytes 7323656 | tf_op jit(solution)/shard_map/pallas_call | solution.py:221
  55.0 1.5 collective-permute-start.9
  56.5 4.5 %collective-permute-done.16.refs_12_ = bf16[96,1152]{1,0:T(8,128)(2,1)S(1)} collective-permute-done((bf16[96,1152]{1,0:T(8,128)(2,1)S(1)}, bf16[96,1152]{1,0:T(8,128)(2,1)S(1)}, u32[]{:S(2)}, u32[]{:S(2)}) %collective-permute-start.16) | collective-permute-done | bytes 221216 | tf_op jit(solution)/shard_map/ppermute | solution.py:38
  61.0 13.8 %collective-permute-done.17.refs_13_ = bf16[96,1152]{1,0:T(8,128)(2,1)S(1)} collective-permute-done((bf16[96,1152]{1,0:T(8,128)(2,1)S(1)}, bf16[96,1152]{1,0:T(8,128)(2,1)S(1)}, u32[]{:S(2)}, u32[]{:S(2)}) %collective-permute-start.17) | collective-permute-done | bytes 221216 | tf_op jit(solution)/shard_map/ppermute | solution.py:38
  75.7 1.5 collective-permute-start.14
  77.2 1.7 collective-permute-start.11
  78.8 17.1 %collective-permute-done.14.refs_10_ = bf16[96,1152]{1,0:T(8,128)(2,1)S(1)} collective-permute-done((bf16[96,1152]{1,0:T(8,128)(2,1)S(1)}, bf16[96,1152]{1,0:T(8,128)(2,1)S(1)}, u32[]{:S(2)}, u32[]{:S(2)}) %collective-permute-start.14) | collective-permute-done | bytes 221216 | tf_op jit(solution)/shard_map/ppermute | solution.py:38
  96.7 2.0 collective-permute-start.8
  101.3 1.5 copy-done.26
  105.7 1.4 copy-done.52
  107.1 11.2 %shard_map.307 = (bf16[768,768]{1,0:T(8,128)(2,1)S(1)}, bf16[1024,768]{1,0:T(8,128)(2,1)S(1)}, bf16[1024,768]{1,0:T(8,128)(2,1)S(1)}, bf16[1024,768]{1,0:T(8,128...) custom-call(s32[2]{0:T(128)S(1)} %pad_add_fusion.place_ref.refs_0_, ...), custom_call_target="tpu_custom_call" | custom-call | flops 6039797760 | bytes 18926600 | tf_op jit(solution)/shard_map/pallas_call | solution.py:221
  118.8 1.9 collective-permute-done.19.near_ref
  120.9 10.3 %collective-permute-done.20.far_ref = bf16[256,768]{1,0:T(8,128)(2,1)S(1)} collective-permute-done((bf16[256,768]{1,0:T(8,128)(2,1)S(1)}, bf16[256,768]{1,0:T(8,128)(2,1)S(1)}, u32[]{:S(2)}, u32[]{:S(2)}) %collective-permute-start.20) | collective-permute-done | bytes 393248 | tf_op jit(solution)/shard_map/ppermute | solution.py:28
  131.2 2.1 shard_map.308
  135.4 8.2 %collective-permute-done.22.branch_c = bf16[256,768]{1,0:T(8,128)(2,1)} collective-permute-done((bf16[256,768]{1,0:T(8,128)(2,1)}, bf16[256,768]{1,0:T(8,128)(2,1)}, u32[]{:S(2)}, u32[]{:S(2)}) %collective-permute-start.22) | collective-permute-done | bytes 393248 | tf_op jit(solution)/shard_map/ppermute | solution.py:28
  143.6 2.1 collective-permute-start.23
  145.7 5.8 %shard_map.309 = (bf16[96,1536]{1,0:T(8,128)(2,1)S(1)}, bf16[96,1536]{1,0:T(8,128)(2,1)S(1)}, bf16[96,1536]{1,0:T(8,128)(2,1)S(1)}, bf16[96,1536]{1,0:T(8,128)(2...) custom-call(s32[2]{0:T(128)S(1)} %pad_add_fusion.place_ref.refs_0_, ...), custom_call_target="tpu_custom_call" | custom-call | flops 3623878656 | bytes 12804104 | tf_op jit(solution)/shard_map/pallas_call | solution.py:221
  173.2 15.6 %shard_map.310 = (bf16[96,832]{1,0:T(8,128)(2,1)S(1)}, bf16[96,832]{1,0:T(8,128)(2,1)S(1)}, bf16[96,832]{1,0:T(8,128)(2,1)S(1)}, bf16[96,832]{1,0:T(8,128)(2,1)S...) custom-call(s32[2]{0:T(128)S(1)} %pad_add_fusion.place_ref.refs_0_, ...), custom_call_target="tpu_custom_call" | custom-call | flops 11676942336 | bytes 12288008 | tf_op jit(solution)/shard_map/pallas_call | solution.py:221
  189.5 2.6 collective-permute-start.40
  192.2 5.8 %collective-permute-done.38 = bf16[96,1536]{1,0:T(8,128)(2,1)S(1)} collective-permute-done((bf16[96,1536]{1,0:T(8,128)(2,1)S(1)}, bf16[96,1536]{1,0:T(8,128)(2,1)S(1)}, u32[]{:S(2)}, u32[]{:S(2)}) %collective-permute-start.38) | collective-permute-done | bytes 294944 | tf_op jit(solution)/shard_map/ppermute | solution.py:38
  198.0 2.1 collective-permute-start.42
  200.4 2.3 collective-permute-start.44
  202.9 4.7 %collective-permute-done.40 = bf16[96,1536]{1,0:T(8,128)(2,1)S(1)} collective-permute-done((bf16[96,1536]{1,0:T(8,128)(2,1)S(1)}, bf16[96,1536]{1,0:T(8,128)(2,1)S(1)}, u32[]{:S(2)}, u32[]{:S(2)}) %collective-permute-start.40) | collective-permute-done | bytes 294944 | tf_op jit(solution)/shard_map/ppermute | solution.py:38
  207.9 2.6 collective-permute-done.41
  211.9 23.6 %collective-permute-done.42 = bf16[96,1536]{1,0:T(8,128)(2,1)S(1)} collective-permute-done((bf16[96,1536]{1,0:T(8,128)(2,1)S(1)}, bf16[96,1536]{1,0:T(8,128)(2,1)S(1)}, u32[]{:S(2)}, u32[]{:S(2)}) %collective-permute-start.42) | collective-permute-done | bytes 294944 | tf_op jit(solution)/shard_map/ppermute | solution.py:38
  235.5 2.0 collective-permute-start.25
  237.4 5.4 %collective-permute-done.43 = bf16[96,1536]{1,0:T(8,128)(2,1)S(1)} collective-permute-done((bf16[96,1536]{1,0:T(8,128)(2,1)S(1)}, bf16[96,1536]{1,0:T(8,128)(2,1)S(1)}, u32[]{:S(2)}, u32[]{:S(2)}) %collective-permute-start.43) | collective-permute-done | bytes 294944 | tf_op jit(solution)/shard_map/ppermute | solution.py:38
  242.9 8.2 %collective-permute-done.44 = bf16[96,1536]{1,0:T(8,128)(2,1)S(1)} collective-permute-done((bf16[96,1536]{1,0:T(8,128)(2,1)S(1)}, bf16[96,1536]{1,0:T(8,128)(2,1)S(1)}, u32[]{:S(2)}, u32[]{:S(2)}) %collective-permute-start.44) | collective-permute-done | bytes 294944 | tf_op jit(solution)/shard_map/ppermute | solution.py:38
  252.9 4.8 %collective-permute-start.28 = (bf16[96,832]{1,0:T(8,128)(2,1)S(1)}, bf16[96,832]{1,0:T(8,128)(2,1)S(1)}, u32[]{:S(2)}, u32[]{:S(2)}) collective-permute-start(bf16[96,832]{1,0:T(8,128)(2,1)S(1)} %get-tuple-element.136), channel_id=1, source_target_pairs={{0,5},{1,4},{2,7},{3,6},{4,1},{5,0},{6,3},{7,2},{8,13},{9,12},{10,... | collective-permute-start | bytes 479240 | tf_op jit(solution)/shard_map/ppermute | solution.py:38
  258.9 4.6 %collective-permute-start.30 = (bf16[96,832]{1,0:T(8,128)(2,1)S(1)}, bf16[96,832]{1,0:T(8,128)(2,1)S(1)}, u32[]{:S(2)}, u32[]{:S(2)}) collective-permute-start(bf16[96,832]{1,0:T(8,128)(2,1)S(1)} %get-tuple-element.138), channel_id=1, source_target_pairs={{0,7},{1,6},{2,5},{3,4},{4,3},{5,2},{6,1},{7,0},{8,15},{9,14},{10,... | collective-permute-start | bytes 479240 | tf_op jit(solution)/shard_map/ppermute | solution.py:38
  264.4 2.0 shard_map.311
  266.5 8.2 %collective-permute-done.28 = bf16[96,832]{1,0:T(8,128)(2,1)S(1)} collective-permute-done((bf16[96,832]{1,0:T(8,128)(2,1)S(1)}, bf16[96,832]{1,0:T(8,128)(2,1)S(1)}, u32[]{:S(2)}, u32[]{:S(2)}) %collective-permute-start.28) | collective-permute-done | bytes 159776 | tf_op jit(solution)/shard_map/ppermute | solution.py:38
  274.7 4.7 %collective-permute-done.29 = bf16[96,832]{1,0:T(8,128)(2,1)S(1)} collective-permute-done((bf16[96,832]{1,0:T(8,128)(2,1)S(1)}, bf16[96,832]{1,0:T(8,128)(2,1)S(1)}, u32[]{:S(2)}, u32[]{:S(2)}) %collective-permute-start.29) | collective-permute-done | bytes 159776 | tf_op jit(solution)/shard_map/ppermute | solution.py:38
  279.4 6.4 %collective-permute-done.30 = bf16[96,832]{1,0:T(8,128)(2,1)S(1)} collective-permute-done((bf16[96,832]{1,0:T(8,128)(2,1)S(1)}, bf16[96,832]{1,0:T(8,128)(2,1)S(1)}, u32[]{:S(2)}, u32[]{:S(2)}) %collective-permute-start.30) | collective-permute-done | bytes 159776 | tf_op jit(solution)/shard_map/ppermute | solution.py:38
  286.4 2.1 collective-permute-start.45
  290.3 3.0 collective-permute-start.37
  293.3 3.3 %shard_map.314 = (f32[384,768]{1,0:T(8,128)}, f32[384,768]{1,0:T(8,128)}, f32[384,768]{1,0:T(8,128)}) custom-call(s32[2]{0:T(128)S(1)} %pad_add_fusion.place_ref.refs_0_, bf16[96,1536]{1,0:T(8,128)(2,1)S(1)} %add_convert_fusion.4.refs_0_, bf16[96,1536]{1,0:T(8,128)(2,1)S(1)} %collective-permute-done.45.refs_1_, ...), custom_call_target="tpu_custom_call" | custom-call | flops 5898240 | bytes 7667712 | tf_op jit(solution)/shard_map/pallas_call | solution.py:632
  296.7 3.4 %shard_map.313 = (f32[96,3072]{1,0:T(8,128)}, f32[96,3072]{1,0:T(8,128)}, f32[96,3072]{1,0:T(8,128)}) custom-call(s32[2]{0:T(128)S(1)} %pad_add_fusion.place_ref.refs_0_, bf16[96,1536]{1,0:T(8,128)(2,1)S(1)} %add_convert_fusion.4.refs_0_, bf16[96,1536]{1,0:T(8,128)(2,1)S(1)} %collective-permute-done.45.refs_1_, ...), custom_call_target="tpu_custom_call" | custom-call | flops 5898240 | bytes 7667712 | tf_op jit(solution)/shard_map/pallas_call | solution.py:632
  300.2 3.5 %shard_map.312 = (f32[96,2304]{1,0:T(8,128)}, f32[96,2304]{1,0:T(8,128)}, f32[96,2304]{1,0:T(8,128)}, f32[96,768]{1,0:T(8,128)}, f32[96,768]{1,0:T(8,128)}, /*in...) custom-call(s32[2]{0:T(128)S(1)} %pad_add_fusion.place_ref.refs_0_, ...), custom_call_target="tpu_custom_call" | custom-call | flops 4423680 | bytes 7744520 | tf_op jit(solution)/shard_map/pallas_call | solution.py:221
  (226 shorter events, 54.9 us)
Async XLA Ops:
  7.2 94.1 %all-gather.2.cloned.1.call-start = ((), (), s32[]{:S(2)}) async-start(), calls=%async_computation | async-start | bytes 1990656 | tf_op jit(solution)/shard_map/all_gather | solution.py:725
  15.7 10.6 %collective-permute-start.1 = (bf16[272,768]{1,0:T(8,128)(2,1)S(1)}, bf16[272,768]{1,0:T(8,128)(2,1)S(1)}, u32[]{:S(2)}, u32[]{:S(2)}) collective-permute-start(bf16[272,768]{1,0:T(8,128)(2,1)S(1)} %fusion.1.refs_1_), channel_id=1, source_target_pairs={{0,16},{8,24},{16,0},{24,8},{1,17},{9,25},{17,1},{25,9},{2,18},{10... | collective-permute-start | bytes 1253384 | tf_op jit(solution)/shard_map/ppermute | solution.py:28
  17.0 10.8 %collective-permute-start.6 = (bf16[96,640]{1,0:T(8,128)(2,1)S(1)}, bf16[96,640]{1,0:T(8,128)(2,1)S(1)}, u32[]{:S(2)}, u32[]{:S(2)}) collective-permute-start(bf16[96,640]{1,0:T(8,128)(2,1)S(1)} %get-tuple-element.103.refs_5_), channel_id=1, source_target_pairs={{0,6},{1,7},{2,4},{3,5},{4,2},{5,3},{6,0},{7,1},{8,14},{9,15},{10,... | collective-permute-start | bytes 368648 | tf_op jit(solution)/shard_map/ppermute | solution.py:38
  18.3 9.5 %collective-permute-start.4 = (bf16[96,640]{1,0:T(8,128)(2,1)S(1)}, bf16[96,640]{1,0:T(8,128)(2,1)S(1)}, u32[]{:S(2)}, u32[]{:S(2)}) collective-permute-start(bf16[96,640]{1,0:T(8,128)(2,1)S(1)} %get-tuple-element.103.refs_5_), channel_id=1, source_target_pairs={{0,2},{1,3},{2,0},{3,1},{4,6},{5,7},{6,4},{7,5},{8,10},{9,11},{10,... | collective-permute-start | bytes 368648 | tf_op jit(solution)/shard_map/ppermute | solution.py:38
  20.5 7.3 %collective-permute-start.5 = (bf16[96,640]{1,0:T(8,128)(2,1)S(1)}, bf16[96,640]{1,0:T(8,128)(2,1)S(1)}, u32[]{:S(2)}, u32[]{:S(2)}) collective-permute-start(bf16[96,640]{1,0:T(8,128)(2,1)S(1)} %get-tuple-element.103.refs_5_), channel_id=1, source_target_pairs={{0,4},{1,5},{2,6},{3,7},{4,0},{5,1},{6,2},{7,3},{8,12},{9,13},{10,... | collective-permute-start | bytes 368648 | tf_op jit(solution)/shard_map/ppermute | solution.py:38
  20.5 19.8 %collective-permute-start = (bf16[272,768]{1,0:T(8,128)(2,1)S(1)}, bf16[272,768]{1,0:T(8,128)(2,1)S(1)}, u32[]{:S(2)}, u32[]{:S(2)}) collective-permute-start(bf16[272,768]{1,0:T(8,128)(2,1)S(1)} %fusion.1.refs_1_), channel_id=1, source_target_pairs={{0,8},{8,0},{16,24},{24,16},{1,9},{9,1},{17,25},{25,17},{2,10},{10... | collective-permute-start | bytes 1253384 | tf_op jit(solution)/shard_map/ppermute | solution.py:28
  26.2 15.8 %collective-permute-start.2 = (bf16[272,768]{1,0:T(8,128)(2,1)S(1)}, bf16[272,768]{1,0:T(8,128)(2,1)S(1)}, u32[]{:S(2)}, u32[]{:S(2)}) collective-permute-start(bf16[272,768]{1,0:T(8,128)(2,1)S(1)} %collective-permute-done.1.refs_3_), channel_id=1, source_target_pairs={{0,8},{8,0},{16,24},{24,16},{1,9},{9,1},{17,25},{25,17},{2,10},{10... | collective-permute-start | bytes 1253384 | tf_op jit(solution)/shard_map/ppermute | solution.py:28
  27.8 14.2 %collective-permute-start.7 = (bf16[288,640]{1,0:T(8,128)(2,1)S(1)}, bf16[288,640]{1,0:T(8,128)(2,1)S(1)}, u32[]{:S(2)}, u32[]{:S(2)}) collective-permute-start(bf16[288,640]{1,0:T(8,128)(2,1)S(1)} %pad_maximum_fusion.1), channel_id=1, source_target_pairs={{0,1},{1,0},{2,3},{3,2},{4,5},{5,4},{6,7},{7,6},{8,9},{9,8},{10,11... | collective-permute-start | bytes 1105928 | tf_op jit(solution)/shard_map/ppermute | solution.py:38
  28.2 7.8 %collective-permute-start.3 = (bf16[96,640]{1,0:T(8,128)(2,1)S(1)}, bf16[96,640]{1,0:T(8,128)(2,1)S(1)}, u32[]{:S(2)}, u32[]{:S(2)}) collective-permute-start(bf16[96,640]{1,0:T(8,128)(2,1)S(1)} %get-tuple-element.103.refs_5_), channel_id=1, source_target_pairs={{0,1},{1,0},{2,3},{3,2},{4,5},{5,4},{6,7},{7,6},{8,9},{9,8},{10,11... | collective-permute-start | bytes 368648 | tf_op jit(solution)/shard_map/ppermute | solution.py:38
  29.4 27.2 %collective-permute-start.15 = (bf16[96,1152]{1,0:T(8,128)(2,1)S(1)}, bf16[96,1152]{1,0:T(8,128)(2,1)S(1)}, u32[]{:S(2)}, u32[]{:S(2)}) collective-permute-start(bf16[96,1152]{1,0:T(8,128)(2,1)S(1)} %get-tuple-element.107.refs_9_), channel_id=1, source_target_pairs={{0,2},{1,3},{2,0},{3,1},{4,6},{5,7},{6,4},{7,5},{8,10},{9,11},{10,... | collective-permute-start | bytes 663560 | tf_op jit(solution)/shard_map/ppermute | solution.py:38
  36.0 25.1 %collective-permute-start.16 = (bf16[96,1152]{1,0:T(8,128)(2,1)S(1)}, bf16[96,1152]{1,0:T(8,128)(2,1)S(1)}, u32[]{:S(2)}, u32[]{:S(2)}) collective-permute-start(bf16[96,1152]{1,0:T(8,128)(2,1)S(1)} %get-tuple-element.107.refs_9_), channel_id=1, source_target_pairs={{0,4},{1,5},{2,6},{3,7},{4,0},{5,1},{6,2},{7,3},{8,12},{9,13},{10,... | collective-permute-start | bytes 663560 | tf_op jit(solution)/shard_map/ppermute | solution.py:38
  40.2 34.6 %collective-permute-start.17 = (bf16[96,1152]{1,0:T(8,128)(2,1)S(1)}, bf16[96,1152]{1,0:T(8,128)(2,1)S(1)}, u32[]{:S(2)}, u32[]{:S(2)}) collective-permute-start(bf16[96,1152]{1,0:T(8,128)(2,1)S(1)} %get-tuple-element.107.refs_9_), channel_id=1, source_target_pairs={{0,6},{1,7},{2,4},{3,5},{4,2},{5,3},{6,0},{7,1},{8,14},{9,15},{10,... | collective-permute-start | bytes 663560 | tf_op jit(solution)/shard_map/ppermute | solution.py:38
  42.0 36.8 %collective-permute-start.12 = (bf16[256,768]{1,0:T(8,128)(2,1)S(1)}, bf16[256,768]{1,0:T(8,128)(2,1)S(1)}, u32[]{:S(2)}, u32[]{:S(2)}) collective-permute-start(bf16[256,768]{1,0:T(8,128)(2,1)S(1)} %copy-done.15), channel_id=1, source_target_pairs={{0,16},{8,24},{16,0},{24,8},{1,17},{9,25},{17,1},{25,9},{2,18},{10... | collective-permute-start | bytes 1179656 | tf_op jit(solution)/shard_map/ppermute | solution.py:28
  55.0 43.7 %collective-permute-start.9 = (bf16[1024,192]{1,0:T(8,128)(2,1)S(1)}, bf16[1024,192]{1,0:T(8,128)(2,1)}, u32[]{:S(2)}, u32[]{:S(2)}) collective-permute-start(bf16[1024,192]{1,0:T(8,128)(2,1)S(1)} %get-tuple-element.104.refs_1_.attended_a), channel_id=1, source_target_pairs={{0,16},{8,24},{16,0},{24,8},{1,17},{9,25},{17,1},{25,9},{2,18},{10... | collective-permute-start | bytes 1179656 | tf_op jit(solution)/shard_map/ppermute | solution.py:28
  75.7 23.3 %collective-permute-start.18 = (bf16[288,1152]{1,0:T(8,128)(2,1)}, bf16[288,1152]{1,0:T(8,128)(2,1)S(1)}, u32[]{:S(2)}, u32[]{:S(2)}) collective-permute-start(bf16[288,1152]{1,0:T(8,128)(2,1)} %pad_maximum_fusion), channel_id=1, source_target_pairs={{0,1},{1,0},{2,3},{3,2},{4,5},{5,4},{6,7},{7,6},{8,9},{9,8},{10,11... | collective-permute-start | bytes 1990664 | tf_op jit(solution)/shard_map/ppermute | solution.py:38
  75.7 20.3 %collective-permute-start.14 = (bf16[96,1152]{1,0:T(8,128)(2,1)S(1)}, bf16[96,1152]{1,0:T(8,128)(2,1)S(1)}, u32[]{:S(2)}, u32[]{:S(2)}) collective-permute-start(bf16[96,1152]{1,0:T(8,128)(2,1)S(1)} %get-tuple-element.107.refs_9_), channel_id=1, source_target_pairs={{0,1},{1,0},{2,3},{3,2},{4,5},{5,4},{6,7},{7,6},{8,9},{9,8},{10,11... | collective-permute-start | bytes 663560 | tf_op jit(solution)/shard_map/ppermute | solution.py:38
  77.2 21.8 %collective-permute-start.11 = (bf16[256,768]{1,0:T(8,128)(2,1)S(1)}, bf16[256,768]{1,0:T(8,128)(2,1)}, u32[]{:S(2)}, u32[]{:S(2)}) collective-permute-start(bf16[256,768]{1,0:T(8,128)(2,1)S(1)} %copy-done.15), channel_id=1, source_target_pairs={{0,8},{8,0},{16,24},{24,16},{1,9},{9,1},{17,25},{25,17},{2,10},{10... | collective-permute-start | bytes 1179656 | tf_op jit(solution)/shard_map/ppermute | solution.py:28
  78.8 20.1 %collective-permute-start.13 = (bf16[256,768]{1,0:T(8,128)(2,1)S(1)}, bf16[256,768]{1,0:T(8,128)(2,1)}, u32[]{:S(2)}, u32[]{:S(2)}) collective-permute-start(bf16[256,768]{1,0:T(8,128)(2,1)S(1)} %collective-permute-done.12.refs_7_), channel_id=1, source_target_pairs={{0,8},{8,0},{16,24},{24,16},{1,9},{9,1},{17,25},{25,17},{2,10},{10... | collective-permute-start | bytes 1179656 | tf_op jit(solution)/shard_map/ppermute | solution.py:28
  96.7 3.7 %collective-permute-start.8 = (bf16[1024,192]{1,0:T(8,128)(2,1)S(1)}, bf16[1024,192]{1,0:T(8,128)(2,1)}, u32[]{:S(2)}, u32[]{:S(2)}) collective-permute-start(bf16[1024,192]{1,0:T(8,128)(2,1)S(1)} %get-tuple-element.104.refs_1_.attended_a), channel_id=1, source_target_pairs={{0,8},{8,0},{16,24},{24,16},{1,9},{9,1},{17,25},{25,17},{2,10},{10... | collective-permute-start | bytes 1179656 | tf_op jit(solution)/shard_map/ppermute | solution.py:28
  98.7 2.6 collective-permute-start.10
  120.8 10.4 %collective-permute-start.20 = (bf16[256,768]{1,0:T(8,128)(2,1)S(1)}, bf16[256,768]{1,0:T(8,128)(2,1)S(1)}, u32[]{:S(2)}, u32[]{:S(2)}) collective-permute-start(bf16[256,768]{1,0:T(8,128)(2,1)S(1)} %add_convert_fusion.3), channel_id=1, source_target_pairs={{0,16},{8,24},{16,0},{24,8},{1,17},{9,25},{17,1},{25,9},{2,18},{10... | collective-permute-start | bytes 1179656 | tf_op jit(solution)/shard_map/ppermute | solution.py:28
  133.9 9.7 %collective-permute-start.22 = (bf16[256,768]{1,0:T(8,128)(2,1)}, bf16[256,768]{1,0:T(8,128)(2,1)}, u32[]{:S(2)}, u32[]{:S(2)}) collective-permute-start(bf16[256,768]{1,0:T(8,128)(2,1)} %get-tuple-element.115.branch_a), channel_id=1, source_target_pairs={{0,16},{8,24},{16,0},{24,8},{1,17},{9,25},{17,1},{25,9},{2,18},{10... | collective-permute-start | bytes 1179656 | tf_op jit(solution)/shard_map/ppermute | solution.py:28
  134.2 26.8 %collective-permute-start.21 = (bf16[256,768]{1,0:T(8,128)(2,1)}, bf16[256,768]{1,0:T(8,128)(2,1)}, u32[]{:S(2)}, u32[]{:S(2)}) collective-permute-start(bf16[256,768]{1,0:T(8,128)(2,1)} %get-tuple-element.115.branch_a), channel_id=1, source_target_pairs={{0,8},{8,0},{16,24},{24,16},{1,9},{9,1},{17,25},{25,17},{2,10},{10... | collective-permute-start | bytes 1179656 | tf_op jit(solution)/shard_map/ppermute | solution.py:28
  143.6 17.4 %collective-permute-start.23 = (bf16[256,768]{1,0:T(8,128)(2,1)}, bf16[256,768]{1,0:T(8,128)(2,1)}, u32[]{:S(2)}, u32[]{:S(2)}) collective-permute-start(bf16[256,768]{1,0:T(8,128)(2,1)} %collective-permute-done.22.branch_c), channel_id=1, source_target_pairs={{0,8},{8,0},{16,24},{24,16},{1,9},{9,1},{17,25},{25,17},{2,10},{10... | collective-permute-start | bytes 1179656 | tf_op jit(solution)/shard_map/ppermute | solution.py:28
  160.9 39.1 %collective-permute-start.33 = (bf16[512,768]{1,0:T(8,128)(2,1)}, bf16[512,768]{1,0:T(8,128)(2,1)S(1)}, u32[]{:S(2)}, u32[]{:S(2)}) collective-permute-start(bf16[512,768]{1,0:T(8,128)(2,1)} %copy-done.27), channel_id=1, source_target_pairs={{0,8},{8,0},{16,24},{24,16},{1,9},{9,1},{17,25},{25,17},{2,10},{10... | collective-permute-start | bytes 2359304 | tf_op jit(solution)/shard_map/ppermute | solution.py:28
  188.9 11.6 %collective-permute-start.31 = (bf16[512,768]{1,0:T(8,128)(2,1)S(1)}, bf16[512,768]{1,0:T(8,128)(2,1)S(1)}, u32[]{:S(2)}, u32[]{:S(2)}) collective-permute-start(bf16[512,768]{1,0:T(8,128)(2,1)S(1)} %get-tuple-element.140), channel_id=1, source_target_pairs={{0,8},{8,0},{16,24},{24,16},{1,9},{9,1},{17,25},{25,17},{2,10},{10... | collective-permute-start | bytes 2359304 | tf_op jit(solution)/shard_map/ppermute | solution.py:28
  189.4 8.6 %collective-permute-start.38 = (bf16[96,1536]{1,0:T(8,128)(2,1)S(1)}, bf16[96,1536]{1,0:T(8,128)(2,1)S(1)}, u32[]{:S(2)}, u32[]{:S(2)}) collective-permute-start(bf16[96,1536]{1,0:T(8,128)(2,1)S(1)} %copy-done.44), channel_id=1, source_target_pairs={{0,1},{1,0},{2,3},{3,2},{4,5},{5,4},{6,7},{7,6},{8,9},{9,8},{10,11... | collective-permute-start | bytes 884744 | tf_op jit(solution)/shard_map/ppermute | solution.py:38
  189.4 8.6 %collective-permute-start.39 = (bf16[96,1536]{1,0:T(8,128)(2,1)S(1)}, bf16[96,1536]{1,0:T(8,128)(2,1)S(1)}, u32[]{:S(2)}, u32[]{:S(2)}) collective-permute-start(bf16[96,1536]{1,0:T(8,128)(2,1)S(1)} %copy-done.42), channel_id=1, source_target_pairs={{0,2},{1,3},{2,0},{3,1},{4,6},{5,7},{6,4},{7,5},{8,10},{9,11},{10,... | collective-permute-start | bytes 884744 | tf_op jit(solution)/shard_map/ppermute | solution.py:38
  189.5 18.1 %collective-permute-start.40 = (bf16[96,1536]{1,0:T(8,128)(2,1)S(1)}, bf16[96,1536]{1,0:T(8,128)(2,1)S(1)}, u32[]{:S(2)}, u32[]{:S(2)}) collective-permute-start(bf16[96,1536]{1,0:T(8,128)(2,1)S(1)} %copy-done.40), channel_id=1, source_target_pairs={{0,3},{1,2},{2,1},{3,0},{4,7},{5,6},{6,5},{7,4},{8,11},{9,10},{10,... | collective-permute-start | bytes 884744 | tf_op jit(solution)/shard_map/ppermute | solution.py:38
  198.0 12.6 %collective-permute-start.41 = (bf16[96,1536]{1,0:T(8,128)(2,1)S(1)}, bf16[96,1536]{1,0:T(8,128)(2,1)S(1)}, u32[]{:S(2)}, u32[]{:S(2)}) collective-permute-start(bf16[96,1536]{1,0:T(8,128)(2,1)S(1)} %copy-done.38), channel_id=1, source_target_pairs={{0,4},{1,5},{2,6},{3,7},{4,0},{5,1},{6,2},{7,3},{8,12},{9,13},{10,... | collective-permute-start | bytes 884744 | tf_op jit(solution)/shard_map/ppermute | solution.py:38
  198.0 37.5 %collective-permute-start.42 = (bf16[96,1536]{1,0:T(8,128)(2,1)S(1)}, bf16[96,1536]{1,0:T(8,128)(2,1)S(1)}, u32[]{:S(2)}, u32[]{:S(2)}) collective-permute-start(bf16[96,1536]{1,0:T(8,128)(2,1)S(1)} %copy-done.36), channel_id=1, source_target_pairs={{0,5},{1,4},{2,7},{3,6},{4,1},{5,0},{6,3},{7,2},{8,13},{9,12},{10,... | collective-permute-start | bytes 884744 | tf_op jit(solution)/shard_map/ppermute | solution.py:38
  200.1 42.8 %collective-permute-start.43 = (bf16[96,1536]{1,0:T(8,128)(2,1)S(1)}, bf16[96,1536]{1,0:T(8,128)(2,1)S(1)}, u32[]{:S(2)}, u32[]{:S(2)}) collective-permute-start(bf16[96,1536]{1,0:T(8,128)(2,1)S(1)} %copy-done.34), channel_id=1, source_target_pairs={{0,6},{1,7},{2,4},{3,5},{4,2},{5,3},{6,0},{7,1},{8,14},{9,15},{10,... | collective-permute-start | bytes 884744 | tf_op jit(solution)/shard_map/ppermute | solution.py:38
  200.4 50.6 %collective-permute-start.44 = (bf16[96,1536]{1,0:T(8,128)(2,1)S(1)}, bf16[96,1536]{1,0:T(8,128)(2,1)S(1)}, u32[]{:S(2)}, u32[]{:S(2)}) collective-permute-start(bf16[96,1536]{1,0:T(8,128)(2,1)S(1)} %copy-done.32), channel_id=1, source_target_pairs={{0,7},{1,6},{2,5},{3,4},{4,3},{5,2},{6,1},{7,0},{8,15},{9,14},{10,... | collective-permute-start | bytes 884744 | tf_op jit(solution)/shard_map/ppermute | solution.py:38
  207.6 50.1 %collective-permute-start.34 = (bf16[256,768]{1,0:T(8,128)(2,1)S(1)}, bf16[256,768]{1,0:T(8,128)(2,1)S(1)}, u32[]{:S(2)}, u32[]{:S(2)}) collective-permute-start(bf16[256,768]{1,0:T(8,128)(2,1)S(1)} %add_convert_fusion.1), channel_id=1, source_target_pairs={{0,16},{8,24},{16,0},{24,8},{1,17},{9,25},{17,1},{25,9},{2,18},{10... | collective-permute-start | bytes 1179656 | tf_op jit(solution)/shard_map/ppermute | solution.py:28
  210.5 41.1 %collective-permute-start.24 = (bf16[96,832]{1,0:T(8,128)(2,1)S(1)}, bf16[96,832]{1,0:T(8,128)(2,1)S(1)}, u32[]{:S(2)}, u32[]{:S(2)}) collective-permute-start(bf16[96,832]{1,0:T(8,128)(2,1)S(1)} %get-tuple-element.132), channel_id=1, source_target_pairs={{0,1},{1,0},{2,3},{3,2},{4,5},{5,4},{6,7},{7,6},{8,9},{9,8},{10,11... | collective-permute-start | bytes 479240 | tf_op jit(solution)/shard_map/ppermute | solution.py:38
  235.5 17.4 %collective-permute-start.25 = (bf16[96,832]{1,0:T(8,128)(2,1)S(1)}, bf16[96,832]{1,0:T(8,128)(2,1)S(1)}, u32[]{:S(2)}, u32[]{:S(2)}) collective-permute-start(bf16[96,832]{1,0:T(8,128)(2,1)S(1)} %get-tuple-element.133), channel_id=1, source_target_pairs={{0,2},{1,3},{2,0},{3,1},{4,6},{5,7},{6,4},{7,5},{8,10},{9,11},{10,... | collective-permute-start | bytes 479240 | tf_op jit(solution)/shard_map/ppermute | solution.py:38
  242.9 10.0 %collective-permute-start.26 = (bf16[96,832]{1,0:T(8,128)(2,1)S(1)}, bf16[96,832]{1,0:T(8,128)(2,1)S(1)}, u32[]{:S(2)}, u32[]{:S(2)}) collective-permute-start(bf16[96,832]{1,0:T(8,128)(2,1)S(1)} %get-tuple-element.134), channel_id=1, source_target_pairs={{0,3},{1,2},{2,1},{3,0},{4,7},{5,6},{6,5},{7,4},{8,11},{9,10},{10,... | collective-permute-start | bytes 479240 | tf_op jit(solution)/shard_map/ppermute | solution.py:38
  251.0 7.9 %collective-permute-start.32 = (bf16[256,768]{1,0:T(8,128)(2,1)S(1)}, bf16[256,768]{1,0:T(8,128)(2,1)S(1)}, u32[]{:S(2)}, u32[]{:S(2)}) collective-permute-start(bf16[256,768]{1,0:T(8,128)(2,1)S(1)} %add_convert_fusion.2), channel_id=1, source_target_pairs={{0,16},{8,24},{16,0},{24,8},{1,17},{9,25},{17,1},{25,9},{2,18},{10... | collective-permute-start | bytes 1179656 | tf_op jit(solution)/shard_map/ppermute | solution.py:28
  251.7 36.8 %collective-permute-start.46 = (bf16[96,1536]{1,0:T(8,128)(2,1)S(1)}, bf16[96,1536]{1,0:T(8,128)(2,1)S(1)}, u32[]{:S(2)}, u32[]{:S(2)}) collective-permute-start(bf16[96,1536]{1,0:T(8,128)(2,1)S(1)} %add_convert_fusion.4.refs_0_), channel_id=1, source_target_pairs={{0,16},{8,24},{16,0},{24,8},{1,17},{9,25},{17,1},{25,9},{2,18},{10... | collective-permute-start | bytes 884744 | tf_op jit(solution)/shard_map/ppermute | solution.py:28
  252.9 13.6 %collective-permute-start.27 = (bf16[96,832]{1,0:T(8,128)(2,1)S(1)}, bf16[96,832]{1,0:T(8,128)(2,1)S(1)}, u32[]{:S(2)}, u32[]{:S(2)}) collective-permute-start(bf16[96,832]{1,0:T(8,128)(2,1)S(1)} %get-tuple-element.135), channel_id=1, source_target_pairs={{0,4},{1,5},{2,6},{3,7},{4,0},{5,1},{6,2},{7,3},{8,12},{9,13},{10,... | collective-permute-start | bytes 479240 | tf_op jit(solution)/shard_map/ppermute | solution.py:38
  252.9 21.8 %collective-permute-start.28 = (bf16[96,832]{1,0:T(8,128)(2,1)S(1)}, bf16[96,832]{1,0:T(8,128)(2,1)S(1)}, u32[]{:S(2)}, u32[]{:S(2)}) collective-permute-start(bf16[96,832]{1,0:T(8,128)(2,1)S(1)} %get-tuple-element.136), channel_id=1, source_target_pairs={{0,5},{1,4},{2,7},{3,6},{4,1},{5,0},{6,3},{7,2},{8,13},{9,12},{10,... | collective-permute-start | bytes 479240 | tf_op jit(solution)/shard_map/ppermute | solution.py:38
  257.7 21.7 %collective-permute-start.29 = (bf16[96,832]{1,0:T(8,128)(2,1)S(1)}, bf16[96,832]{1,0:T(8,128)(2,1)S(1)}, u32[]{:S(2)}, u32[]{:S(2)}) collective-permute-start(bf16[96,832]{1,0:T(8,128)(2,1)S(1)} %get-tuple-element.137), channel_id=1, source_target_pairs={{0,6},{1,7},{2,4},{3,5},{4,2},{5,3},{6,0},{7,1},{8,14},{9,15},{10,... | collective-permute-start | bytes 479240 | tf_op jit(solution)/shard_map/ppermute | solution.py:38
  258.9 26.8 %collective-permute-start.30 = (bf16[96,832]{1,0:T(8,128)(2,1)S(1)}, bf16[96,832]{1,0:T(8,128)(2,1)S(1)}, u32[]{:S(2)}, u32[]{:S(2)}) collective-permute-start(bf16[96,832]{1,0:T(8,128)(2,1)S(1)} %get-tuple-element.138), channel_id=1, source_target_pairs={{0,7},{1,6},{2,5},{3,4},{4,3},{5,2},{6,1},{7,0},{8,15},{9,14},{10,... | collective-permute-start | bytes 479240 | tf_op jit(solution)/shard_map/ppermute | solution.py:38
  286.0 4.3 %collective-permute-start.36 = (bf16[96,832]{1,0:T(8,128)(2,1)S(1)}, bf16[96,832]{1,0:T(8,128)(2,1)S(1)}, u32[]{:S(2)}, u32[]{:S(2)}) collective-permute-start(bf16[96,832]{1,0:T(8,128)(2,1)S(1)} %add_convert_fusion.5.refs_0_), channel_id=1, source_target_pairs={{0,16},{8,24},{16,0},{24,8},{1,17},{9,25},{17,1},{25,9},{2,18},{10... | collective-permute-start | bytes 479240 | tf_op jit(solution)/shard_map/ppermute | solution.py:28
  286.4 6.9 %collective-permute-start.45 = (bf16[96,1536]{1,0:T(8,128)(2,1)S(1)}, bf16[96,1536]{1,0:T(8,128)(2,1)S(1)}, u32[]{:S(2)}, u32[]{:S(2)}) collective-permute-start(bf16[96,1536]{1,0:T(8,128)(2,1)S(1)} %add_convert_fusion.4.refs_0_), channel_id=1, source_target_pairs={{0,8},{8,0},{16,24},{24,16},{1,9},{9,1},{17,25},{25,17},{2,10},{10... | collective-permute-start | bytes 884744 | tf_op jit(solution)/shard_map/ppermute | solution.py:28
  288.5 4.8 %collective-permute-start.47 = (bf16[96,1536]{1,0:T(8,128)(2,1)S(1)}, bf16[96,1536]{1,0:T(8,128)(2,1)S(1)}, u32[]{:S(2)}, u32[]{:S(2)}) collective-permute-start(bf16[96,1536]{1,0:T(8,128)(2,1)S(1)} %collective-permute-done.46.refs_2_), channel_id=1, source_target_pairs={{0,8},{8,0},{16,24},{24,16},{1,9},{9,1},{17,25},{25,17},{2,10},{10... | collective-permute-start | bytes 884744 | tf_op jit(solution)/shard_map/ppermute | solution.py:28
  288.5 11.6 %collective-permute-start.35 = (bf16[96,832]{1,0:T(8,128)(2,1)S(1)}, bf16[96,832]{1,0:T(8,128)(2,1)S(1)}, u32[]{:S(2)}, u32[]{:S(2)}) collective-permute-start(bf16[96,832]{1,0:T(8,128)(2,1)S(1)} %add_convert_fusion.5.refs_0_), channel_id=1, source_target_pairs={{0,8},{8,0},{16,24},{24,16},{1,9},{9,1},{17,25},{25,17},{2,10},{10... | collective-permute-start | bytes 479240 | tf_op jit(solution)/shard_map/ppermute | solution.py:28
  290.3 9.8 %collective-permute-start.37 = (bf16[96,832]{1,0:T(8,128)(2,1)S(1)}, bf16[96,832]{1,0:T(8,128)(2,1)S(1)}, u32[]{:S(2)}, u32[]{:S(2)}) collective-permute-start(bf16[96,832]{1,0:T(8,128)(2,1)S(1)} %collective-permute-done.36.refs_2_), channel_id=1, source_target_pairs={{0,8},{8,0},{16,24},{24,16},{1,9},{9,1},{17,25},{25,17},{2,10},{10... | collective-permute-start | bytes 479240 | tf_op jit(solution)/shard_map/ppermute | solution.py:28
  (72 other events, 750.7 us)
Sparse Core Ops, SparseCore 0:
  15.7 56.8 all-gather.1
where the time goes:
time: 312 us; the launch traced here: 311 us
  waiting for transfers between devices  136 us (44%)
  starting transfers between devices  60.3 us (19%)
  Pallas kernels  58.3 us (19%)
  local copies, waits for them, and re-layouts  38.8 us (12%)
  between operations  14.7 us (5%)
    ppermute x24, waiting for transfers between devices, swap_shard(): lax.ppermute(block, 'shard', [(i, i ^ bits) for i in range(lax.axis_size(...  107 us
    pallas_call x8, Pallas kernels, call(): pl.pallas_call(kernel, out_shape=tuple(outs), in_specs=[pl.BlockSpec(memo...  51.6 us
    ppermute x24, starting transfers between devices, swap_shard(): lax.ppermute(block, 'shard', [(i, i ^ bits) for i in range(lax.axis_size(...  38.1 us
    unnamed x142, local copies, waits for them, and re-layouts  35.7 us
    ppermute x24, waiting for transfers between devices, swapped(): return lax.ppermute(block, 'rep', [(i, i ^ bit) for i in range(SPAN)])  28.5 us
    ppermute x24, starting transfers between devices, swapped(): return lax.ppermute(block, 'rep', [(i, i ^ bit) for i in range(SPAN)])  22.2 us
    pallas_call x2, Pallas kernels, grid_adam(): pl.pallas_call(kernel, grid=(steps,), out_shape=[shape(rows, columns, dty...  6.68 us
  transfers between devices with their start and end apart: 49, of which 21 were waited for; matrix products, arithmetic and copies ran while one was open for 2% of the time, Pallas kernels for 12%

commit v1 on v0

--- a/solution.py
+++ b/solution.py
@@ -62,34 +62,60 @@
         full = lax.all_gather(block, "shard", axis=0, tiled=True)
         return Pieces([full], None, block.shape[0])
     cross = swap_shard(block, 1)
-    sent = block if gate is None else after(block, gate)
+    sent = block if gate is None else after(block, (gate, cross))
     one = swap_shard(sent, 2)
     two = swap_shard(sent, 4)
     three = swap_shard(sent, 6)
-    other = swap_shard(jnp.concatenate([one, two, three], axis=0), 1)
+    other = jnp.concatenate([one, two, three], axis=0)
+    other = swap_shard(after(other, cross), 1)
     codes = [[0], [1], [2], [4], [6], [3, 5, 7]]
     return Pieces([block, cross, one, two, three, other], codes, block.shape[0])
 
 
-def scatter(blocks):
-    return [blocks[0]] + [swap_shard(block, code + 1) for code, block in enumerate(blocks[1:])]
-
-
-def scatter_end(blocks):
-    total = blocks[0].astype(F32)
-    for block in blocks[1:]:
+def middle_kernel(place_ref, kept_ref, received_ref, own_ref, *sent_refs):
+    high = place_ref[1] // 2
+    rows = own_ref.shape[0]
+    for bits in range(len(sent_refs) + 1):
+        block = pl.ds(pl.multiple_of((high ^ bits) * rows, rows), rows)
+        value = kept_ref[block, :].astype(F32) + received_ref[block, :].astype(F32)
+        if bits == 0:
+            own_ref[...] = value
+        else:
+            sent_refs[bits - 1][...] = value.astype(BF16)
+
+
+def scatter_middle(place, kept, sent):
+    received = swap_shard(sent, 1)
+    count = FEW // 2
+    rows, columns = kept.shape[0] // count, kept.shape[1]
+    own, *sends = call(
+        middle_kernel,
+        [shape(rows, columns, dtype=F32)] + [shape(rows, columns)] * (count - 1),
+        [],
+        kept.size,
+        56,
+        place,
+        kept,
+        received,
+    )
+    return own, [swap_shard(send, 2 * (bits + 1)) for bits, send in enumerate(sends)]
+
+
+def scatter_end(own, received):
+    total = own
+    for block in received:
         total = total + block.astype(F32)
     return total.astype(BF16)
 
 
-def emit(place_ref, full_ref, refs):
-    if len(refs) == 1:
-        refs[0][...] = full_ref[...]
-        return
-    rows = full_ref.shape[0] // len(refs)
-    for code, ref in enumerate(refs):
-        start = pl.multiple_of((place_ref[1] ^ code) * rows, rows)
-        ref[...] = full_ref[pl.ds(start, rows), :]
+def split_halves(place_ref, full_ref, kept_ref, sent_ref):
+    low = place_ref[1] & 1
+    rows = full_ref.shape[0] // FEW
+    for at in range(FEW // 2):
+        target = slice(at * rows, (at + 1) * rows)
+        for ref, bit in ((kept_ref, low), (sent_ref, 1 - low)):
+            start = pl.multiple_of((2 * at + bit) * rows, rows)
+            ref[target, :] = full_ref[pl.ds(start, rows), :]
 
 
 def norm_parts(values):
@@ -440,7 +466,11 @@
             dot(act_ref[block, :], wide_ref[:, -width:]), index ^ rep, near_ref, far_ref, own_ref
         )
 
-    emit(place_ref, grad_ref, grad_refs)
+    if len(grad_refs) == 2:
+        split_halves(place_ref, grad_ref, *grad_refs)
+    else:
+        grad_refs[0][...] = grad_ref[...]
+
 
 def fourth_kernel(
     place_ref,
@@ -565,7 +595,11 @@
             BF16
         )
     grad_ref[:, 4 * part :] = small_grads[...].T[:, :64].astype(BF16)
-    emit(place_ref, grad_ref, grad_refs)
+    if len(grad_refs) == 2:
+        split_halves(place_ref, grad_ref, *grad_refs)
+    else:
+        grad_refs[0][...] = grad_ref[...]
+
 
 def sixth_kernel(
     place_ref, own_ref, near_ref, far_ref, tokens_ref, resid_grad_ref, small_ref, out_ref
@@ -629,7 +663,7 @@
 def grid_adam(kernel, steps, place, blocks, block_spec, arrays):
     rows, columns = arrays[0].shape
     spec = pl.BlockSpec((rows // steps, columns), lambda i: (i, 0))
-    return pl.pallas_call(
+    return list(pl.pallas_call(
         kernel,
         grid=(steps,),
         out_shape=[shape(rows, columns, dtype=F32)] * 3,
@@ -641,7 +675,7 @@
         cost_estimate=pl.CostEstimate(
             flops=20 * rows * columns, bytes_accessed=26 * rows * columns, transcendentals=0
         ),
-    )(place, *blocks, *arrays)
+    )(place, *blocks, *arrays))
 
 
 def in_order(blocks, rep):
@@ -703,7 +737,7 @@
             ],
             [pltpu.VMEM((128, 128), F32)],
             owned * width,
-            16,
+            56,
             place,
             qkv_weight,
             out_weight,
@@ -756,8 +790,8 @@
             shape(8, total, dtype=F32),
         ],
         [pltpu.VMEM((width, 128), BF16)],
-        2 * total * width * 3 * part + 16 * total * total * part,
-        20,
+        12 * total * width * width + 24 * total * total * part,
+        56,
         place,
         *token_blocks,
         *first_pieces.arrays,
@@ -788,8 +822,8 @@
             shape(rows, width, dtype=F32),
         ],
         [pltpu.VMEM((width, ff_part), BF16)],
-        10 * total * width * width,
-        28,
+        32 * total * width * width,
+        56,
         place,
         *attended_blocks,
         *cot_blocks,
@@ -803,7 +837,7 @@
     hidden_two_terms = own, near, far
     *wide_grad, mixed_near, mixed_far, mixed_own, unit_sums = call(
         third_kernel,
-        [shape(owned, 2 * width)] * FEW * few
+        [shape(ff_part // 2, 2 * width)] * 2 * few
         + [shape(ff_part, 2 * width)] * (not few)
         + [
             shape(2 * rows, width),
@@ -812,8 +846,8 @@
             shape(8, ff_part, dtype=F32),
         ],
         [pltpu.VMEM((ff_part, 2 * width), BF16)],
-        6 * total * width * width,
-        22,
+        18 * total * width * width,
+        56,
         place,
         after(act_low, far_send),
         hidden_two,
@@ -821,8 +855,8 @@
         all_cot,
         third_full,
     )
-    if few:
-        wide_blocks = scatter(lax.optimization_barrier((wide_grad, far))[0])
+    near, unit_sums = lax.optimization_barrier((near, unit_sums))
+    hidden_two_terms = own, near, far
     resid_grad, branch, sums = call(
         fourth_kernel,
         [
@@ -832,7 +866,7 @@
         ],
         [],
         10 * rows * width,
-        16,
+        56,
         place,
         *hidden_two_terms,
         residual,
@@ -841,13 +875,17 @@
     )
     branch_blocks = rep_blocks(branch)
     near_mixed, far_mixed, _ = rep_sum(after(mixed_near, branch), mixed_far, branch_blocks[2])
+    if few:
+        kept = after(wide_grad[0], branch_blocks[2])
+        wide_own, wide_received = scatter_middle(place, kept, after(wide_grad[1], far))
+        branch_blocks = (after(branch, wide_own),) + branch_blocks[1:]
     unit_rows = lax.dynamic_update_slice(
         jnp.zeros((shards, SPAN, units), F32), unit_sums[0].reshape(shards, 1, units), (0, rep, 0)
     ).reshape(ff // width, width)
     unit_rows = jnp.pad(unit_rows, ((0, 8 - ff // width), (0, 0)))
     *last_grad, near_send, far_part, own = call(
         fifth_kernel,
-        [shape(owned, 4 * part + 64)] * FEW * few
+        [shape(width // 2, 4 * part + 64)] * 2 * few
         + [shape(width, 4 * part + 64)] * (not few)
         + [
             shape(2 * rows, width),
@@ -864,8 +902,8 @@
             pltpu.VMEM((width, 4 * part + 64), BF16),
             pltpu.VMEM((total, width), BF16),
         ],
-        6 * total * width * width + 40 * total * total * part,
-        32,
+        12 * total * width * width + 72 * total * total * part,
+        56,
         place,
         *branch_blocks,
         *attended_blocks,
@@ -884,8 +922,10 @@
     )
     near, far, far_send = rep_sum(near_send, far_part)
     if few:
-        last_blocks = scatter(last_grad)
-        wide_blocks = rep_blocks(scatter_end(wide_blocks))
+        last_kept, last_sent = last_grad
+        last_sent, wide_received = lax.optimization_barrier((last_sent, wide_received))
+        last_own, last_received = scatter_middle(place, last_kept, last_sent)
+        wide_blocks = rep_blocks(scatter_end(wide_own, wide_received))
     else:
         last_total, wide_total = (
             lax.psum_scatter(grad, "shard", scatter_dimension=0, tiled=True)
@@ -901,7 +941,7 @@
         [shape(rows, width, dtype=F32)],
         [],
         10 * rows * width,
-        16,
+        56,
         place,
         own,
         near,
@@ -927,17 +967,17 @@
             pl.BlockSpec((units, width), lambda i: (0, 0)),
             (down_weight, down_first, down_second),
         )
-        last_blocks, input_grad, mixed = lax.optimization_barrier(
-            (last_blocks, input_grad, mixed)
-        )
-        last_total = scatter_end(last_blocks)
+        last_received, input_grad, mixed, up_res[0], down_res[0] = lax.optimization_barrier(
+            (last_received, input_grad, mixed, up_res[0], down_res[0])
+        )
+        last_total = scatter_end(last_own, last_received)
         results = call(
             adam_kernel,
             [shape(*ref.shape, dtype=F32) for ref in (qkv_weight, out_weight, small_weights)
              for _ in range(3)],
             [],
             20 * qkv_weight.size,
-            24,
+            56,
             place,
             *rep_blocks(last_total),
             qkv_weight,

time: 312 us -> 246 us (0.79)
  waiting for transfers between devices: 136 us -> 59.2 us
  Pallas kernels: 58.3 us -> 85.2 us
  local copies, waits for them, and re-layouts: 38.8 us -> 14 us
  other arithmetic: 2.65 us -> 7.63 us
    ppermute x24 -> x18, waiting for transfers between devices: 107 us -> 48.7 us  [swap_shard(): lax.ppermute(block, 'shard', [(i, i ^ bits) for i in range(lax.axis_size(...]
    unnamed x142 -> x88, local copies, waits for them, and re-layouts: 35.7 us -> 5.53 us
    pallas_call x8 -> x10, Pallas kernels: 51.6 us -> 78.5 us  [call(): pl.pallas_call(kernel, out_shape=tuple(outs), in_specs=[pl.BlockSpec(memo...]
    ppermute x24, starting transfers between devices: 22.2 us -> 40.5 us  [swapped(): return lax.ppermute(block, 'rep', [(i, i ^ bit) for i in range(SPAN)])]
    ppermute x24, waiting for transfers between devices: 28.5 us -> 10.5 us  [swapped(): return lax.ppermute(block, 'rep', [(i, i ^ bit) for i in range(SPAN)])]
    ppermute x24 -> x18, starting transfers between devices: 38.1 us -> 20.5 us  [swap_shard(): lax.ppermute(block, 'shard', [(i, i ^ bits) for i in range(lax.axis_size(...]
    convert_element_type x3, other arithmetic: 0.22 us -> 4.27 us  [rep_sum(): far_send = (far_part + near[:rows].astype(F32)).astype(BF16)]
  transfers between devices with their start and end apart: 49 -> 43, of which waited for: 21 -> 12; matrix products, arithmetic and copies ran while one was open for 2% -> 6% of each run, Pallas kernels for 12% -> 24%
where the time goes in v1:
time: 246 us; the launch traced here: 242 us
  Pallas kernels  85.2 us (35%)
  starting transfers between devices  61 us (25%)
  waiting for transfers between devices  59.2 us (24%)
  between operations  14.6 us (6%)
  local copies, waits for them, and re-layouts  14 us (6%)
  other arithmetic  7.63 us (3%)
    pallas_call x10, Pallas kernels, call(): pl.pallas_call(kernel, out_shape=tuple(outs), in_specs=[pl.BlockSpec(memo...  78.5 us
    ppermute x18, waiting for transfers between devices, swap_shard(): lax.ppermute(block, 'shard', [(i, i ^ bits) for i in range(lax.axis_size(...  48.7 us
    ppermute x24, starting transfers between devices, swapped(): return lax.ppermute(block, 'rep', [(i, i ^ bit) for i in range(SPAN)])  40.5 us
    ppermute x18, starting transfers between devices, swap_shard(): lax.ppermute(block, 'shard', [(i, i ^ bits) for i in range(lax.axis_size(...  20.5 us
    ppermute x24, waiting for transfers between devices, swapped(): return lax.ppermute(block, 'rep', [(i, i ^ bit) for i in range(SPAN)])  10.5 us
    pallas_call x2, Pallas kernels, grid_adam(): pl.pallas_call(kernel, grid=(steps,), out_shape=[shape(rows, columns, dty...  6.67 us
    unnamed x88, local copies, waits for them, and re-layouts  5.53 us
  transfers between devices with their start and end apart: 43, of which 12 were waited for; matrix products, arithmetic and copies ran while one was open for 6% of the time, Pallas kernels for 24%

profile of v1, /device:TPU:11, one launch (start us, length us, event | category | flops | bytes accessed | tf_op | source)
XLA Modules:
  0.0 241.7 jit_solution(8161307816990485820)
XLA Ops:
  7.9 4.5 %shard_map.305 = (bf16[96,640]{1,0:T(8,128)(2,1)}, bf16[96,1152]{1,0:T(8,128)(2,1)}, bf16[96,1152]{1,0:T(8,128)(2,1)}) custom-call(s32[2]{0:T(128)} %pad_add_fusion.place_ref.refs_0_, f32[96,2304]{1,0:T(8,128)} %refs_4_.5, f32[96,768]{1,0:T(8,128)} %refs_7_.1, f32[96,3072]{1,0:T(8,128)} %refs_4_.3, f32[384,768]{1,0:T(8,128)} %refs_4_.4, f32[12,96]{1,0:T(8,128)} %refs_10_.1), custom_call_target="tpu_custom_call" | custom-call | flops 73728 | bytes 4108808 | tf_op jit(solution)/shard_map/pallas_call | solution.py:247
  12.5 1.3 collective-permute-start.1
  13.8 1.3 collective-permute-start.6
  15.1 2.2 collective-permute-start.4
  17.5 2.8 %collective-permute-done.6.refs_9_ = bf16[96,640]{1,0:T(8,128)(2,1)S(1)} collective-permute-done((bf16[96,640]{1,0:T(8,128)(2,1)}, bf16[96,640]{1,0:T(8,128)(2,1)S(1)}, u32[]{:S(2)}, u32[]{:S(2)}) %collective-permute-start.6) | collective-permute-done | bytes 122912 | tf_op jit(solution)/shard_map/ppermute | solution.py:38
  20.3 5.7 %collective-permute-start = (bf16[272,768]{1,0:T(8,128)(2,1)S(1)}, bf16[272,768]{1,0:T(8,128)(2,1)S(1)}, u32[]{:S(2)}, u32[]{:S(2)}) collective-permute-start(bf16[272,768]{1,0:T(8,128)(2,1)S(1)} %fusion.1.refs_1_), channel_id=1, source_target_pairs={{0,8},{8,0},{16,24},{24,16},{1,9},{9,1},{17,25},{25,17},{2,10},{10... | collective-permute-start | bytes 1253384 | tf_op jit(solution)/shard_map/ppermute | solution.py:28
  26.5 1.2 collective-permute-start.14
  27.7 8.9 %collective-permute-done.14.refs_10_ = bf16[96,1152]{1,0:T(8,128)(2,1)S(1)} collective-permute-done((bf16[96,1152]{1,0:T(8,128)(2,1)S(1)}, bf16[96,1152]{1,0:T(8,128)(2,1)S(1)}, u32[]{:S(2)}, u32[]{:S(2)}) %collective-permute-start.14) | collective-permute-done | bytes 221216 | tf_op jit(solution)/shard_map/ppermute | solution.py:38
  36.6 3.5 %collective-permute-start.15 = (bf16[96,1152]{1,0:T(8,128)(2,1)S(1)}, bf16[96,1152]{1,0:T(8,128)(2,1)S(1)}, u32[]{:S(2)}, u32[]{:S(2)}) collective-permute-start(bf16[96,1152]{1,0:T(8,128)(2,1)S(1)} %copy-done.40), channel_id=1, source_target_pairs={{0,2},{1,3},{2,0},{3,1},{4,6},{5,7},{6,4},{7,5},{8,10},{9,11},{10,... | collective-permute-start | bytes 663560 | tf_op jit(solution)/shard_map/ppermute | solution.py:38
  42.8 10.3 %shard_map.306 = (bf16[1024,768]{1,0:T(8,128)(2,1)}, bf16[768,576]{1,0:T(8,128)(2,1)}, f32[16,768]{1,0:T(8,128)}, bf16[1024,192]{1,0:T(8,128)(2,1)}, bf16[1024,1...) custom-call(s32[2]{0:T(128)} %pad_add_fusion.place_ref.refs_0_, ...), custom_call_target="tpu_custom_call" | custom-call | flops 12079595520 | bytes 7323656 | tf_op jit(solution)/shard_map/pallas_call | solution.py:247
  54.1 17.6 %collective-permute-done.17.refs_13_ = bf16[96,1152]{1,0:T(8,128)(2,1)S(1)} collective-permute-done((bf16[96,1152]{1,0:T(8,128)(2,1)S(1)}, bf16[96,1152]{1,0:T(8,128)(2,1)S(1)}, u32[]{:S(2)}, u32[]{:S(2)}) %collective-permute-start.17) | collective-permute-done | bytes 221216 | tf_op jit(solution)/shard_map/ppermute | solution.py:38
  71.8 1.3 collective-permute-start.18
  73.1 3.6 %collective-permute-start.11 = (bf16[256,768]{1,0:T(8,128)(2,1)S(1)}, bf16[256,768]{1,0:T(8,128)(2,1)}, u32[]{:S(2)}, u32[]{:S(2)}) collective-permute-start(bf16[256,768]{1,0:T(8,128)(2,1)S(1)} %copy-done.18), channel_id=1, source_target_pairs={{0,8},{8,0},{16,24},{24,16},{1,9},{9,1},{17,25},{25,17},{2,10},{10... | collective-permute-start | bytes 1179656 | tf_op jit(solution)/shard_map/ppermute | solution.py:28
  78.8 5.1 %collective-permute-done.18.refs_14_ = bf16[288,1152]{1,0:T(8,128)(2,1)S(1)} collective-permute-done((bf16[288,1152]{1,0:T(8,128)(2,1)S(1)}, bf16[288,1152]{1,0:T(8,128)(2,1)S(1)}, u32[]{:S(2)}, u32[]{:S(2)}) %collective-permute-start.18) | collective-permute-done | bytes 663584 | tf_op jit(solution)/shard_map/ppermute | solution.py:38
  84.8 17.2 %shard_map.307 = (bf16[768,768]{1,0:T(8,128)(2,1)}, bf16[1024,768]{1,0:T(8,128)(2,1)}, bf16[1024,768]{1,0:T(8,128)(2,1)}, bf16[1024,768]{1,0:T(8,128)(2,1)}, bf1...) custom-call(s32[2]{0:T(128)} %pad_add_fusion.place_ref.refs_0_, ...), custom_call_target="tpu_custom_call" | custom-call | flops 19327352832 | bytes 18926600 | tf_op jit(solution)/shard_map/pallas_call | solution.py:247
  101.9 5.3 %collective-permute-start.19 = (bf16[512,768]{1,0:T(8,128)(2,1)}, bf16[512,768]{1,0:T(8,128)(2,1)S(1)}, u32[]{:S(2)}, u32[]{:S(2)}) collective-permute-start(bf16[512,768]{1,0:T(8,128)(2,1)} %get-tuple-element.110), channel_id=1, source_target_pairs={{0,8},{8,0},{16,24},{24,16},{1,9},{9,1},{17,25},{25,17},{2,10},{10... | collective-permute-start | bytes 2359304 | tf_op jit(solution)/shard_map/ppermute | solution.py:28
  107.3 2.1 collective-permute-done.19.near_ref
  109.4 1.5 add_convert_fusion.3
  110.9 10.5 %shard_map.308 = (bf16[384,1536]{1,0:T(8,128)(2,1)}, bf16[384,1536]{1,0:T(8,128)(2,1)}, bf16[512,768]{1,0:T(8,128)(2,1)}, f32[256,768]{1,0:T(8,128)}, f32[256,768]{1,0:T(8,128)}, /*index=5*/f32[8,768]{1,0:T(8,128)}) custom-call(s32[2]{0:T(128)} %pad_add_fusion.place_ref.refs_0_, bf16[1024,768]{1,0:T(8,128)(2,1)} %get-tuple-element.113.act_ref, ...), custom_call_target="tpu_custom_call" | custom-call | flops 10871635968 | bytes 12804104 | tf_op jit(solution)/shard_map/pallas_call | solution.py:247
  121.5 1.3 collective-permute-start.22
  122.8 3.6 %shard_map.309 = (f32[256,768]{1,0:T(8,128)}, bf16[256,768]{1,0:T(8,128)(2,1)}, f32[8,768]{1,0:T(8,128)}) custom-call(s32[2]{0:T(128)} %pad_add_fusion.place_ref.refs_0_, f32[256,768]{1,0:T(8,128)} %get-tuple-element.109.own_ref, bf16[512,768]{1,0:T(8,128)(2,1)} %copy-done.9, bf16[256,768]{1,0:T(8,128)(2,1)} %copy-done.19, ...), custom_call_target="tpu_custom_call" | custom-call | flops 1966080 | bytes 4399112 | tf_op jit(solution)/shard_map/pallas_call | solution.py:247
  126.4 1.5 collective-permute-start.21
  127.8 1.2 collective-permute-start.23
  129.1 6.9 %collective-permute-done.21.branch_c = bf16[256,768]{1,0:T(8,128)(2,1)S(1)} collective-permute-done((bf16[256,768]{1,0:T(8,128)(2,1)}, bf16[256,768]{1,0:T(8,128)(2,1)S(1)}, u32[]{:S(2)}, u32[]{:S(2)}) %collective-permute-start.21) | collective-permute-done | bytes 393248 | tf_op jit(solution)/shard_map/ppermute | solution.py:28
  136.0 2.1 collective-permute-start.24
  139.9 8.3 %collective-permute-done.22.received_ref = bf16[384,1536]{1,0:T(8,128)(2,1)S(1)} collective-permute-done((bf16[384,1536]{1,0:T(8,128)(2,1)}, bf16[384,1536]{1,0:T(8,128)(2,1)S(1)}, u32[]{:S(2)}, u32[]{:S(2)}) %collective-permute-start.22) | collective-permute-done | bytes 1179680 | tf_op jit(solution)/shard_map/ppermute | solution.py:38
  149.3 2.9 %shard_map.310 = (f32[96,1536]{1,0:T(8,128)}, bf16[96,1536]{1,0:T(8,128)(2,1)}, bf16[96,1536]{1,0:T(8,128)(2,1)}, bf16[96,1536]{1,0:T(8,128)(2,1)}) custom-call(s32[2]{0:T(128)} %pad_add_fusion.place_ref.refs_0_, bf16[384,1536]{1,0:T(8,128)(2,1)} %get-tuple-element.122.kept_ref, bf16[384,1536]{1,0:T(8,128)(2,1)} %copy-done.11), custom_call_target="tpu_custom_call" | custom-call | flops 589824 | bytes 3833864 | tf_op jit(solution)/shard_map/pallas_call | solution.py:247
  152.2 3.2 %collective-permute-start.26 = (bf16[96,1536]{1,0:T(8,128)(2,1)}, bf16[96,1536]{1,0:T(8,128)(2,1)S(1)}, u32[]{:S(2)}, u32[]{:S(2)}) collective-permute-start(bf16[96,1536]{1,0:T(8,128)(2,1)} %get-tuple-element.140), channel_id=1, source_target_pairs={{0,4},{1,5},{2,6},{3,7},{4,0},{5,1},{6,2},{7,3},{8,12},{9,13},{10,... | collective-permute-start | bytes 884744 | tf_op jit(solution)/shard_map/ppermute | solution.py:38
  156.2 18.8 %shard_map.311 = (bf16[384,832]{1,0:T(8,128)(2,1)}, bf16[384,832]{1,0:T(8,128)(2,1)}, bf16[512,768]{1,0:T(8,128)(2,1)}, f32[256,768]{1,0:T(8,128)}, f32[256,768]{1,0:T(8,128)}) custom-call(s32[2]{0:T(128)} %pad_add_fusion.place_ref.refs_0_, bf16[256,768]{1,0:T(8,128)(2,1)} %get-tuple-element.126.branch_a, bf16[256,768]{1,0:T(8,128)(2,1)} %copy-done.37, ...), custom_call_target="tpu_custom_call" | custom-call | flops 21743271936 | bytes 12288008 | tf_op jit(solution)/shard_map/pallas_call | solution.py:247
  175.0 2.4 %collective-permute-start.32 = (bf16[512,768]{1,0:T(8,128)(2,1)}, bf16[512,768]{1,0:T(8,128)(2,1)S(1)}, u32[]{:S(2)}, u32[]{:S(2)}) collective-permute-start(bf16[512,768]{1,0:T(8,128)(2,1)} %get-tuple-element.147), channel_id=1, source_target_pairs={{0,8},{8,0},{16,24},{24,16},{1,9},{9,1},{17,25},{25,17},{2,10},{10... | collective-permute-start | bytes 2359304 | tf_op jit(solution)/shard_map/ppermute | solution.py:28
  177.5 1.7 collective-permute-done.27
  179.4 1.9 collective-permute-start.37
  181.3 2.2 copy.39
  183.5 1.4 collective-permute-start.28
  184.9 1.8 add_convert_fusion.1
  186.9 3.1 %collective-permute-start.36 = (bf16[96,1536]{1,0:T(8,128)(2,1)S(1)}, bf16[96,1536]{1,0:T(8,128)(2,1)S(1)}, u32[]{:S(2)}, u32[]{:S(2)}) collective-permute-start(bf16[96,1536]{1,0:T(8,128)(2,1)S(1)} %add_convert_fusion.4.refs_0_), channel_id=1, source_target_pairs={{0,8},{8,0},{16,24},{24,16},{1,9},{9,1},{17,25},{25,17},{2,10},{10... | collective-permute-start | bytes 884744 | tf_op jit(solution)/shard_map/ppermute | solution.py:28
  191.0 1.6 collective-permute-start.33
  193.4 3.3 %collective-permute-done.28 = bf16[384,832]{0,1:T(8,128)(2,1)} collective-permute-done((bf16[384,832]{0,1:T(8,128)(2,1)}, bf16[384,832]{0,1:T(8,128)(2,1)}, u32[]{:S(2)}, u32[]{:S(2)}) %collective-permute-start.28) | collective-permute-done | bytes 639008 | tf_op jit(solution)/shard_map/ppermute | solution.py:38
  196.7 2.3 copy.40.received_ref
  199.0 2.3 shard_map.312
  202.1 2.5 %collective-permute-start.30 = (bf16[96,832]{1,0:T(8,128)(2,1)}, bf16[96,832]{1,0:T(8,128)(2,1)S(1)}, u32[]{:S(2)}, u32[]{:S(2)}) collective-permute-start(bf16[96,832]{1,0:T(8,128)(2,1)} %get-tuple-element.144), channel_id=1, source_target_pairs={{0,4},{1,5},{2,6},{3,7},{4,0},{5,1},{6,2},{7,3},{8,12},{9,13},{10,... | collective-permute-start | bytes 479240 | tf_op jit(solution)/shard_map/ppermute | solution.py:38
  204.7 2.4 %add_convert_fusion = bf16[256,768]{1,0:T(8,128)(2,1)} fusion(f32[256,768]{1,0:T(8,128)S(1)} %copy-done.7, bf16[256,768]{1,0:T(8,128)(2,1)} %collective-permute-done.35, f32[256,768]{1,0:T(8,128)} %get-tuple-element.150, bf16[512,768]{1,0:T(8,128)(2,1)} %collective-permute-done.34, f32[768]{0:T(1024)S(1)} %slice_reduce_fusion), kind=kLoop, calls=%fused_computation.2 | loop fusion | flops 1376256 | bytes 2755584 | tf_op jit(solution)/shard_map/convert_element_type | solution.py:938
  207.1 3.3 %shard_map.315 = (f32[384,768]{1,0:T(8,128)}, f32[384,768]{1,0:T(8,128)}, f32[384,768]{1,0:T(8,128)}) custom-call(s32[2]{0:T(128)S(1)} %copy-done.6, bf16[96,1536]{1,0:T(8,128)(2,1)S(1)} %add_convert_fusion.4.refs_0_, bf16[96,1536]{1,0:T(8,128)(2,1)S(1)} %collective-permute-done.36.refs_1_, bf16[96,1536]{1,0:T(8,128)(2,1)S(1)} %collective-permute-done.37.refs_2_, ...), custom_call_target="tpu_custom_call" | custom-call | flops 5898240 | bytes 7667712 | tf_op jit(solution)/shard_map/pallas_call | solution.py:666
  210.4 3.4 %shard_map.314 = (f32[96,3072]{1,0:T(8,128)}, f32[96,3072]{1,0:T(8,128)}, f32[96,3072]{1,0:T(8,128)}) custom-call(s32[2]{0:T(128)S(1)} %copy-done.6, bf16[96,1536]{1,0:T(8,128)(2,1)S(1)} %add_convert_fusion.4.refs_0_, bf16[96,1536]{1,0:T(8,128)(2,1)S(1)} %collective-permute-done.36.refs_1_, bf16[96,1536]{1,0:T(8,128)(2,1)S(1)} %collective-permute-done.37.refs_2_, ...), custom_call_target="tpu_custom_call" | custom-call | flops 5898240 | bytes 7667712 | tf_op jit(solution)/shard_map/pallas_call | solution.py:666
  214.6 3.4 %shard_map.313 = f32[256,768]{1,0:T(8,128)} custom-call(s32[2]{0:T(128)} %pad_add_fusion.place_ref.refs_0_, f32[256,768]{1,0:T(8,128)} %get-tuple-element.146.own_ref, bf16[512,768]{1,0:T(8,128)(2,1)} %copy-done.8, bf16[256,768]{1,0:T(8,128)(2,1)} %copy-done.17, bf16[256,768]{1,0:T(8,128)(2,1)} %tokens_ref.1, f32[256,768]{1,0:T(8,128)} %get-tuple-element.149.resid_grad_ref, ...), custom_call_target="tpu_custom_call" | custom-call | flops 1966080 | bytes 3981320 | tf_op jit(solution)/shard_map/pallas_call | solution.py:247
  219.4 3.5 %collective-permute-start.39 = (bf16[96,832]{1,0:T(8,128)(2,1)S(1)}, bf16[96,832]{1,0:T(8,128)(2,1)S(1)}, u32[]{:S(2)}, u32[]{:S(2)}) collective-permute-start(bf16[96,832]{1,0:T(8,128)(2,1)S(1)} %add_convert_fusion.5.refs_0_), channel_id=1, source_target_pairs={{0,8},{8,0},{16,24},{24,16},{1,9},{9,1},{17,25},{25,17},{2,10},{10... | collective-permute-start | bytes 479240 | tf_op jit(solution)/shard_map/ppermute | solution.py:28
  223.2 4.7 %collective-permute-start.41 = (bf16[96,832]{1,0:T(8,128)(2,1)S(1)}, bf16[96,832]{1,0:T(8,128)(2,1)S(1)}, u32[]{:S(2)}, u32[]{:S(2)}) collective-permute-start(bf16[96,832]{1,0:T(8,128)(2,1)S(1)} %collective-permute-done.40.refs_2_), channel_id=1, source_target_pairs={{0,8},{8,0},{16,24},{24,16},{1,9},{9,1},{17,25},{25,17},{2,10},{10... | collective-permute-start | bytes 479240 | tf_op jit(solution)/shard_map/ppermute | solution.py:28
  229.6 5.2 %shard_map.316 = (f32[96,2304]{1,0:T(8,128)}, f32[96,2304]{1,0:T(8,128)}, f32[96,2304]{1,0:T(8,128)}, f32[96,768]{1,0:T(8,128)}, f32[96,768]{1,0:T(8,128)}, /*in...) custom-call(s32[2]{0:T(128)} %pad_add_fusion.place_ref.refs_0_, ...), custom_call_target="tpu_custom_call" | custom-call | flops 4423680 | bytes 7744520 | tf_op jit(solution)/shard_map/pallas_call | solution.py:247
  (164 shorter events, 19.0 us)
Async XLA Ops:
  7.2 76.8 %all-gather.2.cloned.1.call-start = ((), (), s32[]{:S(2)}) async-start(), calls=%async_computation | async-start | bytes 1990656 | tf_op jit(solution)/shard_map/all_gather | solution.py:759
  12.3 28.9 %copy-start.18 = (bf16[256,768]{1,0:T(8,128)(2,1)S(1)}, bf16[256,768]{1,0:T(8,128)(2,1)}, u32[]{:S(2)}) copy-start(bf16[256,768]{1,0:T(8,128)(2,1)} %cotangent_ref.1) | copy-start | bytes 1179652
  12.4 28.9 %copy-start.16 = (bf16[272,768]{1,0:T(8,128)(2,1)}, bf16[272,768]{1,0:T(8,128)(2,1)S(1)}, u32[]{:S(2)}) copy-start(bf16[272,768]{1,0:T(8,128)(2,1)S(1)} %fusion.1.refs_1_) | copy-start | bytes 1253380
  12.5 13.5 %collective-permute-start.1 = (bf16[272,768]{1,0:T(8,128)(2,1)S(1)}, bf16[272,768]{1,0:T(8,128)(2,1)S(1)}, u32[]{:S(2)}, u32[]{:S(2)}) collective-permute-start(bf16[272,768]{1,0:T(8,128)(2,1)S(1)} %fusion.1.refs_1_), channel_id=1, source_target_pairs={{0,16},{8,24},{16,0},{24,8},{1,17},{9,25},{17,1},{25,9},{2,18},{10... | collective-permute-start | bytes 1253384 | tf_op jit(solution)/shard_map/ppermute | solution.py:28
  13.8 6.6 %collective-permute-start.6 = (bf16[96,640]{1,0:T(8,128)(2,1)}, bf16[96,640]{1,0:T(8,128)(2,1)S(1)}, u32[]{:S(2)}, u32[]{:S(2)}) collective-permute-start(bf16[96,640]{1,0:T(8,128)(2,1)} %get-tuple-element.99.refs_5_), channel_id=1, source_target_pairs={{0,6},{1,7},{2,4},{3,5},{4,2},{5,3},{6,0},{7,1},{8,14},{9,15},{10,... | collective-permute-start | bytes 368648 | tf_op jit(solution)/shard_map/ppermute | solution.py:38
  15.1 11.0 %collective-permute-start.4 = (bf16[96,640]{1,0:T(8,128)(2,1)}, bf16[96,640]{1,0:T(8,128)(2,1)S(1)}, u32[]{:S(2)}, u32[]{:S(2)}) collective-permute-start(bf16[96,640]{1,0:T(8,128)(2,1)} %get-tuple-element.99.refs_5_), channel_id=1, source_target_pairs={{0,2},{1,3},{2,0},{3,1},{4,6},{5,7},{6,4},{7,5},{8,10},{9,11},{10,... | collective-permute-start | bytes 368648 | tf_op jit(solution)/shard_map/ppermute | solution.py:38
  17.3 8.8 %collective-permute-start.5 = (bf16[96,640]{1,0:T(8,128)(2,1)}, bf16[96,640]{1,0:T(8,128)(2,1)S(1)}, u32[]{:S(2)}, u32[]{:S(2)}) collective-permute-start(bf16[96,640]{1,0:T(8,128)(2,1)} %get-tuple-element.99.refs_5_), channel_id=1, source_target_pairs={{0,4},{1,5},{2,6},{3,7},{4,0},{5,1},{6,2},{7,3},{8,12},{9,13},{10,... | collective-permute-start | bytes 368648 | tf_op jit(solution)/shard_map/ppermute | solution.py:38
  17.3 8.9 %collective-permute-start.3 = (bf16[96,640]{1,0:T(8,128)(2,1)}, bf16[96,640]{1,0:T(8,128)(2,1)S(1)}, u32[]{:S(2)}, u32[]{:S(2)}) collective-permute-start(bf16[96,640]{1,0:T(8,128)(2,1)} %get-tuple-element.99.refs_5_), channel_id=1, source_target_pairs={{0,1},{1,0},{2,3},{3,2},{4,5},{5,4},{6,7},{7,6},{8,9},{9,8},{10,11... | collective-permute-start | bytes 368648 | tf_op jit(solution)/shard_map/ppermute | solution.py:38
  20.3 20.2 %collective-permute-start = (bf16[272,768]{1,0:T(8,128)(2,1)S(1)}, bf16[272,768]{1,0:T(8,128)(2,1)S(1)}, u32[]{:S(2)}, u32[]{:S(2)}) collective-permute-start(bf16[272,768]{1,0:T(8,128)(2,1)S(1)} %fusion.1.refs_1_), channel_id=1, source_target_pairs={{0,8},{8,0},{16,24},{24,16},{1,9},{9,1},{17,25},{25,17},{2,10},{10... | collective-permute-start | bytes 1253384 | tf_op jit(solution)/shard_map/ppermute | solution.py:28
  26.0 15.4 %collective-permute-start.2 = (bf16[272,768]{1,0:T(8,128)(2,1)S(1)}, bf16[272,768]{1,0:T(8,128)(2,1)S(1)}, u32[]{:S(2)}, u32[]{:S(2)}) collective-permute-start(bf16[272,768]{1,0:T(8,128)(2,1)S(1)} %collective-permute-done.1.refs_3_), channel_id=1, source_target_pairs={{0,8},{8,0},{16,24},{24,16},{1,9},{9,1},{17,25},{25,17},{2,10},{10... | collective-permute-start | bytes 1253384 | tf_op jit(solution)/shard_map/ppermute | solution.py:28
  26.2 15.1 %collective-permute-start.7 = (bf16[288,640]{1,0:T(8,128)(2,1)S(1)}, bf16[288,640]{1,0:T(8,128)(2,1)S(1)}, u32[]{:S(2)}, u32[]{:S(2)}) collective-permute-start(bf16[288,640]{1,0:T(8,128)(2,1)S(1)} %pad_maximum_fusion.1), channel_id=1, source_target_pairs={{0,1},{1,0},{2,3},{3,2},{4,5},{5,4},{6,7},{7,6},{8,9},{9,8},{10,11... | collective-permute-start | bytes 1105928 | tf_op jit(solution)/shard_map/ppermute | solution.py:38
  26.5 10.1 %collective-permute-start.14 = (bf16[96,1152]{1,0:T(8,128)(2,1)S(1)}, bf16[96,1152]{1,0:T(8,128)(2,1)S(1)}, u32[]{:S(2)}, u32[]{:S(2)}) collective-permute-start(bf16[96,1152]{1,0:T(8,128)(2,1)S(1)} %copy-done.40), channel_id=1, source_target_pairs={{0,1},{1,0},{2,3},{3,2},{4,5},{5,4},{6,7},{7,6},{8,9},{9,8},{10,11... | collective-permute-start | bytes 663560 | tf_op jit(solution)/shard_map/ppermute | solution.py:38
  36.6 17.5 %collective-permute-start.15 = (bf16[96,1152]{1,0:T(8,128)(2,1)S(1)}, bf16[96,1152]{1,0:T(8,128)(2,1)S(1)}, u32[]{:S(2)}, u32[]{:S(2)}) collective-permute-start(bf16[96,1152]{1,0:T(8,128)(2,1)S(1)} %copy-done.40), channel_id=1, source_target_pairs={{0,2},{1,3},{2,0},{3,1},{4,6},{5,7},{6,4},{7,5},{8,10},{9,11},{10,... | collective-permute-start | bytes 663560 | tf_op jit(solution)/shard_map/ppermute | solution.py:38
  40.0 14.0 %collective-permute-start.16 = (bf16[96,1152]{1,0:T(8,128)(2,1)S(1)}, bf16[96,1152]{1,0:T(8,128)(2,1)S(1)}, u32[]{:S(2)}, u32[]{:S(2)}) collective-permute-start(bf16[96,1152]{1,0:T(8,128)(2,1)S(1)} %copy-done.40), channel_id=1, source_target_pairs={{0,4},{1,5},{2,6},{3,7},{4,0},{5,1},{6,2},{7,3},{8,12},{9,13},{10,... | collective-permute-start | bytes 663560 | tf_op jit(solution)/shard_map/ppermute | solution.py:38
  40.5 31.2 %collective-permute-start.17 = (bf16[96,1152]{1,0:T(8,128)(2,1)S(1)}, bf16[96,1152]{1,0:T(8,128)(2,1)S(1)}, u32[]{:S(2)}, u32[]{:S(2)}) collective-permute-start(bf16[96,1152]{1,0:T(8,128)(2,1)S(1)} %copy-done.40), channel_id=1, source_target_pairs={{0,6},{1,7},{2,4},{3,5},{4,2},{5,3},{6,0},{7,1},{8,14},{9,15},{10,... | collective-permute-start | bytes 663560 | tf_op jit(solution)/shard_map/ppermute | solution.py:38
  41.3 35.4 %collective-permute-start.12 = (bf16[256,768]{1,0:T(8,128)(2,1)S(1)}, bf16[256,768]{1,0:T(8,128)(2,1)S(1)}, u32[]{:S(2)}, u32[]{:S(2)}) collective-permute-start(bf16[256,768]{1,0:T(8,128)(2,1)S(1)} %copy-done.18), channel_id=1, source_target_pairs={{0,16},{8,24},{16,0},{24,8},{1,17},{9,25},{17,1},{25,9},{2,18},{10... | collective-permute-start | bytes 1179656 | tf_op jit(solution)/shard_map/ppermute | solution.py:28
  53.1 23.7 %copy-start.31 = (bf16[1024,192]{1,0:T(8,128)(2,1)S(1)}, bf16[1024,192]{1,0:T(8,128)(2,1)}, u32[]{:S(2)}) copy-start(bf16[1024,192]{1,0:T(8,128)(2,1)} %get-tuple-element.101.refs_1_.attended_a) | copy-start | bytes 1179652
  53.1 24.2 %collective-permute-start.9 = (bf16[1024,192]{1,0:T(8,128)(2,1)}, bf16[1024,192]{1,0:T(8,128)(2,1)}, u32[]{:S(2)}, u32[]{:S(2)}) collective-permute-start(bf16[1024,192]{1,0:T(8,128)(2,1)} %get-tuple-element.101.refs_1_.attended_a), channel_id=1, source_target_pairs={{0,16},{8,24},{16,0},{24,8},{1,17},{9,25},{17,1},{25,9},{2,18},{10... | collective-permute-start | bytes 1179656 | tf_op jit(solution)/shard_map/ppermute | solution.py:28
  54.1 29.9 %copy-start.21 = (bf16[96,1152]{1,0:T(8,128)(2,1)}, bf16[96,1152]{1,0:T(8,128)(2,1)S(1)}, u32[]{:S(2)}) copy-start(bf16[96,1152]{1,0:T(8,128)(2,1)S(1)} %collective-permute-done.15.refs_11_) | copy-start | bytes 663556
  54.1 29.9 %copy-start.22 = (bf16[96,1152]{1,0:T(8,128)(2,1)}, bf16[96,1152]{1,0:T(8,128)(2,1)S(1)}, u32[]{:S(2)}) copy-start(bf16[96,1152]{1,0:T(8,128)(2,1)S(1)} %collective-permute-done.16.refs_12_) | copy-start | bytes 663556
  71.8 12.1 %collective-permute-start.18 = (bf16[288,1152]{1,0:T(8,128)(2,1)S(1)}, bf16[288,1152]{1,0:T(8,128)(2,1)S(1)}, u32[]{:S(2)}, u32[]{:S(2)}) collective-permute-start(bf16[288,1152]{1,0:T(8,128)(2,1)S(1)} %pad_maximum_fusion), channel_id=1, source_target_pairs={{0,1},{1,0},{2,3},{3,2},{4,5},{5,4},{6,7},{7,6},{8,9},{9,8},{10,11... | collective-permute-start | bytes 1990664 | tf_op jit(solution)/shard_map/ppermute | solution.py:38
  73.1 5.7 %collective-permute-start.11 = (bf16[256,768]{1,0:T(8,128)(2,1)S(1)}, bf16[256,768]{1,0:T(8,128)(2,1)}, u32[]{:S(2)}, u32[]{:S(2)}) collective-permute-start(bf16[256,768]{1,0:T(8,128)(2,1)S(1)} %copy-done.18), channel_id=1, source_target_pairs={{0,8},{8,0},{16,24},{24,16},{1,9},{9,1},{17,25},{25,17},{2,10},{10... | collective-permute-start | bytes 1179656 | tf_op jit(solution)/shard_map/ppermute | solution.py:28
  76.7 7.2 %collective-permute-start.13 = (bf16[256,768]{1,0:T(8,128)(2,1)S(1)}, bf16[256,768]{1,0:T(8,128)(2,1)}, u32[]{:S(2)}, u32[]{:S(2)}) collective-permute-start(bf16[256,768]{1,0:T(8,128)(2,1)S(1)} %collective-permute-done.12.refs_7_), channel_id=1, source_target_pairs={{0,8},{8,0},{16,24},{24,16},{1,9},{9,1},{17,25},{25,17},{2,10},{10... | collective-permute-start | bytes 1179656 | tf_op jit(solution)/shard_map/ppermute | solution.py:28
  76.8 7.1 %collective-permute-start.8 = (bf16[1024,192]{1,0:T(8,128)(2,1)S(1)}, bf16[1024,192]{1,0:T(8,128)(2,1)}, u32[]{:S(2)}, u32[]{:S(2)}) collective-permute-start(bf16[1024,192]{1,0:T(8,128)(2,1)S(1)} %copy-done.31), channel_id=1, source_target_pairs={{0,8},{8,0},{16,24},{24,16},{1,9},{9,1},{17,25},{25,17},{2,10},{10... | collective-permute-start | bytes 1179656 | tf_op jit(solution)/shard_map/ppermute | solution.py:28
  77.2 6.7 %collective-permute-start.10 = (bf16[1024,192]{1,0:T(8,128)(2,1)}, bf16[1024,192]{1,0:T(8,128)(2,1)}, u32[]{:S(2)}, u32[]{:S(2)}) collective-permute-start(bf16[1024,192]{1,0:T(8,128)(2,1)} %collective-permute-done.9.refs_3_.attended_c), channel_id=1, source_target_pairs={{0,8},{8,0},{16,24},{24,16},{1,9},{9,1},{17,25},{25,17},{2,10},{10... | collective-permute-start | bytes 1179656 | tf_op jit(solution)/shard_map/ppermute | solution.py:28
  101.9 7.4 %collective-permute-start.19 = (bf16[512,768]{1,0:T(8,128)(2,1)}, bf16[512,768]{1,0:T(8,128)(2,1)S(1)}, u32[]{:S(2)}, u32[]{:S(2)}) collective-permute-start(bf16[512,768]{1,0:T(8,128)(2,1)} %get-tuple-element.110), channel_id=1, source_target_pairs={{0,8},{8,0},{16,24},{24,16},{1,9},{9,1},{17,25},{25,17},{2,10},{10... | collective-permute-start | bytes 2359304 | tf_op jit(solution)/shard_map/ppermute | solution.py:28
  110.9 10.6 %collective-permute-start.20 = (bf16[256,768]{1,0:T(8,128)(2,1)S(1)}, bf16[256,768]{1,0:T(8,128)(2,1)S(1)}, u32[]{:S(2)}, u32[]{:S(2)}) collective-permute-start(bf16[256,768]{1,0:T(8,128)(2,1)S(1)} %add_convert_fusion.3), channel_id=1, source_target_pairs={{0,16},{8,24},{16,0},{24,8},{1,17},{9,25},{17,1},{25,9},{2,18},{10... | collective-permute-start | bytes 1179656 | tf_op jit(solution)/shard_map/ppermute | solution.py:28
  121.5 26.8 %collective-permute-start.22 = (bf16[384,1536]{1,0:T(8,128)(2,1)}, bf16[384,1536]{1,0:T(8,128)(2,1)S(1)}, u32[]{:S(2)}, u32[]{:S(2)}) collective-permute-start(bf16[384,1536]{1,0:T(8,128)(2,1)} %get-tuple-element.124), channel_id=1, source_target_pairs={{0,1},{1,0},{2,3},{3,2},{4,5},{5,4},{6,7},{7,6},{8,9},{9,8},{10,11... | collective-permute-start | bytes 3538952 | tf_op jit(solution)/shard_map/ppermute | solution.py:38
  126.4 9.6 %collective-permute-start.21 = (bf16[256,768]{1,0:T(8,128)(2,1)}, bf16[256,768]{1,0:T(8,128)(2,1)S(1)}, u32[]{:S(2)}, u32[]{:S(2)}) collective-permute-start(bf16[256,768]{1,0:T(8,128)(2,1)} %get-tuple-element.126.branch_a), channel_id=1, source_target_pairs={{0,16},{8,24},{16,0},{24,8},{1,17},{9,25},{17,1},{25,9},{2,18},{10... | collective-permute-start | bytes 1179656 | tf_op jit(solution)/shard_map/ppermute | solution.py:28
  127.8 27.5 %collective-permute-start.23 = (bf16[256,768]{1,0:T(8,128)(2,1)}, bf16[256,768]{1,0:T(8,128)(2,1)S(1)}, u32[]{:S(2)}, u32[]{:S(2)}) collective-permute-start(bf16[256,768]{1,0:T(8,128)(2,1)} %get-tuple-element.126.branch_a), channel_id=1, source_target_pairs={{0,8},{8,0},{16,24},{24,16},{1,9},{9,1},{17,25},{25,17},{2,10},{10... | collective-permute-start | bytes 1179656 | tf_op jit(solution)/shard_map/ppermute | solution.py:28
  136.0 19.4 %collective-permute-start.24 = (bf16[256,768]{1,0:T(8,128)(2,1)S(1)}, bf16[256,768]{1,0:T(8,128)(2,1)S(1)}, u32[]{:S(2)}, u32[]{:S(2)}) collective-permute-start(bf16[256,768]{1,0:T(8,128)(2,1)S(1)} %collective-permute-done.21.branch_c), channel_id=1, source_target_pairs={{0,8},{8,0},{16,24},{24,16},{1,9},{9,1},{17,25},{25,17},{2,10},{10... | collective-permute-start | bytes 1179656 | tf_op jit(solution)/shard_map/ppermute | solution.py:28
  139.9 45.0 %collective-permute-start.34 = (bf16[512,768]{1,0:T(8,128)(2,1)}, bf16[512,768]{1,0:T(8,128)(2,1)}, u32[]{:S(2)}, u32[]{:S(2)}) collective-permute-start(bf16[512,768]{1,0:T(8,128)(2,1)} %get-tuple-element.152), channel_id=1, source_target_pairs={{0,8},{8,0},{16,24},{24,16},{1,9},{9,1},{17,25},{25,17},{2,10},{10... | collective-permute-start | bytes 2359304 | tf_op jit(solution)/shard_map/ppermute | solution.py:28
  152.2 25.3 %collective-permute-start.25 = (bf16[96,1536]{1,0:T(8,128)(2,1)}, bf16[96,1536]{1,0:T(8,128)(2,1)S(1)}, u32[]{:S(2)}, u32[]{:S(2)}) collective-permute-start(bf16[96,1536]{1,0:T(8,128)(2,1)} %get-tuple-element.139), channel_id=1, source_target_pairs={{0,2},{1,3},{2,0},{3,1},{4,6},{5,7},{6,4},{7,5},{8,10},{9,11},{10,... | collective-permute-start | bytes 884744 | tf_op jit(solution)/shard_map/ppermute | solution.py:38
  152.2 25.3 %collective-permute-start.26 = (bf16[96,1536]{1,0:T(8,128)(2,1)}, bf16[96,1536]{1,0:T(8,128)(2,1)S(1)}, u32[]{:S(2)}, u32[]{:S(2)}) collective-permute-start(bf16[96,1536]{1,0:T(8,128)(2,1)} %get-tuple-element.140), channel_id=1, source_target_pairs={{0,4},{1,5},{2,6},{3,7},{4,0},{5,1},{6,2},{7,3},{8,12},{9,13},{10,... | collective-permute-start | bytes 884744 | tf_op jit(solution)/shard_map/ppermute | solution.py:38
  155.4 23.9 %collective-permute-start.27 = (bf16[96,1536]{1,0:T(8,128)(2,1)}, bf16[96,1536]{1,0:T(8,128)(2,1)S(1)}, u32[]{:S(2)}, u32[]{:S(2)}) collective-permute-start(bf16[96,1536]{1,0:T(8,128)(2,1)} %get-tuple-element.141), channel_id=1, source_target_pairs={{0,6},{1,7},{2,4},{3,5},{4,2},{5,3},{6,0},{7,1},{8,14},{9,15},{10,... | collective-permute-start | bytes 884744 | tf_op jit(solution)/shard_map/ppermute | solution.py:38
  175.0 15.0 %collective-permute-start.32 = (bf16[512,768]{1,0:T(8,128)(2,1)}, bf16[512,768]{1,0:T(8,128)(2,1)S(1)}, u32[]{:S(2)}, u32[]{:S(2)}) collective-permute-start(bf16[512,768]{1,0:T(8,128)(2,1)} %get-tuple-element.147), channel_id=1, source_target_pairs={{0,8},{8,0},{16,24},{24,16},{1,9},{9,1},{17,25},{25,17},{2,10},{10... | collective-permute-start | bytes 2359304 | tf_op jit(solution)/shard_map/ppermute | solution.py:28
  179.4 10.6 %collective-permute-start.37 = (bf16[96,1536]{1,0:T(8,128)(2,1)S(1)}, bf16[96,1536]{1,0:T(8,128)(2,1)S(1)}, u32[]{:S(2)}, u32[]{:S(2)}) collective-permute-start(bf16[96,1536]{1,0:T(8,128)(2,1)S(1)} %add_convert_fusion.4.refs_0_), channel_id=1, source_target_pairs={{0,16},{8,24},{16,0},{24,8},{1,17},{9,25},{17,1},{25,9},{2,18},{10... | collective-permute-start | bytes 884744 | tf_op jit(solution)/shard_map/ppermute | solution.py:28
  183.5 13.2 %collective-permute-start.28 = (bf16[384,832]{0,1:T(8,128)(2,1)}, bf16[384,832]{0,1:T(8,128)(2,1)}, u32[]{:S(2)}, u32[]{:S(2)}) collective-permute-start(bf16[384,832]{0,1:T(8,128)(2,1)} %copy.39), channel_id=1, source_target_pairs={{0,1},{1,0},{2,3},{3,2},{4,5},{5,4},{6,7},{7,6},{8,9},{9,8},{10,11... | collective-permute-start | bytes 1916936 | tf_op jit(solution)/shard_map/ppermute | solution.py:38
  186.7 15.4 %collective-permute-start.35 = (bf16[256,768]{1,0:T(8,128)(2,1)}, bf16[256,768]{1,0:T(8,128)(2,1)}, u32[]{:S(2)}, u32[]{:S(2)}) collective-permute-start(bf16[256,768]{1,0:T(8,128)(2,1)} %add_convert_fusion.1), channel_id=1, source_target_pairs={{0,16},{8,24},{16,0},{24,8},{1,17},{9,25},{17,1},{25,9},{2,18},{10... | collective-permute-start | bytes 1179656 | tf_op jit(solution)/shard_map/ppermute | solution.py:28
  186.9 17.8 %collective-permute-start.36 = (bf16[96,1536]{1,0:T(8,128)(2,1)S(1)}, bf16[96,1536]{1,0:T(8,128)(2,1)S(1)}, u32[]{:S(2)}, u32[]{:S(2)}) collective-permute-start(bf16[96,1536]{1,0:T(8,128)(2,1)S(1)} %add_convert_fusion.4.refs_0_), channel_id=1, source_target_pairs={{0,8},{8,0},{16,24},{24,16},{1,9},{9,1},{17,25},{25,17},{2,10},{10... | collective-permute-start | bytes 884744 | tf_op jit(solution)/shard_map/ppermute | solution.py:28
  190.0 17.1 %collective-permute-start.38 = (bf16[96,1536]{1,0:T(8,128)(2,1)S(1)}, bf16[96,1536]{1,0:T(8,128)(2,1)S(1)}, u32[]{:S(2)}, u32[]{:S(2)}) collective-permute-start(bf16[96,1536]{1,0:T(8,128)(2,1)S(1)} %collective-permute-done.37.refs_2_), channel_id=1, source_target_pairs={{0,8},{8,0},{16,24},{24,16},{1,9},{9,1},{17,25},{25,17},{2,10},{10... | collective-permute-start | bytes 884744 | tf_op jit(solution)/shard_map/ppermute | solution.py:28
  191.0 22.8 %collective-permute-start.33 = (bf16[256,768]{1,0:T(8,128)(2,1)}, bf16[256,768]{1,0:T(8,128)(2,1)S(1)}, u32[]{:S(2)}, u32[]{:S(2)}) collective-permute-start(bf16[256,768]{1,0:T(8,128)(2,1)} %add_convert_fusion.2), channel_id=1, source_target_pairs={{0,16},{8,24},{16,0},{24,8},{1,17},{9,25},{17,1},{25,9},{2,18},{10... | collective-permute-start | bytes 1179656 | tf_op jit(solution)/shard_map/ppermute | solution.py:28
  201.3 16.7 %collective-permute-start.29 = (bf16[96,832]{1,0:T(8,128)(2,1)}, bf16[96,832]{1,0:T(8,128)(2,1)S(1)}, u32[]{:S(2)}, u32[]{:S(2)}) collective-permute-start(bf16[96,832]{1,0:T(8,128)(2,1)} %get-tuple-element.143), channel_id=1, source_target_pairs={{0,2},{1,3},{2,0},{3,1},{4,6},{5,7},{6,4},{7,5},{8,10},{9,11},{10,... | collective-permute-start | bytes 479240 | tf_op jit(solution)/shard_map/ppermute | solution.py:38
  202.1 15.8 %collective-permute-start.30 = (bf16[96,832]{1,0:T(8,128)(2,1)}, bf16[96,832]{1,0:T(8,128)(2,1)S(1)}, u32[]{:S(2)}, u32[]{:S(2)}) collective-permute-start(bf16[96,832]{1,0:T(8,128)(2,1)} %get-tuple-element.144), channel_id=1, source_target_pairs={{0,4},{1,5},{2,6},{3,7},{4,0},{5,1},{6,2},{7,3},{8,12},{9,13},{10,... | collective-permute-start | bytes 479240 | tf_op jit(solution)/shard_map/ppermute | solution.py:38
  204.6 14.2 %collective-permute-start.31 = (bf16[96,832]{1,0:T(8,128)(2,1)}, bf16[96,832]{1,0:T(8,128)(2,1)S(1)}, u32[]{:S(2)}, u32[]{:S(2)}) collective-permute-start(bf16[96,832]{1,0:T(8,128)(2,1)} %get-tuple-element.145), channel_id=1, source_target_pairs={{0,6},{1,7},{2,4},{3,5},{4,2},{5,3},{6,0},{7,1},{8,14},{9,15},{10,... | collective-permute-start | bytes 479240 | tf_op jit(solution)/shard_map/ppermute | solution.py:38
  218.9 4.3 %collective-permute-start.40 = (bf16[96,832]{1,0:T(8,128)(2,1)S(1)}, bf16[96,832]{1,0:T(8,128)(2,1)S(1)}, u32[]{:S(2)}, u32[]{:S(2)}) collective-permute-start(bf16[96,832]{1,0:T(8,128)(2,1)S(1)} %add_convert_fusion.5.refs_0_), channel_id=1, source_target_pairs={{0,16},{8,24},{16,0},{24,8},{1,17},{9,25},{17,1},{25,9},{2,18},{10... | collective-permute-start | bytes 479240 | tf_op jit(solution)/shard_map/ppermute | solution.py:28
  219.4 8.5 %collective-permute-start.39 = (bf16[96,832]{1,0:T(8,128)(2,1)S(1)}, bf16[96,832]{1,0:T(8,128)(2,1)S(1)}, u32[]{:S(2)}, u32[]{:S(2)}) collective-permute-start(bf16[96,832]{1,0:T(8,128)(2,1)S(1)} %add_convert_fusion.5.refs_0_), channel_id=1, source_target_pairs={{0,8},{8,0},{16,24},{24,16},{1,9},{9,1},{17,25},{25,17},{2,10},{10... | collective-permute-start | bytes 479240 | tf_op jit(solution)/shard_map/ppermute | solution.py:28
  223.2 5.7 %collective-permute-start.41 = (bf16[96,832]{1,0:T(8,128)(2,1)S(1)}, bf16[96,832]{1,0:T(8,128)(2,1)S(1)}, u32[]{:S(2)}, u32[]{:S(2)}) collective-permute-start(bf16[96,832]{1,0:T(8,128)(2,1)S(1)} %collective-permute-done.40.refs_2_), channel_id=1, source_target_pairs={{0,8},{8,0},{16,24},{24,16},{1,9},{9,1},{17,25},{25,17},{2,10},{10... | collective-permute-start | bytes 479240 | tf_op jit(solution)/shard_map/ppermute | solution.py:28
  (39 other events, 272.0 us)
Sparse Core Ops, SparseCore 0:
  12.5 60.4 all-gather.1

commit v2 on v1

--- a/solution.py
+++ b/solution.py
@@ -28,9 +28,11 @@
     return lax.ppermute(block, "rep", [(i, i ^ bit) for i in range(SPAN)])
 
 
-def rep_blocks(block):
+def rep_blocks(block, gate=None):
     far = swapped(block, 2)
     near = swapped(block, 1)
+    if gate is not None:
+        far = after(far, gate)
     return (block, near, far, swapped(far, 1))
 
 
@@ -56,20 +58,25 @@
                 store(start, ref, index * self.rows, self.rows)
 
 
-def shard_gather(block, gate=None):
-    shards = lax.axis_size("shard")
-    if shards != FEW:
-        full = lax.all_gather(block, "shard", axis=0, tiled=True)
-        return Pieces([full], None, block.shape[0])
-    cross = swap_shard(block, 1)
-    sent = block if gate is None else after(block, (gate, cross))
-    one = swap_shard(sent, 2)
-    two = swap_shard(sent, 4)
-    three = swap_shard(sent, 6)
-    other = jnp.concatenate([one, two, three], axis=0)
-    other = swap_shard(after(other, cross), 1)
+def shard_gather(block, *others):
+    blocks = (block,) + others
+    if lax.axis_size("shard") != FEW:
+        return [
+            Pieces([lax.all_gather(b, "shard", axis=0, tiled=True)], None, b.shape[0])
+            for b in blocks
+        ]
+    crossed = [swap_shard(b, 1) for b in blocks]
     codes = [[0], [1], [2], [4], [6], [3, 5, 7]]
-    return Pieces([block, cross, one, two, three, other], codes, block.shape[0])
+    results = []
+    gate = None
+    for b, cross in zip(blocks, crossed):
+        sent = b if gate is None else after(b, (gate, crossed))
+        one, two, three = (swap_shard(sent, bits) for bits in (2, 4, 6))
+        gate = three
+        other = jnp.concatenate([one, two, three], axis=0)
+        other = swap_shard(after(other, crossed), 1)
+        results.append(Pieces([b, cross, one, two, three, other], codes, b.shape[0]))
+    return results
 
 
 def middle_kernel(place_ref, kept_ref, received_ref, own_ref, *sent_refs):
@@ -85,7 +92,10 @@
 
 
 def scatter_middle(place, kept, sent):
-    received = swap_shard(sent, 1)
+    return scatter_high(place, kept, swap_shard(sent, 1))
+
+
+def scatter_high(place, kept, received):
     count = FEW // 2
     rows, columns = kept.shape[0] // count, kept.shape[1]
     own, *sends = call(
@@ -439,20 +449,28 @@
         send_parts(grad, index ^ rep, near_ref, far_ref, own_ref)
 
 
-def third_kernel(place_ref, act_ref, hidden_ref, pre_ref, cot_ref, wide_ref, *refs):
-    grad_refs, (near_ref, far_ref, own_ref, sum_ref, grad_ref) = refs[:-5], refs[-5:]
-    rep = place_ref[0]
-    total, width = cot_ref.shape
-    rows = total // SPAN
+def down_grad_kernel(place_ref, act_ref, cot_ref, *refs):
+    grad_refs, grad_ref = refs[:-1], refs[-1]
     units = act_ref.shape[1]
     step = units // 3
     for first in range(0, units, step):
-        grad_ref[first : first + step, :width] = contract_rows(
+        grad_ref[first : first + step, :] = contract_rows(
             act_ref[:, first : first + step], cot_ref[...]
         ).astype(BF16)
+    if len(grad_refs) == 2:
+        split_halves(place_ref, grad_ref, *grad_refs)
+    else:
+        grad_refs[0][...] = grad_ref[...]
+
+
+def third_kernel(place_ref, act_ref, hidden_ref, pre_ref, wide_ref, *refs):
+    grad_refs, (near_ref, far_ref, own_ref, sum_ref, grad_ref) = refs[:-5], refs[-5:]
+    rep = place_ref[0]
+    total, width = hidden_ref.shape
+    rows = total // SPAN
     step = width // 3
     for first in range(0, width, step):
-        grad_ref[first : first + step, width:] = contract_rows(
+        grad_ref[first : first + step, :] = contract_rows(
             hidden_ref[:, first : first + step], pre_ref[...]
         ).astype(BF16)
     sum_ref[...] = jnp.broadcast_to(
@@ -594,7 +612,7 @@
         grad_ref[from_rows, 3 * part : 4 * part] = contract_rows(ref[...], branch_part).astype(
             BF16
         )
-    grad_ref[:, 4 * part :] = small_grads[...].T[:, :64].astype(BF16)
+    grad_ref[:, 4 * part :] = small_grads[...].T.astype(BF16)
     if len(grad_refs) == 2:
         split_halves(place_ref, grad_ref, *grad_refs)
     else:
@@ -629,7 +647,7 @@
     small = blocks[0][:, 4 * part :]
     for block in blocks[1:]:
         small = small + block[:, 4 * part :]
-    small = jnp.concatenate([small, small], axis=1).T[:12, :]
+    small = small.T[: ins[6].shape[0], :]
     grads = (jnp.concatenate(qkv, axis=1), jnp.concatenate(out, axis=1), small)
     for at, (gradient, rate) in enumerate(zip(grads, (RATE_MATRIX, RATE_MATRIX, RATE_SMALL))):
         weight, first, second = (ref[...] for ref in ins[3 * at : 3 * at + 3])
@@ -673,7 +691,7 @@
         out_specs=[spec] * 3,
         compiler_params=pltpu.CompilerParams(vmem_limit_bytes=16 * 2**20),
         cost_estimate=pl.CostEstimate(
-            flops=20 * rows * columns, bytes_accessed=26 * rows * columns, transcendentals=0
+            flops=0, bytes_accessed=0, transcendentals=0
         ),
     )(place, *blocks, *arrays))
 
@@ -757,11 +775,11 @@
         second_send = jnp.concatenate([low_out[:, :half], low_up.reshape(owned, -1)], axis=1)
         third_send = jnp.concatenate([low_out[:, half:], low_down], axis=1)
     third_full = lax.all_gather(third_send, "shard", axis=0, tiled=True)
-    first_pieces = shard_gather(first_send)
-    second_pieces = shard_gather(second_send, first_pieces.arrays[-2 * few])
+    first_pieces, second_pieces = shard_gather(first_send, second_send)
 
     seg_block = jnp.pad(segments.astype(BF16)[None, :], ((0, 15), (0, width - rows)))
-    token_blocks = rep_blocks(jnp.concatenate([tokens, seg_block], axis=0))
+    with_seg = jnp.concatenate([tokens, seg_block], axis=0)
+    token_blocks = rep_blocks(with_seg)
     cot_blocks = rep_blocks(after(cotangent, token_blocks[2]))
 
     (
@@ -835,27 +853,18 @@
     )
     near, far, far_send = rep_sum(near_send, far_part)
     hidden_two_terms = own, near, far
-    *wide_grad, mixed_near, mixed_far, mixed_own, unit_sums = call(
-        third_kernel,
-        [shape(ff_part // 2, 2 * width)] * 2 * few
-        + [shape(ff_part, 2 * width)] * (not few)
-        + [
-            shape(2 * rows, width),
-            shape(rows, width, dtype=F32),
-            shape(rows, width, dtype=F32),
-            shape(8, ff_part, dtype=F32),
-        ],
-        [pltpu.VMEM((ff_part, 2 * width), BF16)],
-        18 * total * width * width,
+    down_grad = call(
+        down_grad_kernel,
+        [shape(ff_part // 2, width)] * 2 * few + [shape(ff_part, width)] * (not few),
+        [pltpu.VMEM((ff_part, width), BF16)],
+        6 * total * width * width,
         56,
         place,
         after(act_low, far_send),
-        hidden_two,
-        pre_low,
         all_cot,
-        third_full,
-    )
-    near, unit_sums = lax.optimization_barrier((near, unit_sums))
+    )
+    if few:
+        down_received = swap_shard(down_grad[1], 1)
     hidden_two_terms = own, near, far
     resid_grad, branch, sums = call(
         fourth_kernel,
@@ -874,19 +883,40 @@
         small,
     )
     branch_blocks = rep_blocks(branch)
+    gate = down_grad[0]
+    if few:
+        down_own, down_received = scatter_high(place, after(down_grad[0], branch), down_received)
+        gate = down_own
+    *up_grad, mixed_near, mixed_far, mixed_own, unit_sums = call(
+        third_kernel,
+        [shape(width // 2, ff_part)] * 2 * few
+        + [shape(width, ff_part)] * (not few)
+        + [
+            shape(2 * rows, width),
+            shape(rows, width, dtype=F32),
+            shape(rows, width, dtype=F32),
+            shape(8, ff_part, dtype=F32),
+        ],
+        [pltpu.VMEM((width, ff_part), BF16)],
+        12 * total * width * width,
+        56,
+        place,
+        after(act_low, gate),
+        hidden_two,
+        pre_low,
+        third_full,
+    )
+    if few:
+        up_received = swap_shard(up_grad[1], 1)
     near_mixed, far_mixed, _ = rep_sum(after(mixed_near, branch), mixed_far, branch_blocks[2])
-    if few:
-        kept = after(wide_grad[0], branch_blocks[2])
-        wide_own, wide_received = scatter_middle(place, kept, after(wide_grad[1], far))
-        branch_blocks = (after(branch, wide_own),) + branch_blocks[1:]
     unit_rows = lax.dynamic_update_slice(
         jnp.zeros((shards, SPAN, units), F32), unit_sums[0].reshape(shards, 1, units), (0, rep, 0)
     ).reshape(ff // width, width)
     unit_rows = jnp.pad(unit_rows, ((0, 8 - ff // width), (0, 0)))
     *last_grad, near_send, far_part, own = call(
         fifth_kernel,
-        [shape(width // 2, 4 * part + 64)] * 2 * few
-        + [shape(width, 4 * part + 64)] * (not few)
+        [shape(width // 2, 4 * part + 128)] * 2 * few
+        + [shape(width, 4 * part + 128)] * (not few)
         + [
             shape(2 * rows, width),
             shape(rows, width, dtype=F32),
@@ -899,7 +929,7 @@
             pltpu.VMEM((total, part), F32),
             pltpu.VMEM((total, part), F32),
             pltpu.VMEM((128, width), F32),
-            pltpu.VMEM((width, 4 * part + 64), BF16),
+            pltpu.VMEM((width, 4 * part + 128), BF16),
             pltpu.VMEM((total, width), BF16),
         ],
         12 * total * width * width + 72 * total * total * part,
@@ -923,15 +953,21 @@
     near, far, far_send = rep_sum(near_send, far_part)
     if few:
         last_kept, last_sent = last_grad
-        last_sent, wide_received = lax.optimization_barrier((last_sent, wide_received))
+        last_sent, down_received = lax.optimization_barrier((last_sent, down_received))
         last_own, last_received = scatter_middle(place, last_kept, last_sent)
-        wide_blocks = rep_blocks(scatter_end(wide_own, wide_received))
+        up_own, up_received = scatter_high(
+            place, after(up_grad[0], (last_grad[0], down_received)), up_received
+        )
+        down_own, up_received = after((down_own, up_received), last_own)
+        wide_total = jnp.concatenate(
+            [scatter_end(down_own, down_received), scatter_end(up_own, up_received)], axis=1
+        )
+        wide_blocks = rep_blocks(wide_total, last_received)
     else:
-        last_total, wide_total = (
+        last_total, down_total, up_total = (
             lax.psum_scatter(grad, "shard", scatter_dimension=0, tiled=True)
-            for grad in (last_grad[0], wide_grad[0])
-        )
-        wide_blocks = rep_blocks(wide_total)
+            for grad in (last_grad[0], down_grad[0], up_grad[0])
+        )
     mixed = residual + (
         mixed_own + near_mixed[rows:].astype(F32) + far_mixed.astype(F32) + small[7]
     )
@@ -967,10 +1003,15 @@
             pl.BlockSpec((units, width), lambda i: (0, 0)),
             (down_weight, down_first, down_second),
         )
-        last_received, input_grad, mixed, up_res[0], down_res[0] = lax.optimization_barrier(
-            (last_received, input_grad, mixed, up_res[0], down_res[0])
+        last_received, input_grad, mixed = lax.optimization_barrier(
+            (last_received, input_grad, mixed)
         )
         last_total = scatter_end(last_own, last_received)
+        last_blocks = rep_blocks(last_total)
+        last_near, up_res[0], down_res[0] = lax.optimization_barrier(
+            (last_blocks[1], up_res[0], down_res[0])
+        )
+        last_blocks = (last_blocks[0], last_near) + last_blocks[2:]
         results = call(
             adam_kernel,
             [shape(*ref.shape, dtype=F32) for ref in (qkv_weight, out_weight, small_weights)
@@ -979,7 +1020,7 @@
             20 * qkv_weight.size,
             56,
             place,
-            *rep_blocks(last_total),
+            *last_blocks,
             qkv_weight,
             qkv_first,
             qkv_second,
@@ -992,9 +1033,9 @@
         )
         qkv_res, out_res, small_res = results[:3], results[3:6], results[6:]
     else:
-        wide_own = in_order(wide_blocks, rep)
-        down_own = jnp.concatenate([g[:, :width] for g in wide_own], axis=0).astype(F32)
-        up_own = [g[:, width:].reshape(owned, shards, units) for g in wide_own]
+        down_own = jnp.concatenate(in_order(rep_blocks(down_total), rep), axis=0).astype(F32)
+        up_own = in_order(rep_blocks(up_total), rep)
+        up_own = [g.reshape(owned, shards, units) for g in up_own]
         up_own = jnp.stack(up_own, axis=2).reshape(owned, ff).astype(F32)
         up_res = adam_update(up_weight, up_own, up_first, up_second, RATE_MATRIX)
         down_res = adam_update(down_weight, down_own, down_first, down_second, RATE_MATRIX)

time: 246 us -> 233 us (0.947)
  waiting for transfers between devices: 59.2 us -> 48.7 us
  other arithmetic: 7.63 us -> 3.6 us
  Pallas kernels: 85.2 us -> 89.2 us
    ppermute x18 -> x22, waiting for transfers between devices: 48.7 us -> 27.1 us  [swap_shard(): lax.ppermute(block, 'shard', [(i, i ^ bits) for i in range(lax.axis_size(...]
    ppermute x24, waiting for transfers between devices: 10.5 us -> 21.5 us  [swapped(): return lax.ppermute(block, 'rep', [(i, i ^ bit) for i in range(SPAN)])]
    pallas_call x10 -> x12, Pallas kernels: 78.5 us -> 82.5 us  [call(): pl.pallas_call(kernel, out_shape=tuple(outs), in_specs=[pl.BlockSpec(memo...]
    ppermute x24, starting transfers between devices: 40.5 us -> 44 us  [swapped(): return lax.ppermute(block, 'rep', [(i, i ^ bit) for i in range(SPAN)])]
    convert_element_type x3, other arithmetic: 4.27 us -> 1.64 us  [rep_sum(): far_send = (far_part + near[:rows].astype(F32)).astype(BF16)]
    ppermute x18 -> x22, starting transfers between devices: 20.5 us -> 18.2 us  [swap_shard(): lax.ppermute(block, 'shard', [(i, i ^ bits) for i in range(lax.axis_size(...]
    unnamed x88 -> x102, local copies, waits for them, and re-layouts: 5.53 us -> 7.56 us
  transfers between devices with their start and end apart: 43 -> 47, of which waited for: 12 -> 17; matrix products, arithmetic and copies ran while one was open for 6% -> 2% of each run, Pallas kernels for 24% -> 27%
where the time goes in v2:
time: 233 us; the launch traced here: 230 us
  Pallas kernels  89.2 us (38%)
  starting transfers between devices  62.3 us (27%)
  waiting for transfers between devices  48.7 us (21%)
  between operations  14.5 us (6%)
  local copies, waits for them, and re-layouts  11.7 us (5%)
  other arithmetic  3.6 us (2%)
    pallas_call x12, Pallas kernels, call(): pl.pallas_call(kernel, out_shape=tuple(outs), in_specs=[pl.BlockSpec(memo...  82.5 us
    ppermute x24, starting transfers between devices, swapped(): return lax.ppermute(block, 'rep', [(i, i ^ bit) for i in range(SPAN)])  44 us
    ppermute x22, waiting for transfers between devices, swap_shard(): lax.ppermute(block, 'shard', [(i, i ^ bits) for i in range(lax.axis_size(...  27.1 us
    ppermute x24, waiting for transfers between devices, swapped(): return lax.ppermute(block, 'rep', [(i, i ^ bit) for i in range(SPAN)])  21.5 us
    ppermute x22, starting transfers between devices, swap_shard(): lax.ppermute(block, 'shard', [(i, i ^ bits) for i in range(lax.axis_size(...  18.2 us
    unnamed x102, local copies, waits for them, and re-layouts  7.56 us
    pallas_call x2, Pallas kernels, grid_adam(): pl.pallas_call(kernel, grid=(steps,), out_shape=[shape(rows, columns, dty...  6.66 us
  transfers between devices with their start and end apart: 47, of which 17 were waited for; matrix products, arithmetic and copies ran while one was open for 2% of the time, Pallas kernels for 27%

profile of v2, /device:TPU:11, one launch (start us, length us, event | category | flops | bytes accessed | tf_op | source)
XLA Modules:
  0.0 229.9 jit_solution(18045289676280495666)
XLA Ops:
  7.9 4.5 %shard_map.305 = (bf16[96,640]{1,0:T(8,128)(2,1)}, bf16[96,1152]{1,0:T(8,128)(2,1)}, bf16[96,1152]{1,0:T(8,128)(2,1)}) custom-call(s32[2]{0:T(128)} %pad_add_fusion.place_ref.refs_0_, f32[96,2304]{1,0:T(8,128)} %refs_4_.5, f32[96,768]{1,0:T(8,128)} %refs_7_.1, f32[96,3072]{1,0:T(8,128)} %refs_4_.3, f32[384,768]{1,0:T(8,128)} %refs_4_.4, f32[12,96]{1,0:T(8,128)} %refs_10_.1), custom_call_target="tpu_custom_call" | custom-call | flops 73728 | bytes 4108808 | tf_op jit(solution)/shard_map/pallas_call | solution.py:257
  12.5 1.3 collective-permute-start.1
  13.8 1.3 collective-permute-start.6
  15.1 2.2 collective-permute-start.4
  17.6 2.8 %collective-permute-done.6.refs_9_ = bf16[96,640]{1,0:T(8,128)(2,1)S(1)} collective-permute-done((bf16[96,640]{1,0:T(8,128)(2,1)}, bf16[96,640]{1,0:T(8,128)(2,1)S(1)}, u32[]{:S(2)}, u32[]{:S(2)}) %collective-permute-start.6) | collective-permute-done | bytes 122912 | tf_op jit(solution)/shard_map/ppermute | solution.py:40
  20.6 2.0 collective-permute-done.4.refs_7_
  22.7 4.7 %collective-permute-start = (bf16[272,768]{1,0:T(8,128)(2,1)S(1)}, bf16[272,768]{1,0:T(8,128)(2,1)S(1)}, u32[]{:S(2)}, u32[]{:S(2)}) collective-permute-start(bf16[272,768]{1,0:T(8,128)(2,1)S(1)} %fusion.1.refs_1_), channel_id=1, source_target_pairs={{0,8},{8,0},{16,24},{24,16},{1,9},{9,1},{17,25},{25,17},{2,10},{10... | collective-permute-start | bytes 1253384 | tf_op jit(solution)/shard_map/ppermute | solution.py:28
  29.0 1.4 collective-permute-start.15
  30.5 1.2 collective-permute-start.17
  31.7 4.7 %collective-permute-done.8.refs_10_ = bf16[288,640]{1,0:T(8,128)(2,1)S(1)} collective-permute-done((bf16[288,640]{1,0:T(8,128)(2,1)S(1)}, bf16[288,640]{1,0:T(8,128)(2,1)S(1)}, u32[]{:S(2)}, u32[]{:S(2)}) %collective-permute-start.8) | collective-permute-done | bytes 368672 | tf_op jit(solution)/shard_map/ppermute | solution.py:40
  37.8 10.2 %shard_map.306 = (bf16[1024,768]{1,0:T(8,128)(2,1)}, bf16[768,576]{1,0:T(8,128)(2,1)}, f32[16,768]{1,0:T(8,128)}, bf16[1024,192]{1,0:T(8,128)(2,1)}, bf16[1024,1...) custom-call(s32[2]{0:T(128)} %pad_add_fusion.place_ref.refs_0_, ...), custom_call_target="tpu_custom_call" | custom-call | flops 12079595520 | bytes 7323656 | tf_op jit(solution)/shard_map/pallas_call | solution.py:257
  49.0 7.6 %collective-permute-done.17.refs_13_ = bf16[96,1152]{1,0:T(8,128)(2,1)S(1)} collective-permute-done((bf16[96,1152]{1,0:T(8,128)(2,1)S(1)}, bf16[96,1152]{1,0:T(8,128)(2,1)S(1)}, u32[]{:S(2)}, u32[]{:S(2)}) %collective-permute-start.17) | collective-permute-done | bytes 221216 | tf_op jit(solution)/shard_map/ppermute | solution.py:40
  57.3 12.6 %collective-permute-start.12 = (bf16[256,768]{1,0:T(8,128)(2,1)S(1)}, bf16[256,768]{1,0:T(8,128)(2,1)}, u32[]{:S(2)}, u32[]{:S(2)}) collective-permute-start(bf16[256,768]{1,0:T(8,128)(2,1)S(1)} %copy-done.20), channel_id=1, source_target_pairs={{0,8},{8,0},{16,24},{24,16},{1,9},{9,1},{17,25},{25,17},{2,10},{10... | collective-permute-start | bytes 1179656 | tf_op jit(solution)/shard_map/ppermute | solution.py:28
  73.4 17.2 %shard_map.307 = (bf16[768,768]{1,0:T(8,128)(2,1)}, bf16[1024,768]{1,0:T(8,128)(2,1)}, bf16[1024,768]{1,0:T(8,128)(2,1)}, bf16[1024,768]{1,0:T(8,128)(2,1)}, bf1...) custom-call(s32[2]{0:T(128)} %pad_add_fusion.place_ref.refs_0_, ...), custom_call_target="tpu_custom_call" | custom-call | flops 19327352832 | bytes 18926600 | tf_op jit(solution)/shard_map/pallas_call | solution.py:257
  90.6 6.6 %collective-permute-start.19 = (bf16[512,768]{1,0:T(8,128)(2,1)}, bf16[512,768]{1,0:T(8,128)(2,1)S(1)}, u32[]{:S(2)}, u32[]{:S(2)}) collective-permute-start(bf16[512,768]{1,0:T(8,128)(2,1)} %get-tuple-element.120), channel_id=1, source_target_pairs={{0,8},{8,0},{16,24},{24,16},{1,9},{9,1},{17,25},{25,17},{2,10},{10... | collective-permute-start | bytes 2359304 | tf_op jit(solution)/shard_map/ppermute | solution.py:28
  97.2 2.1 collective-permute-done.19.near_ref
  99.4 1.5 add_convert_fusion.3
  101.2 4.6 %shard_map.309 = (bf16[384,768]{1,0:T(8,128)(2,1)}, bf16[384,768]{1,0:T(8,128)(2,1)}) custom-call(s32[2]{0:T(128)} %pad_add_fusion.place_ref.refs_0_, bf16[1024,768]{1,0:T(8,128)(2,1)} %get-tuple-element.140.act_ref, bf16[1024,768]{1,0:T(8,128)(2,1)} %get-tuple-element.135.cot_ref), custom_call_target="tpu_custom_call" | custom-call | flops 3623878656 | bytes 4325384 | tf_op jit(solution)/shard_map/pallas_call | solution.py:257
  106.8 4.5 %collective-permute-done.20.far_ref = bf16[256,768]{1,0:T(8,128)(2,1)S(1)} collective-permute-done((bf16[256,768]{1,0:T(8,128)(2,1)S(1)}, bf16[256,768]{1,0:T(8,128)(2,1)S(1)}, u32[]{:S(2)}, u32[]{:S(2)}) %collective-permute-start.20) | collective-permute-done | bytes 393248 | tf_op jit(solution)/shard_map/ppermute | solution.py:28
  112.0 3.6 %shard_map.308 = (f32[256,768]{1,0:T(8,128)}, bf16[256,768]{1,0:T(8,128)(2,1)}, f32[8,768]{1,0:T(8,128)}) custom-call(s32[2]{0:T(128)} %pad_add_fusion.place_ref.refs_0_, f32[256,768]{1,0:T(8,128)} %get-tuple-element.119.own_ref, bf16[512,768]{1,0:T(8,128)(2,1)} %copy-done.9, bf16[256,768]{1,0:T(8,128)(2,1)} %copy-done.21, ...), custom_call_target="tpu_custom_call" | custom-call | flops 1966080 | bytes 4399112 | tf_op jit(solution)/shard_map/pallas_call | solution.py:257
  115.9 1.5 collective-permute-start.21
  117.4 2.9 %collective-permute-done.24.received_ref = bf16[384,768]{1,0:T(8,128)(2,1)S(1)} collective-permute-done((bf16[384,768]{1,0:T(8,128)(2,1)}, bf16[384,768]{1,0:T(8,128)(2,1)S(1)}, u32[]{:S(2)}, u32[]{:S(2)}) %collective-permute-start.24) | collective-permute-done | bytes 589856 | tf_op jit(solution)/shard_map/ppermute | solution.py:40
  121.1 2.2 shard_map.310
  123.3 2.0 collective-permute-done.22.branch_c
  125.2 2.1 collective-permute-start.23
  127.4 8.4 %shard_map.311 = (bf16[384,768]{1,0:T(8,128)(2,1)}, bf16[384,768]{1,0:T(8,128)(2,1)}, bf16[512,768]{1,0:T(8,128)(2,1)}, f32[256,768]{1,0:T(8,128)}, f32[256,768]{1,0:T(8,128)}, /*index=5*/f32[8,768]{1,0:T(8,128)}) custom-call(s32[2]{0:T(128)} %pad_add_fusion.place_ref.refs_0_, bf16[1024,768]{1,0:T(8,128)(2,1)} %get-tuple-element.140.act_ref, ...), custom_call_target="tpu_custom_call" | custom-call | flops 7247757312 | bytes 10051592 | tf_op jit(solution)/shard_map/pallas_call | solution.py:257
  137.5 2.2 collective-permute-start.26
  140.2 1.1 collective-permute-start.37
  141.3 1.3 collective-permute-start.34
  142.6 18.8 %shard_map.312 = (bf16[384,896]{1,0:T(8,128)(2,1)}, bf16[384,896]{1,0:T(8,128)(2,1)}, bf16[512,768]{1,0:T(8,128)(2,1)}, f32[256,768]{1,0:T(8,128)}, f32[256,768]{1,0:T(8,128)}) custom-call(s32[2]{0:T(128)} %pad_add_fusion.place_ref.refs_0_, bf16[256,768]{1,0:T(8,128)(2,1)} %get-tuple-element.123.branch_a, bf16[256,768]{1,0:T(8,128)(2,1)} %copy-done.41, ...), custom_call_target="tpu_custom_call" | custom-call | flops 21743271936 | bytes 12386312 | tf_op jit(solution)/shard_map/pallas_call | solution.py:257
  161.8 1.0 collective-permute-start.32
  164.9 2.2 shard_map.315
  167.8 1.5 collective-permute-start.39
  169.2 4.5 %collective-permute-done.35 = bf16[256,768]{1,0:T(8,128)(2,1)S(1)} collective-permute-done((bf16[256,768]{1,0:T(8,128)(2,1)S(1)}, bf16[256,768]{1,0:T(8,128)(2,1)S(1)}, u32[]{:S(2)}, u32[]{:S(2)}) %collective-permute-start.35) | collective-permute-done | bytes 393248 | tf_op jit(solution)/shard_map/ppermute | solution.py:28
  175.6 2.2 collective-permute-done.28.received_ref
  178.7 2.3 shard_map.313
  181.0 2.5 %collective-permute-done.40 = bf16[96,768]{1,0:T(8,128)(2,1)S(1)} collective-permute-done((bf16[96,768]{1,0:T(8,128)(2,1)}, bf16[96,768]{1,0:T(8,128)(2,1)S(1)}, u32[]{:S(2)}, u32[]{:S(2)}) %collective-permute-start.40) | collective-permute-done | bytes 147488 | tf_op jit(solution)/shard_map/ppermute | solution.py:40
  183.5 1.7 collective-permute-start.30
  186.2 1.2 collective-permute-start.33
  188.3 7.0 %collective-permute-done.33.far_ref = bf16[256,768]{1,0:T(8,128)(2,1)S(1)} collective-permute-done((bf16[256,768]{1,0:T(8,128)(2,1)S(1)}, bf16[256,768]{1,0:T(8,128)(2,1)S(1)}, u32[]{:S(2)}, u32[]{:S(2)}) %collective-permute-start.33) | collective-permute-done | bytes 393248 | tf_op jit(solution)/shard_map/ppermute | solution.py:28
  196.1 3.5 %shard_map.314 = f32[256,768]{1,0:T(8,128)} custom-call(s32[2]{0:T(128)} %pad_add_fusion.place_ref.refs_0_, f32[256,768]{1,0:T(8,128)} %get-tuple-element.153.own_ref, bf16[512,768]{1,0:T(8,128)(2,1)} %copy-done.8, bf16[256,768]{1,0:T(8,128)(2,1)} %copy-done.19, bf16[256,768]{1,0:T(8,128)(2,1)} %tokens_ref.1, f32[256,768]{1,0:T(8,128)} %get-tuple-element.156.resid_grad_ref, ...), custom_call_target="tpu_custom_call" | custom-call | flops 1966080 | bytes 3981320 | tf_op jit(solution)/shard_map/pallas_call | solution.py:257
  199.5 1.5 collective-permute-done.31
  201.2 1.2 collective-permute-start.44
  202.4 3.4 %collective-permute-start.41 = (bf16[96,1536]{1,0:T(8,128)(2,1)S(1)}, bf16[96,1536]{1,0:T(8,128)(2,1)S(1)}, u32[]{:S(2)}, u32[]{:S(2)}) collective-permute-start(bf16[96,1536]{1,0:T(8,128)(2,1)S(1)} %pad_maximum_fusion.2.refs_0_), channel_id=1, source_target_pairs={{0,8},{8,0},{16,24},{24,16},{1,9},{9,1},{17,25},{25,17},{2,10},{10... | collective-permute-start | bytes 884744 | tf_op jit(solution)/shard_map/ppermute | solution.py:28
  206.4 3.5 %collective-permute-start.45 = (bf16[96,896]{1,0:T(8,128)(2,1)S(1)}, bf16[96,896]{1,0:T(8,128)(2,1)S(1)}, u32[]{:S(2)}, u32[]{:S(2)}) collective-permute-start(bf16[96,896]{1,0:T(8,128)(2,1)S(1)} %collective-permute-done.44.refs_2_), channel_id=1, source_target_pairs={{0,8},{8,0},{16,24},{24,16},{1,9},{9,1},{17,25},{25,17},{2,10},{10... | collective-permute-start | bytes 516104 | tf_op jit(solution)/shard_map/ppermute | solution.py:28
  209.9 3.2 %shard_map.317 = (f32[384,768]{1,0:T(8,128)}, f32[384,768]{1,0:T(8,128)}, f32[384,768]{1,0:T(8,128)}) custom-call(s32[2]{0:T(128)S(1)} %copy-done.6, bf16[96,1536]{1,0:T(8,128)(2,1)S(1)} %pad_maximum_fusion.2.refs_0_, bf16[96,1536]{1,0:T(8,128)(2,1)S(1)} %collective-permute-done.41.refs_1_, bf16[96,1536]{1,0:T(8,128)(2,1)S(1)} %collective-permute-done.42.refs_2_, ...), custom_call_target="tpu_custom_call" | custom-call | tf_op jit(solution)/shard_map/pallas_call | solution.py:684
  213.2 3.4 %shard_map.316 = (f32[96,3072]{1,0:T(8,128)}, f32[96,3072]{1,0:T(8,128)}, f32[96,3072]{1,0:T(8,128)}) custom-call(s32[2]{0:T(128)S(1)} %copy-done.6, bf16[96,1536]{1,0:T(8,128)(2,1)S(1)} %pad_maximum_fusion.2.refs_0_, bf16[96,1536]{1,0:T(8,128)(2,1)S(1)} %collective-permute-done.41.refs_1_, bf16[96,1536]{1,0:T(8,128)(2,1)S(1)} %collective-permute-done.42.refs_2_, ...), custom_call_target="tpu_custom_call" | custom-call | tf_op jit(solution)/shard_map/pallas_call | solution.py:684
  217.9 5.2 %shard_map.318 = (f32[96,2304]{1,0:T(8,128)}, f32[96,2304]{1,0:T(8,128)}, f32[96,2304]{1,0:T(8,128)}, f32[96,768]{1,0:T(8,128)}, f32[96,768]{1,0:T(8,128)}, /*in...) custom-call(s32[2]{0:T(128)} %pad_add_fusion.place_ref.refs_0_, ...), custom_call_target="tpu_custom_call" | custom-call | flops 4423680 | bytes 7793672 | tf_op jit(solution)/shard_map/pallas_call | solution.py:257
  (187 shorter events, 25.5 us)
Async XLA Ops:
  7.2 66.2 %all-gather.2.cloned.1.call-start = ((), (), s32[]{:S(2)}) async-start(), calls=%async_computation | async-start | bytes 1990656 | tf_op jit(solution)/shard_map/all_gather | solution.py:777
  12.5 14.8 %collective-permute-start.1 = (bf16[272,768]{1,0:T(8,128)(2,1)S(1)}, bf16[272,768]{1,0:T(8,128)(2,1)S(1)}, u32[]{:S(2)}, u32[]{:S(2)}) collective-permute-start(bf16[272,768]{1,0:T(8,128)(2,1)S(1)} %fusion.1.refs_1_), channel_id=1, source_target_pairs={{0,16},{8,24},{16,0},{24,8},{1,17},{9,25},{17,1},{25,9},{2,18},{10... | collective-permute-start | bytes 1253384 | tf_op jit(solution)/shard_map/ppermute | solution.py:28
  13.8 6.6 %collective-permute-start.6 = (bf16[96,640]{1,0:T(8,128)(2,1)}, bf16[96,640]{1,0:T(8,128)(2,1)S(1)}, u32[]{:S(2)}, u32[]{:S(2)}) collective-permute-start(bf16[96,640]{1,0:T(8,128)(2,1)} %get-tuple-element.109.refs_5_), channel_id=1, source_target_pairs={{0,6},{1,7},{2,4},{3,5},{4,2},{5,3},{6,0},{7,1},{8,14},{9,15},{10,... | collective-permute-start | bytes 368648 | tf_op jit(solution)/shard_map/ppermute | solution.py:40
  15.1 7.5 %collective-permute-start.4 = (bf16[96,640]{1,0:T(8,128)(2,1)}, bf16[96,640]{1,0:T(8,128)(2,1)S(1)}, u32[]{:S(2)}, u32[]{:S(2)}) collective-permute-start(bf16[96,640]{1,0:T(8,128)(2,1)} %get-tuple-element.109.refs_5_), channel_id=1, source_target_pairs={{0,2},{1,3},{2,0},{3,1},{4,6},{5,7},{6,4},{7,5},{8,10},{9,11},{10,... | collective-permute-start | bytes 368648 | tf_op jit(solution)/shard_map/ppermute | solution.py:40
  17.3 10.1 %collective-permute-start.5 = (bf16[96,640]{1,0:T(8,128)(2,1)}, bf16[96,640]{1,0:T(8,128)(2,1)S(1)}, u32[]{:S(2)}, u32[]{:S(2)}) collective-permute-start(bf16[96,640]{1,0:T(8,128)(2,1)} %get-tuple-element.109.refs_5_), channel_id=1, source_target_pairs={{0,4},{1,5},{2,6},{3,7},{4,0},{5,1},{6,2},{7,3},{8,12},{9,13},{10,... | collective-permute-start | bytes 368648 | tf_op jit(solution)/shard_map/ppermute | solution.py:40
  17.3 11.0 %collective-permute-start.7 = (bf16[96,1152]{1,0:T(8,128)(2,1)}, bf16[96,1152]{1,0:T(8,128)(2,1)S(1)}, u32[]{:S(2)}, u32[]{:S(2)}) collective-permute-start(bf16[96,1152]{1,0:T(8,128)(2,1)} %get-tuple-element.114.refs_9_), channel_id=1, source_target_pairs={{0,1},{1,0},{2,3},{3,2},{4,5},{5,4},{6,7},{7,6},{8,9},{9,8},{10,11... | collective-permute-start | bytes 663560 | tf_op jit(solution)/shard_map/ppermute | solution.py:40
  20.4 7.9 %collective-permute-start.3 = (bf16[96,640]{1,0:T(8,128)(2,1)}, bf16[96,640]{1,0:T(8,128)(2,1)S(1)}, u32[]{:S(2)}, u32[]{:S(2)}) collective-permute-start(bf16[96,640]{1,0:T(8,128)(2,1)} %get-tuple-element.109.refs_5_), channel_id=1, source_target_pairs={{0,1},{1,0},{2,3},{3,2},{4,5},{5,4},{6,7},{7,6},{8,9},{9,8},{10,11... | collective-permute-start | bytes 368648 | tf_op jit(solution)/shard_map/ppermute | solution.py:40
  22.7 7.8 %collective-permute-start = (bf16[272,768]{1,0:T(8,128)(2,1)S(1)}, bf16[272,768]{1,0:T(8,128)(2,1)S(1)}, u32[]{:S(2)}, u32[]{:S(2)}) collective-permute-start(bf16[272,768]{1,0:T(8,128)(2,1)S(1)} %fusion.1.refs_1_), channel_id=1, source_target_pairs={{0,8},{8,0},{16,24},{24,16},{1,9},{9,1},{17,25},{25,17},{2,10},{10... | collective-permute-start | bytes 1253384 | tf_op jit(solution)/shard_map/ppermute | solution.py:28
  27.4 9.0 %collective-permute-start.2 = (bf16[272,768]{1,0:T(8,128)(2,1)S(1)}, bf16[272,768]{1,0:T(8,128)(2,1)S(1)}, u32[]{:S(2)}, u32[]{:S(2)}) collective-permute-start(bf16[272,768]{1,0:T(8,128)(2,1)S(1)} %collective-permute-done.1.refs_3_), channel_id=1, source_target_pairs={{0,8},{8,0},{16,24},{24,16},{1,9},{9,1},{17,25},{25,17},{2,10},{10... | collective-permute-start | bytes 1253384 | tf_op jit(solution)/shard_map/ppermute | solution.py:28
  29.0 7.3 %collective-permute-start.8 = (bf16[288,640]{1,0:T(8,128)(2,1)S(1)}, bf16[288,640]{1,0:T(8,128)(2,1)S(1)}, u32[]{:S(2)}, u32[]{:S(2)}) collective-permute-start(bf16[288,640]{1,0:T(8,128)(2,1)S(1)} %pad_maximum_fusion.1), channel_id=1, source_target_pairs={{0,1},{1,0},{2,3},{3,2},{4,5},{5,4},{6,7},{7,6},{8,9},{9,8},{10,11... | collective-permute-start | bytes 1105928 | tf_op jit(solution)/shard_map/ppermute | solution.py:40
  29.0 19.9 %collective-permute-start.15 = (bf16[96,1152]{1,0:T(8,128)(2,1)S(1)}, bf16[96,1152]{1,0:T(8,128)(2,1)S(1)}, u32[]{:S(2)}, u32[]{:S(2)}) collective-permute-start(bf16[96,1152]{1,0:T(8,128)(2,1)S(1)} %copy-done.44), channel_id=1, source_target_pairs={{0,2},{1,3},{2,0},{3,1},{4,6},{5,7},{6,4},{7,5},{8,10},{9,11},{10,... | collective-permute-start | bytes 663560 | tf_op jit(solution)/shard_map/ppermute | solution.py:40
  30.4 18.6 %collective-permute-start.16 = (bf16[96,1152]{1,0:T(8,128)(2,1)S(1)}, bf16[96,1152]{1,0:T(8,128)(2,1)S(1)}, u32[]{:S(2)}, u32[]{:S(2)}) collective-permute-start(bf16[96,1152]{1,0:T(8,128)(2,1)S(1)} %copy-done.44), channel_id=1, source_target_pairs={{0,4},{1,5},{2,6},{3,7},{4,0},{5,1},{6,2},{7,3},{8,12},{9,13},{10,... | collective-permute-start | bytes 663560 | tf_op jit(solution)/shard_map/ppermute | solution.py:40
  30.5 26.1 %collective-permute-start.17 = (bf16[96,1152]{1,0:T(8,128)(2,1)S(1)}, bf16[96,1152]{1,0:T(8,128)(2,1)S(1)}, u32[]{:S(2)}, u32[]{:S(2)}) collective-permute-start(bf16[96,1152]{1,0:T(8,128)(2,1)S(1)} %copy-done.44), channel_id=1, source_target_pairs={{0,6},{1,7},{2,4},{3,5},{4,2},{5,3},{6,0},{7,1},{8,14},{9,15},{10,... | collective-permute-start | bytes 663560 | tf_op jit(solution)/shard_map/ppermute | solution.py:40
  36.3 33.5 %collective-permute-start.13 = (bf16[256,768]{1,0:T(8,128)(2,1)S(1)}, bf16[256,768]{1,0:T(8,128)(2,1)}, u32[]{:S(2)}, u32[]{:S(2)}) collective-permute-start(bf16[256,768]{1,0:T(8,128)(2,1)S(1)} %copy-done.20), channel_id=1, source_target_pairs={{0,16},{8,24},{16,0},{24,8},{1,17},{9,25},{17,1},{25,9},{2,18},{10... | collective-permute-start | bytes 1179656 | tf_op jit(solution)/shard_map/ppermute | solution.py:28
  48.1 22.3 %collective-permute-start.10 = (bf16[1024,192]{1,0:T(8,128)(2,1)}, bf16[1024,192]{1,0:T(8,128)(2,1)S(1)}, u32[]{:S(2)}, u32[]{:S(2)}) collective-permute-start(bf16[1024,192]{1,0:T(8,128)(2,1)} %get-tuple-element.112.refs_1_.attended_a), channel_id=1, source_target_pairs={{0,16},{8,24},{16,0},{24,8},{1,17},{9,25},{17,1},{25,9},{2,18},{10... | collective-permute-start | bytes 1179656 | tf_op jit(solution)/shard_map/ppermute | solution.py:28
  48.9 24.4 %copy-start.25 = (bf16[96,1152]{1,0:T(8,128)(2,1)}, bf16[96,1152]{1,0:T(8,128)(2,1)S(1)}, u32[]{:S(2)}) copy-start(bf16[96,1152]{1,0:T(8,128)(2,1)S(1)} %collective-permute-done.15.refs_11_) | copy-start | bytes 663556
  56.7 15.3 %collective-permute-start.18 = (bf16[288,1152]{1,0:T(8,128)(2,1)S(1)}, bf16[288,1152]{1,0:T(8,128)(2,1)S(1)}, u32[]{:S(2)}, u32[]{:S(2)}) collective-permute-start(bf16[288,1152]{1,0:T(8,128)(2,1)S(1)} %pad_maximum_fusion), channel_id=1, source_target_pairs={{0,1},{1,0},{2,3},{3,2},{4,5},{5,4},{6,7},{7,6},{8,9},{9,8},{10,11... | collective-permute-start | bytes 1990664 | tf_op jit(solution)/shard_map/ppermute | solution.py:40
  57.3 14.7 %collective-permute-start.12 = (bf16[256,768]{1,0:T(8,128)(2,1)S(1)}, bf16[256,768]{1,0:T(8,128)(2,1)}, u32[]{:S(2)}, u32[]{:S(2)}) collective-permute-start(bf16[256,768]{1,0:T(8,128)(2,1)S(1)} %copy-done.20), channel_id=1, source_target_pairs={{0,8},{8,0},{16,24},{24,16},{1,9},{9,1},{17,25},{25,17},{2,10},{10... | collective-permute-start | bytes 1179656 | tf_op jit(solution)/shard_map/ppermute | solution.py:28
  69.8 2.3 %collective-permute-start.14 = (bf16[256,768]{1,0:T(8,128)(2,1)}, bf16[256,768]{1,0:T(8,128)(2,1)}, u32[]{:S(2)}, u32[]{:S(2)}) collective-permute-start(bf16[256,768]{1,0:T(8,128)(2,1)} %collective-permute-done.13.refs_7_), channel_id=1, source_target_pairs={{0,8},{8,0},{16,24},{24,16},{1,9},{9,1},{17,25},{25,17},{2,10},{10... | collective-permute-start | bytes 1179656 | tf_op jit(solution)/shard_map/ppermute | solution.py:28
  69.9 2.8 %collective-permute-start.9 = (bf16[1024,192]{1,0:T(8,128)(2,1)S(1)}, bf16[1024,192]{1,0:T(8,128)(2,1)}, u32[]{:S(2)}, u32[]{:S(2)}) collective-permute-start(bf16[1024,192]{1,0:T(8,128)(2,1)S(1)} %copy-done.35), channel_id=1, source_target_pairs={{0,8},{8,0},{16,24},{24,16},{1,9},{9,1},{17,25},{25,17},{2,10},{10... | collective-permute-start | bytes 1179656 | tf_op jit(solution)/shard_map/ppermute | solution.py:28
  70.4 3.0 %collective-permute-start.11 = (bf16[1024,192]{1,0:T(8,128)(2,1)S(1)}, bf16[1024,192]{1,0:T(8,128)(2,1)}, u32[]{:S(2)}, u32[]{:S(2)}) collective-permute-start(bf16[1024,192]{1,0:T(8,128)(2,1)S(1)} %collective-permute-done.10.refs_3_.attended_c), channel_id=1, source_target_pairs={{0,8},{8,0},{16,24},{24,16},{1,9},{9,1},{17,25},{25,17},{2,10},{10... | collective-permute-start | bytes 1179656 | tf_op jit(solution)/shard_map/ppermute | solution.py:28
  90.6 8.7 %collective-permute-start.19 = (bf16[512,768]{1,0:T(8,128)(2,1)}, bf16[512,768]{1,0:T(8,128)(2,1)S(1)}, u32[]{:S(2)}, u32[]{:S(2)}) collective-permute-start(bf16[512,768]{1,0:T(8,128)(2,1)} %get-tuple-element.120), channel_id=1, source_target_pairs={{0,8},{8,0},{16,24},{24,16},{1,9},{9,1},{17,25},{25,17},{2,10},{10... | collective-permute-start | bytes 2359304 | tf_op jit(solution)/shard_map/ppermute | solution.py:28
  100.9 10.4 %collective-permute-start.20 = (bf16[256,768]{1,0:T(8,128)(2,1)S(1)}, bf16[256,768]{1,0:T(8,128)(2,1)S(1)}, u32[]{:S(2)}, u32[]{:S(2)}) collective-permute-start(bf16[256,768]{1,0:T(8,128)(2,1)S(1)} %add_convert_fusion.3), channel_id=1, source_target_pairs={{0,16},{8,24},{16,0},{24,8},{1,17},{9,25},{17,1},{25,9},{2,18},{10... | collective-permute-start | bytes 1179656 | tf_op jit(solution)/shard_map/ppermute | solution.py:28
  105.8 14.4 %collective-permute-start.24 = (bf16[384,768]{1,0:T(8,128)(2,1)}, bf16[384,768]{1,0:T(8,128)(2,1)S(1)}, u32[]{:S(2)}, u32[]{:S(2)}) collective-permute-start(bf16[384,768]{1,0:T(8,128)(2,1)} %get-tuple-element.138), channel_id=1, source_target_pairs={{0,1},{1,0},{2,3},{3,2},{4,5},{5,4},{6,7},{7,6},{8,9},{9,8},{10,11... | collective-permute-start | bytes 1769480 | tf_op jit(solution)/shard_map/ppermute | solution.py:40
  115.6 9.6 %collective-permute-start.22 = (bf16[256,768]{1,0:T(8,128)(2,1)}, bf16[256,768]{1,0:T(8,128)(2,1)S(1)}, u32[]{:S(2)}, u32[]{:S(2)}) collective-permute-start(bf16[256,768]{1,0:T(8,128)(2,1)} %get-tuple-element.123.branch_a), channel_id=1, source_target_pairs={{0,16},{8,24},{16,0},{24,8},{1,17},{9,25},{17,1},{25,9},{2,18},{10... | collective-permute-start | bytes 1179656 | tf_op jit(solution)/shard_map/ppermute | solution.py:28
  115.9 24.3 %collective-permute-start.21 = (bf16[256,768]{1,0:T(8,128)(2,1)}, bf16[256,768]{1,0:T(8,128)(2,1)S(1)}, u32[]{:S(2)}, u32[]{:S(2)}) collective-permute-start(bf16[256,768]{1,0:T(8,128)(2,1)} %get-tuple-element.123.branch_a), channel_id=1, source_target_pairs={{0,8},{8,0},{16,24},{24,16},{1,9},{9,1},{17,25},{25,17},{2,10},{10... | collective-permute-start | bytes 1179656 | tf_op jit(solution)/shard_map/ppermute | solution.py:28
  125.2 16.0 %collective-permute-start.23 = (bf16[256,768]{1,0:T(8,128)(2,1)S(1)}, bf16[256,768]{1,0:T(8,128)(2,1)S(1)}, u32[]{:S(2)}, u32[]{:S(2)}) collective-permute-start(bf16[256,768]{1,0:T(8,128)(2,1)S(1)} %collective-permute-done.22.branch_c), channel_id=1, source_target_pairs={{0,8},{8,0},{16,24},{24,16},{1,9},{9,1},{17,25},{25,17},{2,10},{10... | collective-permute-start | bytes 1179656 | tf_op jit(solution)/shard_map/ppermute | solution.py:28
  137.5 23.8 %collective-permute-start.25 = (bf16[96,768]{1,0:T(8,128)(2,1)S(1)}, bf16[96,768]{1,0:T(8,128)(2,1)S(1)}, u32[]{:S(2)}, u32[]{:S(2)}) collective-permute-start(bf16[96,768]{1,0:T(8,128)(2,1)S(1)} %copy-done.48), channel_id=1, source_target_pairs={{0,2},{1,3},{2,0},{3,1},{4,6},{5,7},{6,4},{7,5},{8,10},{9,11},{10,... | collective-permute-start | bytes 442376 | tf_op jit(solution)/shard_map/ppermute | solution.py:40
  137.5 23.8 %collective-permute-start.26 = (bf16[96,768]{1,0:T(8,128)(2,1)S(1)}, bf16[96,768]{1,0:T(8,128)(2,1)S(1)}, u32[]{:S(2)}, u32[]{:S(2)}) collective-permute-start(bf16[96,768]{1,0:T(8,128)(2,1)S(1)} %copy-done.47), channel_id=1, source_target_pairs={{0,4},{1,5},{2,6},{3,7},{4,0},{5,1},{6,2},{7,3},{8,12},{9,13},{10,... | collective-permute-start | bytes 442376 | tf_op jit(solution)/shard_map/ppermute | solution.py:40
  139.7 21.6 %collective-permute-start.27 = (bf16[96,768]{1,0:T(8,128)(2,1)S(1)}, bf16[96,768]{1,0:T(8,128)(2,1)S(1)}, u32[]{:S(2)}, u32[]{:S(2)}) collective-permute-start(bf16[96,768]{1,0:T(8,128)(2,1)S(1)} %copy-done.46), channel_id=1, source_target_pairs={{0,6},{1,7},{2,4},{3,5},{4,2},{5,3},{6,0},{7,1},{8,14},{9,15},{10,... | collective-permute-start | bytes 442376 | tf_op jit(solution)/shard_map/ppermute | solution.py:40
  140.2 23.9 %collective-permute-start.37 = (bf16[384,768]{1,0:T(8,128)(2,1)}, bf16[384,768]{1,0:T(8,128)(2,1)S(1)}, u32[]{:S(2)}, u32[]{:S(2)}) collective-permute-start(bf16[384,768]{1,0:T(8,128)(2,1)} %get-tuple-element.173), channel_id=1, source_target_pairs={{0,1},{1,0},{2,3},{3,2},{4,5},{5,4},{6,7},{7,6},{8,9},{9,8},{10,11... | collective-permute-start | bytes 1769480 | tf_op jit(solution)/shard_map/ppermute | solution.py:40
  141.3 21.6 %collective-permute-start.34 = (bf16[512,768]{1,0:T(8,128)(2,1)}, bf16[512,768]{1,0:T(8,128)(2,1)S(1)}, u32[]{:S(2)}, u32[]{:S(2)}) collective-permute-start(bf16[512,768]{1,0:T(8,128)(2,1)} %get-tuple-element.159), channel_id=1, source_target_pairs={{0,8},{8,0},{16,24},{24,16},{1,9},{9,1},{17,25},{25,17},{2,10},{10... | collective-permute-start | bytes 2359304 | tf_op jit(solution)/shard_map/ppermute | solution.py:28
  161.4 16.5 %collective-permute-start.28 = (bf16[384,896]{1,0:T(8,128)(2,1)}, bf16[384,896]{1,0:T(8,128)(2,1)S(1)}, u32[]{:S(2)}, u32[]{:S(2)}) collective-permute-start(bf16[384,896]{1,0:T(8,128)(2,1)} %get-tuple-element.149), channel_id=1, source_target_pairs={{0,1},{1,0},{2,3},{3,2},{4,5},{5,4},{6,7},{7,6},{8,9},{9,8},{10,11... | collective-permute-start | bytes 2064392 | tf_op jit(solution)/shard_map/ppermute | solution.py:40
  161.8 24.3 %collective-permute-start.32 = (bf16[512,768]{1,0:T(8,128)(2,1)}, bf16[512,768]{1,0:T(8,128)(2,1)S(1)}, u32[]{:S(2)}, u32[]{:S(2)}) collective-permute-start(bf16[512,768]{1,0:T(8,128)(2,1)} %get-tuple-element.154), channel_id=1, source_target_pairs={{0,8},{8,0},{16,24},{24,16},{1,9},{9,1},{17,25},{25,17},{2,10},{10... | collective-permute-start | bytes 2359304 | tf_op jit(solution)/shard_map/ppermute | solution.py:28
  162.9 10.8 %collective-permute-start.35 = (bf16[256,768]{1,0:T(8,128)(2,1)S(1)}, bf16[256,768]{1,0:T(8,128)(2,1)S(1)}, u32[]{:S(2)}, u32[]{:S(2)}) collective-permute-start(bf16[256,768]{1,0:T(8,128)(2,1)S(1)} %add_convert_fusion.1), channel_id=1, source_target_pairs={{0,16},{8,24},{16,0},{24,8},{1,17},{9,25},{17,1},{25,9},{2,18},{10... | collective-permute-start | bytes 1179656 | tf_op jit(solution)/shard_map/ppermute | solution.py:28
  167.1 13.9 %collective-permute-start.38 = (bf16[96,768]{1,0:T(8,128)(2,1)}, bf16[96,768]{1,0:T(8,128)(2,1)S(1)}, u32[]{:S(2)}, u32[]{:S(2)}) collective-permute-start(bf16[96,768]{1,0:T(8,128)(2,1)} %get-tuple-element.174), channel_id=1, source_target_pairs={{0,2},{1,3},{2,0},{3,1},{4,6},{5,7},{6,4},{7,5},{8,10},{9,11},{10,... | collective-permute-start | bytes 442376 | tf_op jit(solution)/shard_map/ppermute | solution.py:40
  167.8 13.2 %collective-permute-start.39 = (bf16[96,768]{1,0:T(8,128)(2,1)}, bf16[96,768]{1,0:T(8,128)(2,1)S(1)}, u32[]{:S(2)}, u32[]{:S(2)}) collective-permute-start(bf16[96,768]{1,0:T(8,128)(2,1)} %get-tuple-element.175), channel_id=1, source_target_pairs={{0,4},{1,5},{2,6},{3,7},{4,0},{5,1},{6,2},{7,3},{8,12},{9,13},{10,... | collective-permute-start | bytes 442376 | tf_op jit(solution)/shard_map/ppermute | solution.py:40
  173.7 9.8 %collective-permute-start.40 = (bf16[96,768]{1,0:T(8,128)(2,1)}, bf16[96,768]{1,0:T(8,128)(2,1)S(1)}, u32[]{:S(2)}, u32[]{:S(2)}) collective-permute-start(bf16[96,768]{1,0:T(8,128)(2,1)} %get-tuple-element.176), channel_id=1, source_target_pairs={{0,6},{1,7},{2,4},{3,5},{4,2},{5,3},{6,0},{7,1},{8,14},{9,15},{10,... | collective-permute-start | bytes 442376 | tf_op jit(solution)/shard_map/ppermute | solution.py:40
  183.5 16.1 %collective-permute-start.29 = (bf16[96,896]{1,0:T(8,128)(2,1)}, bf16[96,896]{1,0:T(8,128)(2,1)S(1)}, u32[]{:S(2)}, u32[]{:S(2)}) collective-permute-start(bf16[96,896]{1,0:T(8,128)(2,1)} %get-tuple-element.150), channel_id=1, source_target_pairs={{0,2},{1,3},{2,0},{3,1},{4,6},{5,7},{6,4},{7,5},{8,10},{9,11},{10,... | collective-permute-start | bytes 516104 | tf_op jit(solution)/shard_map/ppermute | solution.py:40
  183.5 16.1 %collective-permute-start.30 = (bf16[96,896]{1,0:T(8,128)(2,1)}, bf16[96,896]{1,0:T(8,128)(2,1)S(1)}, u32[]{:S(2)}, u32[]{:S(2)}) collective-permute-start(bf16[96,896]{1,0:T(8,128)(2,1)} %get-tuple-element.151), channel_id=1, source_target_pairs={{0,4},{1,5},{2,6},{3,7},{4,0},{5,1},{6,2},{7,3},{8,12},{9,13},{10,... | collective-permute-start | bytes 516104 | tf_op jit(solution)/shard_map/ppermute | solution.py:40
  185.2 15.9 %collective-permute-start.31 = (bf16[96,896]{1,0:T(8,128)(2,1)}, bf16[96,896]{1,0:T(8,128)(2,1)S(1)}, u32[]{:S(2)}, u32[]{:S(2)}) collective-permute-start(bf16[96,896]{1,0:T(8,128)(2,1)} %get-tuple-element.152), channel_id=1, source_target_pairs={{0,6},{1,7},{2,4},{3,5},{4,2},{5,3},{6,0},{7,1},{8,14},{9,15},{10,... | collective-permute-start | bytes 516104 | tf_op jit(solution)/shard_map/ppermute | solution.py:40
  186.2 9.1 %collective-permute-start.33 = (bf16[256,768]{1,0:T(8,128)(2,1)S(1)}, bf16[256,768]{1,0:T(8,128)(2,1)S(1)}, u32[]{:S(2)}, u32[]{:S(2)}) collective-permute-start(bf16[256,768]{1,0:T(8,128)(2,1)S(1)} %add_convert_fusion.2), channel_id=1, source_target_pairs={{0,16},{8,24},{16,0},{24,8},{1,17},{9,25},{17,1},{25,9},{2,18},{10... | collective-permute-start | bytes 1179656 | tf_op jit(solution)/shard_map/ppermute | solution.py:28
  187.7 18.2 %collective-permute-start.42 = (bf16[96,1536]{1,0:T(8,128)(2,1)S(1)}, bf16[96,1536]{1,0:T(8,128)(2,1)S(1)}, u32[]{:S(2)}, u32[]{:S(2)}) collective-permute-start(bf16[96,1536]{1,0:T(8,128)(2,1)S(1)} %pad_maximum_fusion.2.refs_0_), channel_id=1, source_target_pairs={{0,16},{8,24},{16,0},{24,8},{1,17},{9,25},{17,1},{25,9},{2,18},{10... | collective-permute-start | bytes 884744 | tf_op jit(solution)/shard_map/ppermute | solution.py:28
  201.2 5.1 %collective-permute-start.44 = (bf16[96,896]{1,0:T(8,128)(2,1)S(1)}, bf16[96,896]{1,0:T(8,128)(2,1)S(1)}, u32[]{:S(2)}, u32[]{:S(2)}) collective-permute-start(bf16[96,896]{1,0:T(8,128)(2,1)S(1)} %add_convert_fusion.4.refs_0_), channel_id=1, source_target_pairs={{0,16},{8,24},{16,0},{24,8},{1,17},{9,25},{17,1},{25,9},{2,18},{10... | collective-permute-start | bytes 516104 | tf_op jit(solution)/shard_map/ppermute | solution.py:28
  202.4 7.4 %collective-permute-start.41 = (bf16[96,1536]{1,0:T(8,128)(2,1)S(1)}, bf16[96,1536]{1,0:T(8,128)(2,1)S(1)}, u32[]{:S(2)}, u32[]{:S(2)}) collective-permute-start(bf16[96,1536]{1,0:T(8,128)(2,1)S(1)} %pad_maximum_fusion.2.refs_0_), channel_id=1, source_target_pairs={{0,8},{8,0},{16,24},{24,16},{1,9},{9,1},{17,25},{25,17},{2,10},{10... | collective-permute-start | bytes 884744 | tf_op jit(solution)/shard_map/ppermute | solution.py:28
  205.9 4.0 %collective-permute-start.43 = (bf16[96,1536]{1,0:T(8,128)(2,1)S(1)}, bf16[96,1536]{1,0:T(8,128)(2,1)S(1)}, u32[]{:S(2)}, u32[]{:S(2)}) collective-permute-start(bf16[96,1536]{1,0:T(8,128)(2,1)S(1)} %collective-permute-done.42.refs_2_), channel_id=1, source_target_pairs={{0,8},{8,0},{16,24},{24,16},{1,9},{9,1},{17,25},{25,17},{2,10},{10... | collective-permute-start | bytes 884744 | tf_op jit(solution)/shard_map/ppermute | solution.py:28
  205.9 10.7 %collective-permute-start.36 = (bf16[96,896]{1,0:T(8,128)(2,1)S(1)}, bf16[96,896]{1,0:T(8,128)(2,1)S(1)}, u32[]{:S(2)}, u32[]{:S(2)}) collective-permute-start(bf16[96,896]{1,0:T(8,128)(2,1)S(1)} %add_convert_fusion.4.refs_0_), channel_id=1, source_target_pairs={{0,8},{8,0},{16,24},{24,16},{1,9},{9,1},{17,25},{25,17},{2,10},{10... | collective-permute-start | bytes 516104 | tf_op jit(solution)/shard_map/ppermute | solution.py:28
  206.4 10.2 %collective-permute-start.45 = (bf16[96,896]{1,0:T(8,128)(2,1)S(1)}, bf16[96,896]{1,0:T(8,128)(2,1)S(1)}, u32[]{:S(2)}, u32[]{:S(2)}) collective-permute-start(bf16[96,896]{1,0:T(8,128)(2,1)S(1)} %collective-permute-done.44.refs_2_), channel_id=1, source_target_pairs={{0,8},{8,0},{16,24},{24,16},{1,9},{9,1},{17,25},{25,17},{2,10},{10... | collective-permute-start | bytes 516104 | tf_op jit(solution)/shard_map/ppermute | solution.py:28
  (50 other events, 458.0 us)
Sparse Core Ops, SparseCore 0:
  12.5 54.1 all-gather.1

commit v3 on v2

--- a/solution.py
+++ b/solution.py
@@ -28,9 +28,9 @@
     return lax.ppermute(block, "rep", [(i, i ^ bit) for i in range(SPAN)])
 
 
-def rep_blocks(block, gate=None):
+def rep_blocks(block, gate=None, near_gate=None):
     far = swapped(block, 2)
-    near = swapped(block, 1)
+    near = swapped(block if near_gate is None else after(block, near_gate), 1)
     if gate is not None:
         far = after(far, gate)
     return (block, near, far, swapped(far, 1))
@@ -307,22 +307,10 @@
     return store
 
 
-def prep_kernel(
-    place_ref,
-    qkv_ref,
-    out_ref,
-    up_ref,
-    down_ref,
-    small_ref,
-    first_ref,
-    second_ref,
-    third_ref,
-    small_rows,
-):
+def first_prep_kernel(place_ref, qkv_ref, small_ref, first_ref, small_rows):
     rep = place_ref[0]
-    owned, width = out_ref.shape
-    part, half = width // SPAN, width // 2
-    units = third_ref.shape[0]
+    owned, width = qkv_ref.shape[0], qkv_ref.shape[1] // 3
+    part = width // SPAN
     small_rows[...] = jnp.zeros_like(small_rows)
     small_rows[: small_ref.shape[0], : small_ref.shape[1]] = small_ref[...]
     for which in range(3):
@@ -330,15 +318,21 @@
         options = [qkv_ref[:, first + r * part : first + (r + 1) * part] for r in range(SPAN)]
         first_ref[:, which * part : (which + 1) * part] = chosen(options, rep).astype(BF16)
     first_ref[:, 3 * part :] = small_rows[...].T[:owned, :64].astype(BF16)
-    second_ref[:, :half] = out_ref[:, :half].astype(BF16)
+
+
+def second_prep_kernel(place_ref, out_ref, up_ref, down_ref, second_ref, third_ref):
+    rep = place_ref[0]
+    cut = out_ref.shape[1] // 3
+    units = third_ref.shape[0]
+    second_ref[:, :cut] = out_ref[:, :cut].astype(BF16)
     pieces = []
     for first in range(0, up_ref.shape[1], SPAN * units):
         options = [up_ref[:, first + r * units : first + (r + 1) * units] for r in range(SPAN)]
         pieces.append(chosen(options, rep))
-    second_ref[:, half:] = jnp.concatenate(pieces, axis=1).astype(BF16)
-    third_ref[:, :half] = out_ref[:, half:].astype(BF16)
+    second_ref[:, cut:] = jnp.concatenate(pieces, axis=1).astype(BF16)
+    third_ref[:, : 2 * cut] = out_ref[:, cut:].astype(BF16)
     start = pl.multiple_of(rep * units, units)
-    third_ref[:, half:] = down_ref[pl.ds(start, units), :].astype(BF16)
+    third_ref[:, 2 * cut :] = down_ref[pl.ds(start, units), :].astype(BF16)
 
 
 def first_kernel(pieces, *refs):
@@ -401,8 +395,7 @@
         all_ref,
         small_ref,
         up_bias_ref,
-        out_weight,
-        cot_ref,
+        out_own_ref,
         hidden_ref,
         act_ref,
         pre_ref,
@@ -411,15 +404,19 @@
         far_ref,
         own_ref,
         up_weight,
+        out_weight,
+        cot_ref,
     ) = refs
     rep = place_ref[0]
     total, width = all_ref.shape
     rows = total // SPAN
     part = attended_refs[0].shape[1]
-    half = width // 2
-    pieces.place(place_ref[1], piece_refs, place_store(up_weight, slice(half, None)))
-    pieces.place(place_ref[1], piece_refs, place_store(out_weight, slice(0, half), half))
-    out_weight[:, half:] = wide_ref[:, :half]
+    cut = width // 3
+    pieces.place(place_ref[1], piece_refs, place_store(up_weight, slice(cut, None)))
+    pieces.place(place_ref[1], piece_refs, place_store(out_weight, slice(0, cut), cut))
+    out_weight[:, cut:] = wide_ref[:, : 2 * cut]
+    own_rows = pl.ds(pl.multiple_of(rep * part, part), part)
+    out_own_ref[...] = out_weight[own_rows, :]
     for at in range(SPAN):
         cot_ref[pl.ds(pl.multiple_of((rep ^ at) * rows, rows), rows), :] = cot_refs[at][...]
     out_bias, gain, bias = small_ref[4:5, :], small_ref[5:6, :], small_ref[6:7, :]
@@ -443,14 +440,18 @@
         cdf = 0.5 * (1.0 + lax.erf(pre_act * (0.5**0.5)))
         act_ref[block, :] = (pre_act * cdf).astype(BF16)
         slope = cdf + pre_act * (jnp.exp(-0.5 * pre_act * pre_act) * 0.3989422804014327)
-        pre_low = (contract_cols(cot_ref[block, :], wide_ref[:, half:]) * slope).astype(BF16)
+        pre_low = (contract_cols(cot_ref[block, :], wide_ref[:, 2 * cut :]) * slope).astype(BF16)
         pre_ref[block, :] = pre_low
         grad = contract_cols(pre_low, up_weight[...])
         send_parts(grad, index ^ rep, near_ref, far_ref, own_ref)
 
 
-def down_grad_kernel(place_ref, act_ref, cot_ref, *refs):
-    grad_refs, grad_ref = refs[:-1], refs[-1]
+def down_grad_kernel(place_ref, act_ref, cot_a, cot_b, cot_c, cot_d, *refs):
+    grad_refs, (grad_ref, cot_ref) = refs[:-2], refs[-2:]
+    rows = cot_a.shape[0]
+    for at, ref in enumerate((cot_a, cot_b, cot_c, cot_d)):
+        start = pl.multiple_of((place_ref[0] ^ at) * rows, rows)
+        cot_ref[pl.ds(start, rows), :] = ref[...]
     units = act_ref.shape[1]
     step = units // 3
     for first in range(0, units, step):
@@ -558,11 +559,10 @@
     total, width = all_ref.shape
     rows = total // SPAN
     part = q_ref.shape[1]
-    own_rows = pl.ds(pl.multiple_of(rep * part, part), part)
     for at, ref in enumerate((branch_a, branch_b, branch_c, branch_d)):
         start = pl.multiple_of((rep ^ at) * rows, rows)
         branch_ref[pl.ds(start, rows), :] = ref[...]
-    back_ref[...] = contract_cols(branch_ref[...], out_weight[own_rows, :]).astype(BF16)
+    back_ref[...] = contract_cols(branch_ref[...], out_weight[...]).astype(BF16)
     attend_back(
         q_ref,
         k_ref,
@@ -640,20 +640,51 @@
 
 def adam_kernel(place_ref, *refs):
     blocks = rep_order(refs[:SPAN], place_ref[0])
-    ins, outs = refs[SPAN : SPAN + 9], refs[SPAN + 9 :]
+    small_refs, refs = refs[SPAN : 2 * SPAN], refs[2 * SPAN :]
+    ins, outs = refs[:9], refs[9:]
     part = ins[3].shape[1] // SPAN
     qkv = [b[:, c * part : (c + 1) * part] for c in range(3) for b in blocks]
     out = [b[:, 3 * part : 4 * part] for b in blocks]
-    small = blocks[0][:, 4 * part :]
-    for block in blocks[1:]:
-        small = small + block[:, 4 * part :]
-    small = small.T[: ins[6].shape[0], :]
-    grads = (jnp.concatenate(qkv, axis=1), jnp.concatenate(out, axis=1), small)
-    for at, (gradient, rate) in enumerate(zip(grads, (RATE_MATRIX, RATE_MATRIX, RATE_SMALL))):
+
+    def update(at, gradient, rate):
         weight, first, second = (ref[...] for ref in ins[3 * at : 3 * at + 3])
         results = adam_update(weight, gradient, first, second, rate)
         for ref, value in zip(outs[3 * at : 3 * at + 3], results):
             ref[...] = value
+
+    update(0, jnp.concatenate(qkv, axis=1), RATE_MATRIX)
+    update(1, jnp.concatenate(out, axis=1), RATE_MATRIX)
+
+    @pl.when(pl.program_id(0) == 0)
+    def _():
+        small = small_refs[0][...].astype(F32)
+        for ref in small_refs[1:]:
+            small = small + ref[...].astype(F32)
+        update(2, small.T[: ins[6].shape[0], :], RATE_SMALL)
+
+
+def last_adam(place, blocks, arrays):
+    steps = 3
+    rows, columns = arrays[0].shape
+    width = arrays[3].shape[1]
+
+    def row_block(count):
+        return pl.BlockSpec((rows // steps, count), lambda i: (i, 0))
+
+    whole = pl.BlockSpec(arrays[6].shape, lambda i: (0, 0))
+    specs = [row_block(columns)] * 3 + [row_block(width)] * 3 + [whole] * 3
+    small = pl.BlockSpec((rows, 128), lambda i: (0, width // 128))
+    return pl.pallas_call(
+        adam_kernel,
+        grid=(steps,),
+        out_shape=[shape(*a.shape, dtype=F32) for a in arrays],
+        in_specs=[pl.BlockSpec(memory_space=pltpu.SMEM)]
+        + [row_block(width)] * SPAN
+        + [small] * SPAN
+        + specs,
+        out_specs=specs,
+        compiler_params=pltpu.CompilerParams(vmem_limit_bytes=16 * 2**20),
+    )(place, *blocks, *blocks, *arrays)
 
 
 def up_adam_kernel(place_ref, *refs):
@@ -744,24 +775,28 @@
         return lax.dynamic_slice_in_dim(block, rep * size, size, axis)
 
     few = shards == FEW
-    half = width // 2
+    third = width // 3
     if few:
-        first_send, second_send, third_send = call(
-            prep_kernel,
-            [
-                shape(owned, 3 * part + 64),
-                shape(owned, half + ff_part),
-                shape(units, half + width),
-            ],
+        first_send = call(
+            first_prep_kernel,
+            [shape(owned, 3 * part + 64)],
             [pltpu.VMEM((128, 128), F32)],
             owned * width,
             56,
             place,
             qkv_weight,
+            small_weights,
+        )[0]
+        second_send, third_send = call(
+            second_prep_kernel,
+            [shape(owned, third + ff_part), shape(units, 2 * third + width)],
+            [],
+            owned * width,
+            56,
+            place,
             out_weight,
             up_weight,
             down_weight,
-            small_weights,
         )
     else:
         low_small = small_weights.astype(BF16).T
@@ -772,8 +807,8 @@
         low_up = rep_part(up_weight.astype(BF16).reshape(owned, shards, SPAN, units), 1, 2)
         low_down = rep_part(down_weight, units, 0).astype(BF16)
         low_out = out_weight.astype(BF16)
-        second_send = jnp.concatenate([low_out[:, :half], low_up.reshape(owned, -1)], axis=1)
-        third_send = jnp.concatenate([low_out[:, half:], low_down], axis=1)
+        second_send = jnp.concatenate([low_out[:, :third], low_up.reshape(owned, -1)], axis=1)
+        third_send = jnp.concatenate([low_out[:, third:], low_down], axis=1)
     third_full = lax.all_gather(third_send, "shard", axis=0, tiled=True)
     first_pieces, second_pieces = shard_gather(first_send, second_send)
 
@@ -817,8 +852,7 @@
     up_bias = rep_part(small[8:12].reshape(shards, SPAN, units), 1, 1).reshape(1, -1)
     attended_blocks = rep_blocks(attended)
     (
-        out_part,
-        all_cot,
+        out_own,
         hidden_two,
         act_low,
         pre_low,
@@ -829,8 +863,7 @@
     ) = call(
         lambda *refs: second_kernel(second_pieces, *refs),
         [
-            shape(width, width),
-            shape(total, width),
+            shape(part, width),
             shape(total, width),
             shape(total, ff_part),
             shape(total, ff_part),
@@ -839,7 +872,11 @@
             shape(rows, width, dtype=F32),
             shape(rows, width, dtype=F32),
         ],
-        [pltpu.VMEM((width, ff_part), BF16)],
+        [
+            pltpu.VMEM((width, ff_part), BF16),
+            pltpu.VMEM((width, width), BF16),
+            pltpu.VMEM((total, width), BF16),
+        ],
         32 * total * width * width,
         56,
         place,
@@ -856,15 +893,35 @@
     down_grad = call(
         down_grad_kernel,
         [shape(ff_part // 2, width)] * 2 * few + [shape(ff_part, width)] * (not few),
-        [pltpu.VMEM((ff_part, width), BF16)],
+        [pltpu.VMEM((ff_part, width), BF16), pltpu.VMEM((total, width), BF16)],
         6 * total * width * width,
         56,
         place,
         after(act_low, far_send),
-        all_cot,
+        *cot_blocks,
+    )
+    *up_grad, mixed_near, mixed_far, mixed_own, unit_sums = call(
+        third_kernel,
+        [shape(width // 2, ff_part)] * 2 * few
+        + [shape(width, ff_part)] * (not few)
+        + [
+            shape(2 * rows, width),
+            shape(rows, width, dtype=F32),
+            shape(rows, width, dtype=F32),
+            shape(8, ff_part, dtype=F32),
+        ],
+        [pltpu.VMEM((width, ff_part), BF16)],
+        12 * total * width * width,
+        56,
+        place,
+        after(act_low, down_grad[0]),
+        hidden_two,
+        pre_low,
+        third_full,
     )
     if few:
         down_received = swap_shard(down_grad[1], 1)
+    near, unit_sums = lax.optimization_barrier((near, unit_sums))
     hidden_two_terms = own, near, far
     resid_grad, branch, sums = call(
         fourth_kernel,
@@ -882,33 +939,11 @@
         cotangent,
         small,
     )
-    branch_blocks = rep_blocks(branch)
-    gate = down_grad[0]
+    branch_blocks = rep_blocks(branch, None, down_received if few else None)
     if few:
         down_own, down_received = scatter_high(place, after(down_grad[0], branch), down_received)
-        gate = down_own
-    *up_grad, mixed_near, mixed_far, mixed_own, unit_sums = call(
-        third_kernel,
-        [shape(width // 2, ff_part)] * 2 * few
-        + [shape(width, ff_part)] * (not few)
-        + [
-            shape(2 * rows, width),
-            shape(rows, width, dtype=F32),
-            shape(rows, width, dtype=F32),
-            shape(8, ff_part, dtype=F32),
-        ],
-        [pltpu.VMEM((width, ff_part), BF16)],
-        12 * total * width * width,
-        56,
-        place,
-        after(act_low, gate),
-        hidden_two,
-        pre_low,
-        third_full,
-    )
-    if few:
+        branch_blocks = (after(branch, down_own),) + branch_blocks[1:]
         up_received = swap_shard(up_grad[1], 1)
-    near_mixed, far_mixed, _ = rep_sum(after(mixed_near, branch), mixed_far, branch_blocks[2])
     unit_rows = lax.dynamic_update_slice(
         jnp.zeros((shards, SPAN, units), F32), unit_sums[0].reshape(shards, 1, units), (0, rep, 0)
     ).reshape(ff // width, width)
@@ -937,7 +972,7 @@
         place,
         *branch_blocks,
         *attended_blocks,
-        out_part,
+        out_own,
         qkv_part,
         queries,
         keys,
@@ -950,11 +985,17 @@
         sums,
         unit_rows,
     )
-    near, far, far_send = rep_sum(near_send, far_part)
     if few:
         last_kept, last_sent = last_grad
-        last_sent, down_received = lax.optimization_barrier((last_sent, down_received))
+        last_sent, near_send, down_received, up_received = lax.optimization_barrier(
+            (last_sent, near_send, down_received, up_received)
+        )
+    near, far, _ = rep_sum(near_send, far_part)
+    near_mixed, far_mixed, _ = rep_sum(mixed_near, mixed_far, far)
+    if few:
+        last_kept, far = lax.optimization_barrier((last_kept, far))
         last_own, last_received = scatter_middle(place, last_kept, last_sent)
+        far_mixed = after(far_mixed, last_own)
         up_own, up_received = scatter_high(
             place, after(up_grad[0], (last_grad[0], down_received)), up_received
         )
@@ -1007,29 +1048,21 @@
             (last_received, input_grad, mixed)
         )
         last_total = scatter_end(last_own, last_received)
-        last_blocks = rep_blocks(last_total)
-        last_near, up_res[0], down_res[0] = lax.optimization_barrier(
-            (last_blocks[1], up_res[0], down_res[0])
-        )
-        last_blocks = (last_blocks[0], last_near) + last_blocks[2:]
-        results = call(
-            adam_kernel,
-            [shape(*ref.shape, dtype=F32) for ref in (qkv_weight, out_weight, small_weights)
-             for _ in range(3)],
-            [],
-            20 * qkv_weight.size,
-            56,
+        last_blocks = rep_blocks(last_total, (up_res[0], down_res[0]))
+        results = last_adam(
             place,
-            *last_blocks,
-            qkv_weight,
-            qkv_first,
-            qkv_second,
-            out_weight,
-            out_first,
-            out_second,
-            small_weights,
-            small_first,
-            small_second,
+            last_blocks,
+            (
+                qkv_weight,
+                qkv_first,
+                qkv_second,
+                out_weight,
+                out_first,
+                out_second,
+                small_weights,
+                small_first,
+                small_second,
+            ),
         )
         qkv_res, out_res, small_res = results[:3], results[3:6], results[6:]
     else:

time: 233 us -> 222 us (0.953); the launches traced: 230 us -> 221 us
  local copies, waits for them, and re-layouts: 11.7 us -> 8.17 us
  waiting for transfers between devices: 48.7 us -> 45.8 us
    pallas_call x12, Pallas kernels: 82.5 us -> 77.3 us  [call(): pl.pallas_call(kernel, out_shape=tuple(outs), in_specs=[pl.BlockSpec(memo...]
    ppermute x24, waiting for transfers between devices: 21.5 us -> 17.4 us  [swapped(): return lax.ppermute(block, 'rep', [(i, i ^ bit) for i in range(SPAN)])]
    pallas_call x0 -> x1, Pallas kernels: none -> 3.51 us  [last_adam(): pl.pallas_call(adam_kernel, grid=(steps,), out_shape=[shape(*a.shape, dty...]
    unnamed x102 -> x112, local copies, waits for them, and re-layouts: 7.56 us -> 4.1 us
    ppermute x24, starting transfers between devices: 44 us -> 40.8 us  [swapped(): return lax.ppermute(block, 'rep', [(i, i ^ bit) for i in range(SPAN)])]
  transfers between devices with their start and end apart: 47 -> 47, of which waited for: 17 -> 16; matrix products, arithmetic and copies ran while one was open for 2% -> 3% of each run, Pallas kernels for 27% -> 29%
where the time goes in v3:
time: 222 us; the launch traced here: 221 us
  Pallas kernels  87.5 us (39%)
  starting transfers between devices  60.3 us (27%)
  waiting for transfers between devices  45.8 us (21%)
  between operations  14.8 us (7%)
  local copies, waits for them, and re-layouts  8.17 us (4%)
  other arithmetic  4.91 us (2%)
    pallas_call x12, Pallas kernels, call(): pl.pallas_call(kernel, out_shape=tuple(outs), in_specs=[pl.BlockSpec(memo...  77.3 us
    ppermute x24, starting transfers between devices, swapped(): return lax.ppermute(block, 'rep', [(i, i ^ bit) for i in range(SPAN)])  40.8 us
    ppermute x22, waiting for transfers between devices, swap_shard(): lax.ppermute(block, 'shard', [(i, i ^ bits) for i in range(lax.axis_size(...  28.4 us
    ppermute x22, starting transfers between devices, swap_shard(): lax.ppermute(block, 'shard', [(i, i ^ bits) for i in range(lax.axis_size(...  19.5 us
    ppermute x24, waiting for transfers between devices, swapped(): return lax.ppermute(block, 'rep', [(i, i ^ bit) for i in range(SPAN)])  17.4 us
    pallas_call x2, Pallas kernels, grid_adam(): pl.pallas_call(kernel, grid=(steps,), out_shape=[shape(rows, columns, dty...  6.65 us
  transfers between devices with their start and end apart: 47, of which 16 were waited for; matrix products, arithmetic and copies ran while one was open for 3% of the time, Pallas kernels for 29%

profile of v3, /device:TPU:11, one launch (start us, length us, event | category | flops | bytes accessed | tf_op | source)
XLA Modules:
  0.0 221.4 jit_solution(14853775321644313853)
XLA Ops:
  7.8 3.4 %shard_map.306 = (bf16[96,1024]{1,0:T(8,128)(2,1)}, bf16[96,1280]{1,0:T(8,128)(2,1)}) custom-call(s32[2]{0:T(128)} %pad_add_fusion.place_ref.refs_0_, f32[96,768]{1,0:T(8,128)} %refs_11_.1, f32[96,3072]{1,0:T(8,128)} %refs_4_.2, f32[384,768]{1,0:T(8,128)} %refs_4_.3), custom_call_target="tpu_custom_call" | custom-call | flops 73728 | bytes 3096584 | tf_op jit(solution)/shard_map/pallas_call | solution.py:257
  11.3 1.3 collective-permute-start.1
  12.6 2.3 %shard_map.305.refs_5_ = bf16[96,640]{1,0:T(8,128)(2,1)} custom-call(s32[2]{0:T(128)} %pad_add_fusion.place_ref.refs_0_, f32[96,2304]{1,0:T(8,128)} %refs_8_.1, f32[12,96]{1,0:T(8,128)} %refs_14_.1), custom_call_target="tpu_custom_call" | custom-call | flops 73728 | bytes 1012232 | tf_op jit(solution)/shard_map/pallas_call | solution.py:257
  14.9 1.3 collective-permute-start.6
  16.2 2.2 collective-permute-start.4
  18.6 2.8 %collective-permute-done.6.refs_9_ = bf16[96,640]{1,0:T(8,128)(2,1)S(1)} collective-permute-done((bf16[96,640]{1,0:T(8,128)(2,1)}, bf16[96,640]{1,0:T(8,128)(2,1)S(1)}, u32[]{:S(2)}, u32[]{:S(2)}) %collective-permute-start.6) | collective-permute-done | bytes 122912 | tf_op jit(solution)/shard_map/ppermute | solution.py:40
  21.7 3.1 %collective-permute-done.4.refs_7_ = bf16[96,640]{1,0:T(8,128)(2,1)S(1)} collective-permute-done((bf16[96,640]{1,0:T(8,128)(2,1)}, bf16[96,640]{1,0:T(8,128)(2,1)S(1)}, u32[]{:S(2)}, u32[]{:S(2)}) %collective-permute-start.4) | collective-permute-done | bytes 122912 | tf_op jit(solution)/shard_map/ppermute | solution.py:40
  24.8 5.8 %collective-permute-start = (bf16[272,768]{1,0:T(8,128)(2,1)S(1)}, bf16[272,768]{1,0:T(8,128)(2,1)S(1)}, u32[]{:S(2)}, u32[]{:S(2)}) collective-permute-start(bf16[272,768]{1,0:T(8,128)(2,1)S(1)} %fusion.1.refs_1_), channel_id=1, source_target_pairs={{0,8},{8,0},{16,24},{24,16},{1,9},{9,1},{17,25},{25,17},{2,10},{10... | collective-permute-start | bytes 1253384 | tf_op jit(solution)/shard_map/ppermute | solution.py:28
  31.4 1.2 collective-permute-start.15
  34.1 3.8 %collective-permute-done.8.refs_10_ = bf16[288,640]{1,0:T(8,128)(2,1)S(1)} collective-permute-done((bf16[288,640]{1,0:T(8,128)(2,1)S(1)}, bf16[288,640]{1,0:T(8,128)(2,1)S(1)}, u32[]{:S(2)}, u32[]{:S(2)}) %collective-permute-start.8) | collective-permute-done | bytes 368672 | tf_op jit(solution)/shard_map/ppermute | solution.py:40
  39.4 10.2 %shard_map.307 = (bf16[1024,768]{1,0:T(8,128)(2,1)}, bf16[768,576]{1,0:T(8,128)(2,1)}, f32[16,768]{1,0:T(8,128)}, bf16[1024,192]{1,0:T(8,128)(2,1)}, bf16[1024,1...) custom-call(s32[2]{0:T(128)} %pad_add_fusion.place_ref.refs_0_, ...), custom_call_target="tpu_custom_call" | custom-call | flops 12079595520 | bytes 7323656 | tf_op jit(solution)/shard_map/pallas_call | solution.py:257
  50.5 5.8 %collective-permute-done.17.refs_13_ = bf16[96,1024]{1,0:T(8,128)(2,1)S(1)} collective-permute-done((bf16[96,1024]{1,0:T(8,128)(2,1)S(1)}, bf16[96,1024]{1,0:T(8,128)(2,1)S(1)}, u32[]{:S(2)}, u32[]{:S(2)}) %collective-permute-start.17) | collective-permute-done | bytes 196640 | tf_op jit(solution)/shard_map/ppermute | solution.py:40
  57.1 12.0 %collective-permute-start.12 = (bf16[256,768]{1,0:T(8,128)(2,1)S(1)}, bf16[256,768]{1,0:T(8,128)(2,1)}, u32[]{:S(2)}, u32[]{:S(2)}) collective-permute-start(bf16[256,768]{1,0:T(8,128)(2,1)S(1)} %copy-done.27), channel_id=1, source_target_pairs={{0,8},{8,0},{16,24},{24,16},{1,9},{9,1},{17,25},{25,17},{2,10},{10... | collective-permute-start | bytes 1179656 | tf_op jit(solution)/shard_map/ppermute | solution.py:28
  72.8 16.4 %shard_map.308 = (bf16[192,768]{1,0:T(8,128)(2,1)}, bf16[1024,768]{1,0:T(8,128)(2,1)}, bf16[1024,768]{1,0:T(8,128)(2,1)}, bf16[1024,768]{1,0:T(8,128)(2,1)}, f32...) custom-call(s32[2]{0:T(128)} %pad_add_fusion.place_ref.refs_0_, ...), custom_call_target="tpu_custom_call" | custom-call | flops 19327352832 | bytes 16469000 | tf_op jit(solution)/shard_map/pallas_call | solution.py:257
  89.1 5.7 %collective-permute-start.19 = (bf16[512,768]{1,0:T(8,128)(2,1)}, bf16[512,768]{1,0:T(8,128)(2,1)S(1)}, u32[]{:S(2)}, u32[]{:S(2)}) collective-permute-start(bf16[512,768]{1,0:T(8,128)(2,1)} %get-tuple-element.123), channel_id=1, source_target_pairs={{0,8},{8,0},{16,24},{24,16},{1,9},{9,1},{17,25},{25,17},{2,10},{10... | collective-permute-start | bytes 2359304 | tf_op jit(solution)/shard_map/ppermute | solution.py:28
  94.8 2.1 collective-permute-done.19.near_ref
  96.9 1.5 add_convert_fusion.3
  98.5 4.5 %shard_map.309 = (bf16[384,768]{1,0:T(8,128)(2,1)}, bf16[384,768]{1,0:T(8,128)(2,1)}) custom-call(s32[2]{0:T(128)} %pad_add_fusion.place_ref.refs_0_, bf16[1024,768]{1,0:T(8,128)(2,1)} %get-tuple-element.128.act_ref, bf16[256,768]{1,0:T(8,128)(2,1)} %cotangent_ref.1, bf16[256,768]{1,0:T(8,128)(2,1)} %collective-permute-done.12.refs_6_.cot_b, ...), custom_call_target="tpu_custom_call" | custom-call | flops 3623878656 | bytes 4325384 | tf_op jit(solution)/shard_map/pallas_call | solution.py:257
  103.0 1.2 collective-permute-start.21
  104.2 8.4 %shard_map.310 = (bf16[384,768]{1,0:T(8,128)(2,1)}, bf16[384,768]{1,0:T(8,128)(2,1)}, bf16[512,768]{1,0:T(8,128)(2,1)}, f32[256,768]{1,0:T(8,128)}, f32[256,768]{1,0:T(8,128)}, /*index=5*/f32[8,768]{1,0:T(8,128)}) custom-call(s32[2]{0:T(128)} %pad_add_fusion.place_ref.refs_0_, bf16[1024,768]{1,0:T(8,128)(2,1)} %get-tuple-element.128.act_ref, ...), custom_call_target="tpu_custom_call" | custom-call | flops 7247757312 | bytes 10248200 | tf_op jit(solution)/shard_map/pallas_call | solution.py:257
  113.3 3.7 %shard_map.311 = (f32[256,768]{1,0:T(8,128)}, bf16[256,768]{1,0:T(8,128)(2,1)}, f32[8,768]{1,0:T(8,128)}) custom-call(s32[2]{0:T(128)} %pad_add_fusion.place_ref.refs_0_, f32[256,768]{1,0:T(8,128)} %get-tuple-element.122.own_ref, bf16[512,768]{1,0:T(8,128)(2,1)} %copy-done.18, bf16[256,768]{1,0:T(8,128)(2,1)} %copy-done.28, ...), custom_call_target="tpu_custom_call" | custom-call | flops 1966080 | bytes 4399112 | tf_op jit(solution)/shard_map/pallas_call | solution.py:257
  117.0 1.5 collective-permute-start.23
  118.5 1.2 collective-permute-start.22
  119.7 7.2 %collective-permute-done.23.branch_c = bf16[256,768]{1,0:T(8,128)(2,1)S(1)} collective-permute-done((bf16[256,768]{1,0:T(8,128)(2,1)}, bf16[256,768]{1,0:T(8,128)(2,1)S(1)}, u32[]{:S(2)}, u32[]{:S(2)}) %collective-permute-start.23) | collective-permute-done | bytes 393248 | tf_op jit(solution)/shard_map/ppermute | solution.py:28
  126.9 1.8 collective-permute-start.24
  130.8 2.2 shard_map.312
  133.0 3.4 %collective-permute-start.26 = (bf16[96,768]{1,0:T(8,128)(2,1)}, bf16[96,768]{1,0:T(8,128)(2,1)S(1)}, u32[]{:S(2)}, u32[]{:S(2)}) collective-permute-start(bf16[96,768]{1,0:T(8,128)(2,1)} %get-tuple-element.155), channel_id=1, source_target_pairs={{0,4},{1,5},{2,6},{3,7},{4,0},{5,1},{6,2},{7,3},{8,12},{9,13},{10,... | collective-permute-start | bytes 442376 | tf_op jit(solution)/shard_map/ppermute | solution.py:40
  137.3 18.5 %shard_map.313 = (bf16[384,896]{1,0:T(8,128)(2,1)}, bf16[384,896]{1,0:T(8,128)(2,1)}, bf16[512,768]{1,0:T(8,128)(2,1)}, f32[256,768]{1,0:T(8,128)}, f32[256,768]{1,0:T(8,128)}) custom-call(s32[2]{0:T(128)} %pad_add_fusion.place_ref.refs_0_, bf16[256,768]{1,0:T(8,128)(2,1)} %get-tuple-element.139.branch_a, bf16[256,768]{1,0:T(8,128)(2,1)} %copy-done.47, ...), custom_call_target="tpu_custom_call" | custom-call | flops 21743271936 | bytes 11501576 | tf_op jit(solution)/shard_map/pallas_call | solution.py:257
  157.5 1.6 collective-permute-done.29.near_ref
  159.1 1.5 add_convert_fusion.2
  160.6 1.5 collective-permute-start.30
  162.1 2.2 shard_map.316
  165.4 1.7 collective-permute-start.40
  167.2 3.8 %collective-permute-done.30.far_ref = bf16[256,768]{1,0:T(8,128)(2,1)S(1)} collective-permute-done((bf16[256,768]{1,0:T(8,128)(2,1)S(1)}, bf16[256,768]{1,0:T(8,128)(2,1)S(1)}, u32[]{:S(2)}, u32[]{:S(2)}) %collective-permute-start.30) | collective-permute-done | bytes 393248 | tf_op jit(solution)/shard_map/ppermute | solution.py:28
  171.0 2.6 %collective-permute-done.31.received_ref = bf16[384,896]{1,0:T(8,128)(2,1)S(1)} collective-permute-done((bf16[384,896]{1,0:T(8,128)(2,1)}, bf16[384,896]{1,0:T(8,128)(2,1)S(1)}, u32[]{:S(2)}, u32[]{:S(2)}) %collective-permute-start.31) | collective-permute-done | bytes 688160 | tf_op jit(solution)/shard_map/ppermute | solution.py:40
  174.5 2.3 %shard_map.314 = (f32[96,896]{1,0:T(8,128)}, bf16[96,896]{1,0:T(8,128)(2,1)}, bf16[96,896]{1,0:T(8,128)(2,1)}, bf16[96,896]{1,0:T(8,128)(2,1)}) custom-call(s32[2]{0:T(128)} %pad_add_fusion.place_ref.refs_0_, bf16[384,896]{1,0:T(8,128)(2,1)} %get-tuple-element.159.kept_ref, bf16[384,896]{1,0:T(8,128)(2,1)} %copy-done.22), custom_call_target="tpu_custom_call" | custom-call | flops 344064 | bytes 2236424 | tf_op jit(solution)/shard_map/pallas_call | solution.py:257
  176.8 2.9 %collective-permute-done.41 = bf16[96,768]{1,0:T(8,128)(2,1)S(1)} collective-permute-done((bf16[96,768]{1,0:T(8,128)(2,1)}, bf16[96,768]{1,0:T(8,128)(2,1)S(1)}, u32[]{:S(2)}, u32[]{:S(2)}) %collective-permute-start.41) | collective-permute-done | bytes 147488 | tf_op jit(solution)/shard_map/ppermute | solution.py:40
  179.9 1.5 collective-permute-start.43
  181.4 3.2 %collective-permute-start.33 = (bf16[96,896]{1,0:T(8,128)(2,1)S(1)}, bf16[96,896]{1,0:T(8,128)(2,1)S(1)}, u32[]{:S(2)}, u32[]{:S(2)}) collective-permute-start(bf16[96,896]{1,0:T(8,128)(2,1)S(1)} %copy-done.52), channel_id=1, source_target_pairs={{0,4},{1,5},{2,6},{3,7},{4,0},{5,1},{6,2},{7,3},{8,12},{9,13},{10,... | collective-permute-start | bytes 516104 | tf_op jit(solution)/shard_map/ppermute | solution.py:40
  185.4 3.4 %shard_map.315 = f32[256,768]{1,0:T(8,128)} custom-call(s32[2]{0:T(128)} %pad_add_fusion.place_ref.refs_0_, f32[256,768]{1,0:T(8,128)} %get-tuple-element.164.own_ref, bf16[512,768]{1,0:T(8,128)(2,1)} %copy-done.17, bf16[256,768]{1,0:T(8,128)(2,1)} %copy-done.26, bf16[256,768]{1,0:T(8,128)(2,1)} %tokens_ref.1, f32[256,768]{1,0:T(8,128)} %get-tuple-element.166.resid_grad_ref, ...), custom_call_target="tpu_custom_call" | custom-call | flops 1966080 | bytes 3981320 | tf_op jit(solution)/shard_map/pallas_call | solution.py:257
  188.9 2.6 %collective-permute-start.42 = (bf16[96,1536]{1,0:T(8,128)(2,1)S(1)}, bf16[96,1536]{1,0:T(8,128)(2,1)S(1)}, u32[]{:S(2)}, u32[]{:S(2)}) collective-permute-start(bf16[96,1536]{1,0:T(8,128)(2,1)S(1)} %pad_maximum_fusion.2.refs_0_), channel_id=1, source_target_pairs={{0,8},{8,0},{16,24},{24,16},{1,9},{9,1},{17,25},{25,17},{2,10},{10... | collective-permute-start | bytes 884744 | tf_op jit(solution)/shard_map/ppermute | solution.py:28
  191.5 3.5 %collective-permute-done.33 = bf16[96,896]{1,0:T(8,128)(2,1)S(1)} collective-permute-done((bf16[96,896]{1,0:T(8,128)(2,1)S(1)}, bf16[96,896]{1,0:T(8,128)(2,1)S(1)}, u32[]{:S(2)}, u32[]{:S(2)}) %collective-permute-start.33) | collective-permute-done | bytes 172064 | tf_op jit(solution)/shard_map/ppermute | solution.py:40
  195.1 3.7 %collective-permute-done.34 = bf16[96,896]{1,0:T(8,128)(2,1)S(1)} collective-permute-done((bf16[96,896]{1,0:T(8,128)(2,1)S(1)}, bf16[96,896]{1,0:T(8,128)(2,1)S(1)}, u32[]{:S(2)}, u32[]{:S(2)}) %collective-permute-start.34) | collective-permute-done | bytes 172064 | tf_op jit(solution)/shard_map/ppermute | solution.py:40
  198.8 1.9 collective-permute-start.44
  202.8 3.2 %shard_map.318 = (f32[384,768]{1,0:T(8,128)}, f32[384,768]{1,0:T(8,128)}, f32[384,768]{1,0:T(8,128)}) custom-call(s32[2]{0:T(128)S(1)} %copy-done.12, bf16[96,1536]{1,0:T(8,128)(2,1)S(1)} %pad_maximum_fusion.2.refs_0_, bf16[96,1536]{1,0:T(8,128)(2,1)S(1)} %collective-permute-done.42.refs_1_, bf16[96,1536]{1,0:T(8,128)(2,1)S(1)} %collective-permute-done.43.refs_2_, ...), custom_call_target="tpu_custom_call" | custom-call | tf_op jit(solution)/shard_map/pallas_call | solution.py:715
  206.2 3.4 %shard_map.317 = (f32[96,3072]{1,0:T(8,128)}, f32[96,3072]{1,0:T(8,128)}, f32[96,3072]{1,0:T(8,128)}) custom-call(s32[2]{0:T(128)S(1)} %copy-done.12, bf16[96,1536]{1,0:T(8,128)(2,1)S(1)} %pad_maximum_fusion.2.refs_0_, bf16[96,1536]{1,0:T(8,128)(2,1)S(1)} %collective-permute-done.42.refs_1_, bf16[96,1536]{1,0:T(8,128)(2,1)S(1)} %collective-permute-done.43.refs_2_, ...), custom_call_target="tpu_custom_call" | custom-call | tf_op jit(solution)/shard_map/pallas_call | solution.py:715
  209.8 1.2 collective-permute-done.45.refs_3_.refs_7_
  211.1 3.5 %shard_map.319 = (f32[96,2304]{1,0:T(8,128)}, f32[96,2304]{1,0:T(8,128)}, f32[96,2304]{1,0:T(8,128)}, f32[96,768]{1,0:T(8,128)}, f32[96,768]{1,0:T(8,128)}, /*in...) custom-call(s32[2]{0:T(128)S(1)} %copy-done.12, ...), custom_call_target="tpu_custom_call" | custom-call | tf_op jit(solution)/shard_map/pallas_call | solution.py:677
  (198 shorter events, 20.9 us)
Async XLA Ops:
  7.2 65.5 %all-gather.2.cloned.1.call-start = ((), (), s32[]{:S(2)}) async-start(), calls=%async_computation | async-start | bytes 2211840 | tf_op jit(solution)/shard_map/all_gather | solution.py:812
  11.3 26.6 %copy-start.27 = (bf16[256,768]{1,0:T(8,128)(2,1)S(1)}, bf16[256,768]{1,0:T(8,128)(2,1)}, u32[]{:S(2)}) copy-start(bf16[256,768]{1,0:T(8,128)(2,1)} %cotangent_ref.1) | copy-start | bytes 1179652
  11.3 19.3 %collective-permute-start.1 = (bf16[272,768]{1,0:T(8,128)(2,1)S(1)}, bf16[272,768]{1,0:T(8,128)(2,1)S(1)}, u32[]{:S(2)}, u32[]{:S(2)}) collective-permute-start(bf16[272,768]{1,0:T(8,128)(2,1)S(1)} %fusion.1.refs_1_), channel_id=1, source_target_pairs={{0,16},{8,24},{16,0},{24,8},{1,17},{9,25},{17,1},{25,9},{2,18},{10... | collective-permute-start | bytes 1253384 | tf_op jit(solution)/shard_map/ppermute | solution.py:28
  14.9 6.6 %collective-permute-start.6 = (bf16[96,640]{1,0:T(8,128)(2,1)}, bf16[96,640]{1,0:T(8,128)(2,1)S(1)}, u32[]{:S(2)}, u32[]{:S(2)}) collective-permute-start(bf16[96,640]{1,0:T(8,128)(2,1)} %shard_map.305.refs_5_), channel_id=1, source_target_pairs={{0,6},{1,7},{2,4},{3,5},{4,2},{5,3},{6,0},{7,1},{8,14},{9,15},{10,... | collective-permute-start | bytes 368648 | tf_op jit(solution)/shard_map/ppermute | solution.py:40
  16.2 8.6 %collective-permute-start.4 = (bf16[96,640]{1,0:T(8,128)(2,1)}, bf16[96,640]{1,0:T(8,128)(2,1)S(1)}, u32[]{:S(2)}, u32[]{:S(2)}) collective-permute-start(bf16[96,640]{1,0:T(8,128)(2,1)} %shard_map.305.refs_5_), channel_id=1, source_target_pairs={{0,2},{1,3},{2,0},{3,1},{4,6},{5,7},{6,4},{7,5},{8,10},{9,11},{10,... | collective-permute-start | bytes 368648 | tf_op jit(solution)/shard_map/ppermute | solution.py:40
  18.4 12.3 %collective-permute-start.5 = (bf16[96,640]{1,0:T(8,128)(2,1)}, bf16[96,640]{1,0:T(8,128)(2,1)S(1)}, u32[]{:S(2)}, u32[]{:S(2)}) collective-permute-start(bf16[96,640]{1,0:T(8,128)(2,1)} %shard_map.305.refs_5_), channel_id=1, source_target_pairs={{0,4},{1,5},{2,6},{3,7},{4,0},{5,1},{6,2},{7,3},{8,12},{9,13},{10,... | collective-permute-start | bytes 368648 | tf_op jit(solution)/shard_map/ppermute | solution.py:40
  18.4 12.4 %collective-permute-start.7 = (bf16[96,1024]{1,0:T(8,128)(2,1)S(1)}, bf16[96,1024]{1,0:T(8,128)(2,1)}, u32[]{:S(2)}, u32[]{:S(2)}) collective-permute-start(bf16[96,1024]{1,0:T(8,128)(2,1)S(1)} %copy-done.50), channel_id=1, source_target_pairs={{0,1},{1,0},{2,3},{3,2},{4,5},{5,4},{6,7},{7,6},{8,9},{9,8},{10,11... | collective-permute-start | bytes 589832 | tf_op jit(solution)/shard_map/ppermute | solution.py:40
  21.4 9.3 %collective-permute-start.3 = (bf16[96,640]{1,0:T(8,128)(2,1)}, bf16[96,640]{1,0:T(8,128)(2,1)S(1)}, u32[]{:S(2)}, u32[]{:S(2)}) collective-permute-start(bf16[96,640]{1,0:T(8,128)(2,1)} %shard_map.305.refs_5_), channel_id=1, source_target_pairs={{0,1},{1,0},{2,3},{3,2},{4,5},{5,4},{6,7},{7,6},{8,9},{9,8},{10,11... | collective-permute-start | bytes 368648 | tf_op jit(solution)/shard_map/ppermute | solution.py:40
  24.8 8.3 %collective-permute-start = (bf16[272,768]{1,0:T(8,128)(2,1)S(1)}, bf16[272,768]{1,0:T(8,128)(2,1)S(1)}, u32[]{:S(2)}, u32[]{:S(2)}) collective-permute-start(bf16[272,768]{1,0:T(8,128)(2,1)S(1)} %fusion.1.refs_1_), channel_id=1, source_target_pairs={{0,8},{8,0},{16,24},{24,16},{1,9},{9,1},{17,25},{25,17},{2,10},{10... | collective-permute-start | bytes 1253384 | tf_op jit(solution)/shard_map/ppermute | solution.py:28
  30.6 7.3 %collective-permute-start.2 = (bf16[272,768]{1,0:T(8,128)(2,1)S(1)}, bf16[272,768]{1,0:T(8,128)(2,1)S(1)}, u32[]{:S(2)}, u32[]{:S(2)}) collective-permute-start(bf16[272,768]{1,0:T(8,128)(2,1)S(1)} %collective-permute-done.1.refs_3_), channel_id=1, source_target_pairs={{0,8},{8,0},{16,24},{24,16},{1,9},{9,1},{17,25},{25,17},{2,10},{10... | collective-permute-start | bytes 1253384 | tf_op jit(solution)/shard_map/ppermute | solution.py:28
  30.8 7.1 %collective-permute-start.8 = (bf16[288,640]{1,0:T(8,128)(2,1)S(1)}, bf16[288,640]{1,0:T(8,128)(2,1)S(1)}, u32[]{:S(2)}, u32[]{:S(2)}) collective-permute-start(bf16[288,640]{1,0:T(8,128)(2,1)S(1)} %pad_maximum_fusion.1), channel_id=1, source_target_pairs={{0,1},{1,0},{2,3},{3,2},{4,5},{5,4},{6,7},{7,6},{8,9},{9,8},{10,11... | collective-permute-start | bytes 1105928 | tf_op jit(solution)/shard_map/ppermute | solution.py:40
  31.4 19.1 %collective-permute-start.15 = (bf16[96,1024]{1,0:T(8,128)(2,1)S(1)}, bf16[96,1024]{1,0:T(8,128)(2,1)S(1)}, u32[]{:S(2)}, u32[]{:S(2)}) collective-permute-start(bf16[96,1024]{1,0:T(8,128)(2,1)S(1)} %copy-done.50), channel_id=1, source_target_pairs={{0,2},{1,3},{2,0},{3,1},{4,6},{5,7},{6,4},{7,5},{8,10},{9,11},{10,... | collective-permute-start | bytes 589832 | tf_op jit(solution)/shard_map/ppermute | solution.py:40
  32.6 17.9 %collective-permute-start.16 = (bf16[96,1024]{1,0:T(8,128)(2,1)S(1)}, bf16[96,1024]{1,0:T(8,128)(2,1)S(1)}, u32[]{:S(2)}, u32[]{:S(2)}) collective-permute-start(bf16[96,1024]{1,0:T(8,128)(2,1)S(1)} %copy-done.50), channel_id=1, source_target_pairs={{0,4},{1,5},{2,6},{3,7},{4,0},{5,1},{6,2},{7,3},{8,12},{9,13},{10,... | collective-permute-start | bytes 589832 | tf_op jit(solution)/shard_map/ppermute | solution.py:40
  33.1 23.3 %collective-permute-start.17 = (bf16[96,1024]{1,0:T(8,128)(2,1)S(1)}, bf16[96,1024]{1,0:T(8,128)(2,1)S(1)}, u32[]{:S(2)}, u32[]{:S(2)}) collective-permute-start(bf16[96,1024]{1,0:T(8,128)(2,1)S(1)} %copy-done.50), channel_id=1, source_target_pairs={{0,6},{1,7},{2,4},{3,5},{4,2},{5,3},{6,0},{7,1},{8,14},{9,15},{10,... | collective-permute-start | bytes 589832 | tf_op jit(solution)/shard_map/ppermute | solution.py:40
  37.9 31.3 %collective-permute-start.13 = (bf16[256,768]{1,0:T(8,128)(2,1)S(1)}, bf16[256,768]{1,0:T(8,128)(2,1)}, u32[]{:S(2)}, u32[]{:S(2)}) collective-permute-start(bf16[256,768]{1,0:T(8,128)(2,1)S(1)} %copy-done.27), channel_id=1, source_target_pairs={{0,16},{8,24},{16,0},{24,8},{1,17},{9,25},{17,1},{25,9},{2,18},{10... | collective-permute-start | bytes 1179656 | tf_op jit(solution)/shard_map/ppermute | solution.py:28
  49.6 20.1 %collective-permute-start.10 = (bf16[1024,192]{1,0:T(8,128)(2,1)}, bf16[1024,192]{1,0:T(8,128)(2,1)S(1)}, u32[]{:S(2)}, u32[]{:S(2)}) collective-permute-start(bf16[1024,192]{1,0:T(8,128)(2,1)} %get-tuple-element.115.refs_1_.attended_a), channel_id=1, source_target_pairs={{0,16},{8,24},{16,0},{24,8},{1,17},{9,25},{17,1},{25,9},{2,18},{10... | collective-permute-start | bytes 1179656 | tf_op jit(solution)/shard_map/ppermute | solution.py:28
  56.4 14.9 %collective-permute-start.18 = (bf16[288,1024]{1,0:T(8,128)(2,1)S(1)}, bf16[288,1024]{1,0:T(8,128)(2,1)S(1)}, u32[]{:S(2)}, u32[]{:S(2)}) collective-permute-start(bf16[288,1024]{1,0:T(8,128)(2,1)S(1)} %pad_maximum_fusion), channel_id=1, source_target_pairs={{0,1},{1,0},{2,3},{3,2},{4,5},{5,4},{6,7},{7,6},{8,9},{9,8},{10,11... | collective-permute-start | bytes 1769480 | tf_op jit(solution)/shard_map/ppermute | solution.py:40
  57.1 14.2 %collective-permute-start.12 = (bf16[256,768]{1,0:T(8,128)(2,1)S(1)}, bf16[256,768]{1,0:T(8,128)(2,1)}, u32[]{:S(2)}, u32[]{:S(2)}) collective-permute-start(bf16[256,768]{1,0:T(8,128)(2,1)S(1)} %copy-done.27), channel_id=1, source_target_pairs={{0,8},{8,0},{16,24},{24,16},{1,9},{9,1},{17,25},{25,17},{2,10},{10... | collective-permute-start | bytes 1179656 | tf_op jit(solution)/shard_map/ppermute | solution.py:28
  69.2 2.3 %collective-permute-start.14 = (bf16[256,768]{1,0:T(8,128)(2,1)}, bf16[256,768]{1,0:T(8,128)(2,1)}, u32[]{:S(2)}, u32[]{:S(2)}) collective-permute-start(bf16[256,768]{1,0:T(8,128)(2,1)} %collective-permute-done.13.refs_7_.cot_c), channel_id=1, source_target_pairs={{0,8},{8,0},{16,24},{24,16},{1,9},{9,1},{17,25},{25,17},{2,10},{10... | collective-permute-start | bytes 1179656 | tf_op jit(solution)/shard_map/ppermute | solution.py:28
  69.2 2.8 %collective-permute-start.9 = (bf16[1024,192]{1,0:T(8,128)(2,1)S(1)}, bf16[1024,192]{1,0:T(8,128)(2,1)}, u32[]{:S(2)}, u32[]{:S(2)}) collective-permute-start(bf16[1024,192]{1,0:T(8,128)(2,1)S(1)} %copy-done.41), channel_id=1, source_target_pairs={{0,8},{8,0},{16,24},{24,16},{1,9},{9,1},{17,25},{25,17},{2,10},{10... | collective-permute-start | bytes 1179656 | tf_op jit(solution)/shard_map/ppermute | solution.py:28
  69.7 3.0 %collective-permute-start.11 = (bf16[1024,192]{1,0:T(8,128)(2,1)S(1)}, bf16[1024,192]{1,0:T(8,128)(2,1)}, u32[]{:S(2)}, u32[]{:S(2)}) collective-permute-start(bf16[1024,192]{1,0:T(8,128)(2,1)S(1)} %collective-permute-done.10.refs_3_.attended_c), channel_id=1, source_target_pairs={{0,8},{8,0},{16,24},{24,16},{1,9},{9,1},{17,25},{25,17},{2,10},{10... | collective-permute-start | bytes 1179656 | tf_op jit(solution)/shard_map/ppermute | solution.py:28
  89.1 7.8 %collective-permute-start.19 = (bf16[512,768]{1,0:T(8,128)(2,1)}, bf16[512,768]{1,0:T(8,128)(2,1)S(1)}, u32[]{:S(2)}, u32[]{:S(2)}) collective-permute-start(bf16[512,768]{1,0:T(8,128)(2,1)} %get-tuple-element.123), channel_id=1, source_target_pairs={{0,8},{8,0},{16,24},{24,16},{1,9},{9,1},{17,25},{25,17},{2,10},{10... | collective-permute-start | bytes 2359304 | tf_op jit(solution)/shard_map/ppermute | solution.py:28
  98.4 14.2 %collective-permute-start.20 = (bf16[256,768]{1,0:T(8,128)(2,1)S(1)}, bf16[256,768]{1,0:T(8,128)(2,1)S(1)}, u32[]{:S(2)}, u32[]{:S(2)}) collective-permute-start(bf16[256,768]{1,0:T(8,128)(2,1)S(1)} %add_convert_fusion.3), channel_id=1, source_target_pairs={{0,16},{8,24},{16,0},{24,8},{1,17},{9,25},{17,1},{25,9},{2,18},{10... | collective-permute-start | bytes 1179656 | tf_op jit(solution)/shard_map/ppermute | solution.py:28
  103.0 15.5 %collective-permute-start.21 = (bf16[384,768]{1,0:T(8,128)(2,1)}, bf16[384,768]{1,0:T(8,128)(2,1)S(1)}, u32[]{:S(2)}, u32[]{:S(2)}) collective-permute-start(bf16[384,768]{1,0:T(8,128)(2,1)} %get-tuple-element.136), channel_id=1, source_target_pairs={{0,1},{1,0},{2,3},{3,2},{4,5},{5,4},{6,7},{7,6},{8,9},{9,8},{10,11... | collective-permute-start | bytes 1769480 | tf_op jit(solution)/shard_map/ppermute | solution.py:40
  117.0 9.9 %collective-permute-start.23 = (bf16[256,768]{1,0:T(8,128)(2,1)}, bf16[256,768]{1,0:T(8,128)(2,1)S(1)}, u32[]{:S(2)}, u32[]{:S(2)}) collective-permute-start(bf16[256,768]{1,0:T(8,128)(2,1)} %get-tuple-element.139.branch_a), channel_id=1, source_target_pairs={{0,16},{8,24},{16,0},{24,8},{1,17},{9,25},{17,1},{25,9},{2,18},{10... | collective-permute-start | bytes 1179656 | tf_op jit(solution)/shard_map/ppermute | solution.py:28
  118.5 17.9 %collective-permute-start.22 = (bf16[256,768]{1,0:T(8,128)(2,1)}, bf16[256,768]{1,0:T(8,128)(2,1)S(1)}, u32[]{:S(2)}, u32[]{:S(2)}) collective-permute-start(bf16[256,768]{1,0:T(8,128)(2,1)} %get-tuple-element.139.branch_a), channel_id=1, source_target_pairs={{0,8},{8,0},{16,24},{24,16},{1,9},{9,1},{17,25},{25,17},{2,10},{10... | collective-permute-start | bytes 1179656 | tf_op jit(solution)/shard_map/ppermute | solution.py:28
  126.9 9.5 %collective-permute-start.24 = (bf16[256,768]{1,0:T(8,128)(2,1)S(1)}, bf16[256,768]{1,0:T(8,128)(2,1)S(1)}, u32[]{:S(2)}, u32[]{:S(2)}) collective-permute-start(bf16[256,768]{1,0:T(8,128)(2,1)S(1)} %collective-permute-done.23.branch_c), channel_id=1, source_target_pairs={{0,8},{8,0},{16,24},{24,16},{1,9},{9,1},{17,25},{25,17},{2,10},{10... | collective-permute-start | bytes 1179656 | tf_op jit(solution)/shard_map/ppermute | solution.py:28
  130.5 25.2 %collective-permute-start.28 = (bf16[384,768]{1,0:T(8,128)(2,1)S(1)}, bf16[384,768]{1,0:T(8,128)(2,1)S(1)}, u32[]{:S(2)}, u32[]{:S(2)}) collective-permute-start(bf16[384,768]{1,0:T(8,128)(2,1)S(1)} %copy-done.39), channel_id=1, source_target_pairs={{0,1},{1,0},{2,3},{3,2},{4,5},{5,4},{6,7},{7,6},{8,9},{9,8},{10,11... | collective-permute-start | bytes 1769480 | tf_op jit(solution)/shard_map/ppermute | solution.py:40
  133.0 22.8 %collective-permute-start.25 = (bf16[96,768]{1,0:T(8,128)(2,1)}, bf16[96,768]{1,0:T(8,128)(2,1)S(1)}, u32[]{:S(2)}, u32[]{:S(2)}) collective-permute-start(bf16[96,768]{1,0:T(8,128)(2,1)} %get-tuple-element.154), channel_id=1, source_target_pairs={{0,2},{1,3},{2,0},{3,1},{4,6},{5,7},{6,4},{7,5},{8,10},{9,11},{10,... | collective-permute-start | bytes 442376 | tf_op jit(solution)/shard_map/ppermute | solution.py:40
  133.0 22.8 %collective-permute-start.26 = (bf16[96,768]{1,0:T(8,128)(2,1)}, bf16[96,768]{1,0:T(8,128)(2,1)S(1)}, u32[]{:S(2)}, u32[]{:S(2)}) collective-permute-start(bf16[96,768]{1,0:T(8,128)(2,1)} %get-tuple-element.155), channel_id=1, source_target_pairs={{0,4},{1,5},{2,6},{3,7},{4,0},{5,1},{6,2},{7,3},{8,12},{9,13},{10,... | collective-permute-start | bytes 442376 | tf_op jit(solution)/shard_map/ppermute | solution.py:40
  136.4 19.4 %collective-permute-start.27 = (bf16[96,768]{1,0:T(8,128)(2,1)}, bf16[96,768]{1,0:T(8,128)(2,1)S(1)}, u32[]{:S(2)}, u32[]{:S(2)}) collective-permute-start(bf16[96,768]{1,0:T(8,128)(2,1)} %get-tuple-element.156), channel_id=1, source_target_pairs={{0,6},{1,7},{2,4},{3,5},{4,2},{5,3},{6,0},{7,1},{8,14},{9,15},{10,... | collective-permute-start | bytes 442376 | tf_op jit(solution)/shard_map/ppermute | solution.py:40
  155.8 3.3 %collective-permute-start.29 = (bf16[512,768]{1,0:T(8,128)(2,1)}, bf16[512,768]{1,0:T(8,128)(2,1)S(1)}, u32[]{:S(2)}, u32[]{:S(2)}) collective-permute-start(bf16[512,768]{1,0:T(8,128)(2,1)} %get-tuple-element.158), channel_id=1, source_target_pairs={{0,8},{8,0},{16,24},{24,16},{1,9},{9,1},{17,25},{25,17},{2,10},{10... | collective-permute-start | bytes 2359304 | tf_op jit(solution)/shard_map/ppermute | solution.py:28
  156.7 10.4 %collective-permute-start.35 = (bf16[512,768]{1,0:T(8,128)(2,1)S(1)}, bf16[512,768]{1,0:T(8,128)(2,1)S(1)}, u32[]{:S(2)}, u32[]{:S(2)}) collective-permute-start(bf16[512,768]{1,0:T(8,128)(2,1)S(1)} %copy-done.38), channel_id=1, source_target_pairs={{0,8},{8,0},{16,24},{24,16},{1,9},{9,1},{17,25},{25,17},{2,10},{10... | collective-permute-start | bytes 2359304 | tf_op jit(solution)/shard_map/ppermute | solution.py:28
  156.8 16.8 %collective-permute-start.31 = (bf16[384,896]{1,0:T(8,128)(2,1)}, bf16[384,896]{1,0:T(8,128)(2,1)S(1)}, u32[]{:S(2)}, u32[]{:S(2)}) collective-permute-start(bf16[384,896]{1,0:T(8,128)(2,1)} %get-tuple-element.160), channel_id=1, source_target_pairs={{0,1},{1,0},{2,3},{3,2},{4,5},{5,4},{6,7},{7,6},{8,9},{9,8},{10,11... | collective-permute-start | bytes 2064392 | tf_op jit(solution)/shard_map/ppermute | solution.py:40
  160.6 10.4 %collective-permute-start.30 = (bf16[256,768]{1,0:T(8,128)(2,1)S(1)}, bf16[256,768]{1,0:T(8,128)(2,1)S(1)}, u32[]{:S(2)}, u32[]{:S(2)}) collective-permute-start(bf16[256,768]{1,0:T(8,128)(2,1)S(1)} %add_convert_fusion.2), channel_id=1, source_target_pairs={{0,16},{8,24},{16,0},{24,8},{1,17},{9,25},{17,1},{25,9},{2,18},{10... | collective-permute-start | bytes 1179656 | tf_op jit(solution)/shard_map/ppermute | solution.py:28
  164.3 12.4 %collective-permute-start.39 = (bf16[96,768]{1,0:T(8,128)(2,1)}, bf16[96,768]{1,0:T(8,128)(2,1)S(1)}, u32[]{:S(2)}, u32[]{:S(2)}) collective-permute-start(bf16[96,768]{1,0:T(8,128)(2,1)} %get-tuple-element.184), channel_id=1, source_target_pairs={{0,2},{1,3},{2,0},{3,1},{4,6},{5,7},{6,4},{7,5},{8,10},{9,11},{10,... | collective-permute-start | bytes 442376 | tf_op jit(solution)/shard_map/ppermute | solution.py:40
  165.4 11.3 %collective-permute-start.40 = (bf16[96,768]{1,0:T(8,128)(2,1)}, bf16[96,768]{1,0:T(8,128)(2,1)S(1)}, u32[]{:S(2)}, u32[]{:S(2)}) collective-permute-start(bf16[96,768]{1,0:T(8,128)(2,1)} %get-tuple-element.185), channel_id=1, source_target_pairs={{0,4},{1,5},{2,6},{3,7},{4,0},{5,1},{6,2},{7,3},{8,12},{9,13},{10,... | collective-permute-start | bytes 442376 | tf_op jit(solution)/shard_map/ppermute | solution.py:40
  167.1 12.6 %collective-permute-start.41 = (bf16[96,768]{1,0:T(8,128)(2,1)}, bf16[96,768]{1,0:T(8,128)(2,1)S(1)}, u32[]{:S(2)}, u32[]{:S(2)}) collective-permute-start(bf16[96,768]{1,0:T(8,128)(2,1)} %get-tuple-element.186), channel_id=1, source_target_pairs={{0,6},{1,7},{2,4},{3,5},{4,2},{5,3},{6,0},{7,1},{8,14},{9,15},{10,... | collective-permute-start | bytes 442376 | tf_op jit(solution)/shard_map/ppermute | solution.py:40
  179.7 21.0 %collective-permute-start.36 = (bf16[256,768]{1,0:T(8,128)(2,1)S(1)}, bf16[256,768]{1,0:T(8,128)(2,1)S(1)}, u32[]{:S(2)}, u32[]{:S(2)}) collective-permute-start(bf16[256,768]{1,0:T(8,128)(2,1)S(1)} %add_convert_fusion.1), channel_id=1, source_target_pairs={{0,16},{8,24},{16,0},{24,8},{1,17},{9,25},{17,1},{25,9},{2,18},{10... | collective-permute-start | bytes 1179656 | tf_op jit(solution)/shard_map/ppermute | solution.py:28
  179.9 18.9 %collective-permute-start.43 = (bf16[96,1536]{1,0:T(8,128)(2,1)S(1)}, bf16[96,1536]{1,0:T(8,128)(2,1)S(1)}, u32[]{:S(2)}, u32[]{:S(2)}) collective-permute-start(bf16[96,1536]{1,0:T(8,128)(2,1)S(1)} %pad_maximum_fusion.2.refs_0_), channel_id=1, source_target_pairs={{0,16},{8,24},{16,0},{24,8},{1,17},{9,25},{17,1},{25,9},{2,18},{10... | collective-permute-start | bytes 884744 | tf_op jit(solution)/shard_map/ppermute | solution.py:28
  181.4 7.4 %collective-permute-start.32 = (bf16[96,896]{1,0:T(8,128)(2,1)S(1)}, bf16[96,896]{1,0:T(8,128)(2,1)S(1)}, u32[]{:S(2)}, u32[]{:S(2)}) collective-permute-start(bf16[96,896]{1,0:T(8,128)(2,1)S(1)} %copy-done.53), channel_id=1, source_target_pairs={{0,2},{1,3},{2,0},{3,1},{4,6},{5,7},{6,4},{7,5},{8,10},{9,11},{10,... | collective-permute-start | bytes 516104 | tf_op jit(solution)/shard_map/ppermute | solution.py:40
  181.4 13.6 %collective-permute-start.33 = (bf16[96,896]{1,0:T(8,128)(2,1)S(1)}, bf16[96,896]{1,0:T(8,128)(2,1)S(1)}, u32[]{:S(2)}, u32[]{:S(2)}) collective-permute-start(bf16[96,896]{1,0:T(8,128)(2,1)S(1)} %copy-done.52), channel_id=1, source_target_pairs={{0,4},{1,5},{2,6},{3,7},{4,0},{5,1},{6,2},{7,3},{8,12},{9,13},{10,... | collective-permute-start | bytes 516104 | tf_op jit(solution)/shard_map/ppermute | solution.py:40
  184.6 14.1 %collective-permute-start.34 = (bf16[96,896]{1,0:T(8,128)(2,1)S(1)}, bf16[96,896]{1,0:T(8,128)(2,1)S(1)}, u32[]{:S(2)}, u32[]{:S(2)}) collective-permute-start(bf16[96,896]{1,0:T(8,128)(2,1)S(1)} %copy-done.51), channel_id=1, source_target_pairs={{0,6},{1,7},{2,4},{3,5},{4,2},{5,3},{6,0},{7,1},{8,14},{9,15},{10,... | collective-permute-start | bytes 516104 | tf_op jit(solution)/shard_map/ppermute | solution.py:40
  188.9 13.9 %collective-permute-start.42 = (bf16[96,1536]{1,0:T(8,128)(2,1)S(1)}, bf16[96,1536]{1,0:T(8,128)(2,1)S(1)}, u32[]{:S(2)}, u32[]{:S(2)}) collective-permute-start(bf16[96,1536]{1,0:T(8,128)(2,1)S(1)} %pad_maximum_fusion.2.refs_0_), channel_id=1, source_target_pairs={{0,8},{8,0},{16,24},{24,16},{1,9},{9,1},{17,25},{25,17},{2,10},{10... | collective-permute-start | bytes 884744 | tf_op jit(solution)/shard_map/ppermute | solution.py:28
  198.8 4.0 %collective-permute-start.44 = (bf16[96,1536]{1,0:T(8,128)(2,1)S(1)}, bf16[96,1536]{1,0:T(8,128)(2,1)S(1)}, u32[]{:S(2)}, u32[]{:S(2)}) collective-permute-start(bf16[96,1536]{1,0:T(8,128)(2,1)S(1)} %collective-permute-done.43.refs_2_), channel_id=1, source_target_pairs={{0,8},{8,0},{16,24},{24,16},{1,9},{9,1},{17,25},{25,17},{2,10},{10... | collective-permute-start | bytes 884744 | tf_op jit(solution)/shard_map/ppermute | solution.py:28
  201.7 7.9 %collective-permute-start.38 = (bf16[96,896]{1,0:T(8,128)(2,1)S(1)}, bf16[96,896]{1,0:T(8,128)(2,1)S(1)}, u32[]{:S(2)}, u32[]{:S(2)}) collective-permute-start(bf16[96,896]{1,0:T(8,128)(2,1)S(1)} %add_convert_fusion.4.refs_0_.refs_4_), channel_id=1, source_target_pairs={{0,16},{8,24},{16,0},{24,8},{1,17},{9,25},{17,1},{25,9},{2,18},{10... | collective-permute-start | bytes 516104 | tf_op jit(solution)/shard_map/ppermute | solution.py:28
  202.5 7.3 %collective-permute-start.37 = (bf16[96,896]{1,0:T(8,128)(2,1)S(1)}, bf16[96,896]{1,0:T(8,128)(2,1)S(1)}, u32[]{:S(2)}, u32[]{:S(2)}) collective-permute-start(bf16[96,896]{1,0:T(8,128)(2,1)S(1)} %add_convert_fusion.4.refs_0_.refs_4_), channel_id=1, source_target_pairs={{0,8},{8,0},{16,24},{24,16},{1,9},{9,1},{17,25},{25,17},{2,10},{10... | collective-permute-start | bytes 516104 | tf_op jit(solution)/shard_map/ppermute | solution.py:28
  209.6 1.4 collective-permute-start.45
  (55 other events, 430.9 us)
Sparse Core Ops, SparseCore 0:
  11.3 56.7 all-gather.1
